TPU v7x, 32 devices: a whole 2x2x4 slice. The times are simulated.
32 devices in a mesh: seq: 2 (over x), wt: 16 (over z, y, core).
Axes of the slice: x: 2, y: 2, z: 4, core: 2. Of those that a mesh axis runs over, the one named last changes fastest.
Arguments:
- activations: bfloat16 [16, 2048, 1024], P('wt', 'seq'), may hold values from -6 to 6
- w_query: bfloat16 [1024, 1024], P('wt'), may hold values from -0.1875 to 0.1875
- w_key: bfloat16 [1024, 1024], P('wt'), may hold values from -0.1875 to 0.1875
- w_value: bfloat16 [1024, 1024], P('wt'), may hold values from -0.1875 to 0.1875
- w_gate: bfloat16 [1024, 1024], P('wt'), may hold values from -0.1875 to 0.1875
- w_out: bfloat16 [1024, 1024], P('wt'), may hold values from -0.1875 to 0.1875
- w_first: bfloat16 [1024, 2816], P('wt'), may hold values from -0.1875 to 0.1875
- w_second: bfloat16 [1024, 2816], P('wt'), may hold values from -0.1875 to 0.1875
- w_down: bfloat16 [2816, 1024], P('wt'), may hold values from -0.109375 to 0.109375
- decay_rate: float32 [8], replicated, may hold values from 0.0002 to 0.04
- seq_lengths: int32 [16, 2], P('wt'), may hold values from 0 to 2048, as said below
- out_grad: bfloat16 [16, 2048, 1024], P('wt', 'seq'), may hold values from -6 to 6
Outputs:
- layer_out: bfloat16 [16, 2048, 1024], P('wt', 'seq')
- input_grad: bfloat16 [16, 2048, 1024], P('wt', 'seq')
- grad_query: float32 [1024, 1024], P('wt')
- grad_key: float32 [1024, 1024], P('wt')
- grad_value: float32 [1024, 1024], P('wt')
- grad_gate: float32 [1024, 1024], P('wt')
- grad_out: float32 [1024, 1024], P('wt')
- grad_first: float32 [1024, 2816], P('wt')
- grad_second: float32 [1024, 2816], P('wt')
- grad_down: float32 [2816, 1024], P('wt')
Inputs may be any that keep to these rules, and one draw needn't show every extreme that they name: `seq_lengths`: row g lists the lengths of group g's sequences in token order, then zeros; each nonzero length is a multiple of 1024, a row sums to 2048, and no sequence crosses a multiple of min(4096, 2048) tokens.
All inputs are finite; a program needn't handle non-finite values.
Results may differ from a plain program's by a relative error of at most 0.02.
Values may be sent and summed in bfloat16 or wider, within the bound.
No kernel may reach another device: no remote copies, remote signals or barrier semaphores. Data moves between devices by JAX's collectives and lax.ppermute only.
A program may use at most 256 MiB of HBM per device.

v0:
```python
import jax
import jax.numpy as jnp
from jax import lax
from jax.sharding import PartitionSpec as P

H = 8
HD = 128
BLK = 512


epsilon = 1e-06
head_floor = 1.0
highest = lax.Precision.HIGHEST


def simple_norm(tensor, added=epsilon):
    scale_of = lax.rsqrt(jnp.mean(tensor * tensor, axis=-1, keepdims=True) + added)
    return (tensor * scale_of, scale_of)


def norm_back(normed, scale_of, incoming):
    return scale_of * (incoming - normed * jnp.mean(normed * incoming, axis=-1, keepdims=True))


def matmul(left, right):
    return jnp.dot(left, right, preferred_element_type=jnp.float32)


def transposed_left(left, right):
    return lax.dot_general(
        left, right, (((0,), (0,)), ((), ())), preferred_element_type=jnp.float32
    )


def transposed_right(left, right):
    return lax.dot_general(
        left, right, (((1,), (1,)), ((), ())), preferred_element_type=jnp.float32
    )


def seq_layout(lengths, row_count):
    starts = jnp.cumsum(lengths) - lengths
    live_slot = lengths > 0
    token_index = jnp.arange(row_count, dtype=jnp.int32)
    has_begun = (starts[None, :] <= token_index[:, None]) & live_slot[None, :]
    first_token = jnp.max(jnp.where(has_begun, starts[None, :], 0), axis=1)
    position = (token_index - first_token).astype(jnp.float32)
    block_first = jnp.arange(row_count // BLK, dtype=jnp.int32) * BLK
    is_start = jnp.any((starts[None, :] == block_first[:, None]) & live_slot[None, :], axis=1)
    return (position, is_start)


def decay_tables(head_rates):
    offsets = jnp.arange(BLK, dtype=jnp.float32)
    distance = offsets[:, None] - offsets[None, :]
    decay_mask = jnp.where(
        distance[None] >= 0,
        jnp.exp(-head_rates[:, None, None] * jnp.maximum(distance, 0.0)[None]),
        0.0,
    )
    decay_in = jnp.exp(-head_rates[None, :] * (offsets[:, None] + 1.0))
    decay_out = jnp.exp(-head_rates[None, :] * (BLK - 1.0 - offsets[:, None]))
    across = jnp.exp(-head_rates * BLK)
    return (decay_mask, decay_in, decay_out, across)


def rotation_tables(position):
    frequency = 10000.0 ** (-jnp.arange(HD, dtype=jnp.float32) / HD)
    angles = position[:, None] * frequency[None, :]
    return (jnp.cos(angles)[:, None, :], jnp.sin(angles)[:, None, :])


def rotate(heads, cosine, sine_table):
    heads_float = heads.astype(jnp.float32)
    return jnp.concatenate([heads_float * cosine, heads_float * sine_table], axis=-1).astype(
        jnp.bfloat16
    )


def unrotate(incoming, cosine, sine_table):
    return incoming[..., :HD] * cosine + incoming[..., HD:] * sine_table


def body(
    activations,
    w_query,
    w_key,
    w_value,
    w_gate,
    w_out,
    w_first,
    w_second,
    w_down,
    decay_rate,
    seq_lengths,
    out_grad,
):
    seq_count = lax.axis_size("seq")
    tok_rows = activations.shape[1]
    group_rows = tok_rows * seq_count
    heads_here = H // seq_count
    head_shape = (group_rows, heads_here, HD)
    x_float = activations[0].astype(jnp.float32)
    normed_in, scale_in = simple_norm(x_float)
    input_low = normed_in.astype(jnp.bfloat16)
    full_query, full_key, full_value, full_gate = (
        lax.all_gather(w_query, "wt", axis=0, tiled=True),
        lax.all_gather(w_key, "wt", axis=0, tiled=True),
        lax.all_gather(w_value, "wt", axis=0, tiled=True),
        lax.all_gather(w_gate, "wt", axis=0, tiled=True),
    )
    query_raw = matmul(input_low, full_query)
    key_raw = matmul(input_low, full_key)
    query_sig = jax.nn.sigmoid(query_raw)
    key_sig = jax.nn.sigmoid(key_raw)
    outgoing = jnp.stack(
        [
            query_raw * query_sig,
            key_raw * key_sig,
            matmul(input_low, full_value),
            matmul(input_low, full_gate),
        ]
    ).astype(jnp.bfloat16)
    headed = lax.all_to_all(outgoing, "seq", split_axis=2, concat_axis=1, tiled=True)
    query_heads = headed[0].reshape(head_shape)
    key_heads = headed[1].reshape(head_shape)
    value_heads = headed[2].reshape(head_shape)
    gate_float = headed[3].reshape(head_shape).astype(jnp.float32)
    head_rates = lax.dynamic_slice_in_dim(
        decay_rate, lax.axis_index("seq") * heads_here, heads_here
    )
    position, is_start = seq_layout(seq_lengths[0], group_rows)
    cosine, sine_table = rotation_tables(position)
    query_rot = rotate(query_heads, cosine, sine_table)
    key_rot = rotate(key_heads, cosine, sine_table)
    decay_mask, decay_in, decay_out, across = decay_tables(head_rates)
    nblocks = group_rows // BLK
    keep_next = 1.0 - jnp.concatenate([is_start[1:], jnp.ones((1,), dtype=bool)]).astype(
        jnp.float32
    )
    keep_prev = 1.0 - is_start.astype(jnp.float32)

    def blocked(tensor):
        return tensor.reshape((nblocks, BLK) + tensor.shape[1:])

    def forward_block(carried, item):
        query_block, key_block, value_block, keep_flag = item
        weights = (
            jnp.einsum("ihc,jhc->hij", query_block, key_block, preferred_element_type=jnp.float32)
            * decay_mask
        ).astype(jnp.bfloat16)
        inner_part = jnp.einsum(
            "hij,jhd->ihd", weights, value_block, preferred_element_type=jnp.float32
        )
        outer_part = (
            jnp.einsum("ihc,hcd->ihd", query_block.astype(jnp.float32), carried, precision=highest)
            * decay_in[:, :, None]
        )
        fresh_sum = jnp.einsum(
            "jhc,jhd->hcd",
            key_block.astype(jnp.float32) * decay_out[:, :, None],
            value_block.astype(jnp.float32),
            precision=highest,
        )
        updated = keep_flag * (across[:, None, None] * carried + fresh_sum)
        return (updated, (inner_part + outer_part, carried))

    zero_state = jnp.zeros((heads_here, 2 * HD, HD), jnp.float32)
    final_state, (mixed, states) = lax.scan(
        forward_block,
        zero_state,
        (blocked(query_rot), blocked(key_rot), blocked(value_heads), keep_next),
    )
    mixed = mixed.reshape(head_shape)
    normed_mix, scale_mix = simple_norm(mixed, head_floor)
    gated = (normed_mix * gate_float).astype(jnp.bfloat16).reshape(group_rows, heads_here * HD)
    returned = lax.all_to_all(gated, "seq", split_axis=0, concat_axis=1, tiled=True)
    full_out, full_first, full_second, full_down = (
        lax.all_gather(w_out, "wt", axis=0, tiled=True),
        lax.all_gather(w_first, "wt", axis=0, tiled=True),
        lax.all_gather(w_second, "wt", axis=0, tiled=True),
        lax.all_gather(w_down, "wt", axis=0, tiled=True),
    )
    residual = x_float + matmul(returned, full_out)
    normed_mid, scale_mid = simple_norm(residual)
    mid_low = normed_mid.astype(jnp.bfloat16)
    first_proj = matmul(mid_low, full_first)
    second_proj = matmul(mid_low, full_second)
    middle = (first_proj * second_proj).astype(jnp.bfloat16)
    layer_out = (residual + matmul(middle, full_down)).astype(jnp.bfloat16)[None]
    grad_ff = out_grad[0]
    grad_down = transposed_left(middle, grad_ff)
    grad_mid = transposed_right(grad_ff, full_down).astype(jnp.bfloat16).astype(jnp.float32)
    grad_one = (grad_mid * second_proj).astype(jnp.bfloat16)
    grad_two = (grad_mid * first_proj).astype(jnp.bfloat16)
    grad_first = transposed_left(mid_low, grad_one)
    grad_second = transposed_left(mid_low, grad_two)
    grad_norm_mid = transposed_right(grad_one, full_first) + transposed_right(grad_two, full_second)
    grad_resid = grad_ff.astype(jnp.float32) + norm_back(normed_mid, scale_mid, grad_norm_mid)
    grad_attn = grad_resid.astype(jnp.bfloat16)
    grad_out = transposed_left(returned, grad_attn)
    grad_gated = transposed_right(grad_attn, full_out).astype(jnp.bfloat16)
    grad_headed = lax.all_to_all(grad_gated, "seq", split_axis=1, concat_axis=0, tiled=True)
    grad_gated_h = grad_headed.reshape(head_shape).astype(jnp.float32)
    grad_gate_h = grad_gated_h * normed_mix
    grad_mix = norm_back(normed_mix, scale_mix, grad_gated_h * gate_float).astype(jnp.bfloat16)

    def backward_block(carried, item):
        query_block, key_block, value_block, grad_block, state_before, keep_flag = item
        weights = (
            jnp.einsum("ihc,jhc->hij", query_block, key_block, preferred_element_type=jnp.float32)
            * decay_mask
        ).astype(jnp.bfloat16)
        grad_weights = jnp.einsum(
            "ihd,jhd->hij", grad_block, value_block, preferred_element_type=jnp.float32
        )
        grad_scores = (grad_weights * decay_mask).astype(jnp.bfloat16)
        grad_float = grad_block.astype(jnp.float32)
        key_float = key_block.astype(jnp.float32)
        grad_q = jnp.einsum(
            "hij,jhc->ihc", grad_scores, key_block, preferred_element_type=jnp.float32
        )
        grad_q = grad_q + decay_in[:, :, None] * jnp.einsum(
            "ihd,hcd->ihc", grad_float, state_before, precision=highest
        )
        grad_k = jnp.einsum(
            "hij,ihc->jhc", grad_scores, query_block, preferred_element_type=jnp.float32
        )
        grad_k = grad_k + decay_out[:, :, None] * jnp.einsum(
            "jhd,hcd->jhc", value_block.astype(jnp.float32), carried, precision=highest
        )
        grad_v = jnp.einsum("hij,ihd->jhd", weights, grad_block, preferred_element_type=jnp.float32)
        grad_v = grad_v + jnp.einsum(
            "jhc,hcd->jhd", key_float * decay_out[:, :, None], carried, precision=highest
        )
        grad_state = (
            jnp.einsum(
                "ihc,ihd->hcd",
                query_block.astype(jnp.float32) * decay_in[:, :, None],
                grad_float,
                precision=highest,
            )
            + across[:, None, None] * carried
        )
        return (keep_flag * grad_state, (grad_q, grad_k, grad_v))

    first_carry, (grad_qrot, grad_krot, grad_vheads) = lax.scan(
        backward_block,
        zero_state,
        (
            blocked(query_rot),
            blocked(key_rot),
            blocked(value_heads),
            blocked(grad_mix),
            states,
            keep_prev,
        ),
        reverse=True,
    )
    grad_query_h = unrotate(grad_qrot.reshape(group_rows, heads_here, 2 * HD), cosine, sine_table)
    grad_key_h = unrotate(grad_krot.reshape(group_rows, heads_here, 2 * HD), cosine, sine_table)
    back_stack = jnp.stack(
        [grad_query_h, grad_key_h, grad_vheads.reshape(head_shape), grad_gate_h]
    ).astype(jnp.bfloat16)
    back_stack = back_stack.reshape(4, group_rows, heads_here * HD)
    token_grads = lax.all_to_all(back_stack, "seq", split_axis=1, concat_axis=2, tiled=True)
    grad_query_raw = (
        token_grads[0].astype(jnp.float32) * (query_sig * (1.0 + query_raw * (1.0 - query_sig)))
    ).astype(jnp.bfloat16)
    grad_key_raw = (
        token_grads[1].astype(jnp.float32) * (key_sig * (1.0 + key_raw * (1.0 - key_sig)))
    ).astype(jnp.bfloat16)
    grad_value_raw = token_grads[2]
    grad_gate_raw = token_grads[3]
    grad_query = transposed_left(input_low, grad_query_raw)
    grad_key = transposed_left(input_low, grad_key_raw)
    grad_value = transposed_left(input_low, grad_value_raw)
    grad_gate = transposed_left(input_low, grad_gate_raw)
    grad_norm_in = (
        transposed_right(grad_query_raw, full_query)
        + transposed_right(grad_key_raw, full_key)
        + transposed_right(grad_value_raw, full_value)
        + transposed_right(grad_gate_raw, full_gate)
    )
    input_grad = (grad_resid + norm_back(normed_in, scale_in, grad_norm_in)).astype(jnp.bfloat16)[
        None
    ]
    shares = (
        lax.psum_scatter(
            grad_query.astype(jnp.bfloat16), "wt", scatter_dimension=0, tiled=True
        ).astype(jnp.float32),
        lax.psum_scatter(
            grad_key.astype(jnp.bfloat16), "wt", scatter_dimension=0, tiled=True
        ).astype(jnp.float32),
        lax.psum_scatter(
            grad_value.astype(jnp.bfloat16), "wt", scatter_dimension=0, tiled=True
        ).astype(jnp.float32),
        lax.psum_scatter(
            grad_gate.astype(jnp.bfloat16), "wt", scatter_dimension=0, tiled=True
        ).astype(jnp.float32),
        lax.psum_scatter(
            grad_out.astype(jnp.bfloat16), "wt", scatter_dimension=0, tiled=True
        ).astype(jnp.float32),
        lax.psum_scatter(
            grad_first.astype(jnp.bfloat16), "wt", scatter_dimension=0, tiled=True
        ).astype(jnp.float32),
        lax.psum_scatter(
            grad_second.astype(jnp.bfloat16), "wt", scatter_dimension=0, tiled=True
        ).astype(jnp.float32),
        lax.psum_scatter(
            grad_down.astype(jnp.bfloat16), "wt", scatter_dimension=0, tiled=True
        ).astype(jnp.float32),
    )
    totals = (
        lax.psum(shares[0].astype(jnp.bfloat16), "seq").astype(jnp.float32),
        lax.psum(shares[1].astype(jnp.bfloat16), "seq").astype(jnp.float32),
        lax.psum(shares[2].astype(jnp.bfloat16), "seq").astype(jnp.float32),
        lax.psum(shares[3].astype(jnp.bfloat16), "seq").astype(jnp.float32),
        lax.psum(shares[4].astype(jnp.bfloat16), "seq").astype(jnp.float32),
        lax.psum(shares[5].astype(jnp.bfloat16), "seq").astype(jnp.float32),
        lax.psum(shares[6].astype(jnp.bfloat16), "seq").astype(jnp.float32),
        lax.psum(shares[7].astype(jnp.bfloat16), "seq").astype(jnp.float32),
    )
    return (
        layer_out,
        input_grad,
        totals[0],
        totals[1],
        totals[2],
        totals[3],
        totals[4],
        totals[5],
        totals[6],
        totals[7],
    )


def solution(mesh):
    return jax.shard_map(
        body,
        mesh=mesh,
        in_specs=(
            P("wt", "seq", None),
            P("wt", None),
            P("wt", None),
            P("wt", None),
            P("wt", None),
            P("wt", None),
            P("wt", None),
            P("wt", None),
            P("wt", None),
            P(),
            P("wt", None),
            P("wt", "seq", None),
        ),
        out_specs=(
            P("wt", "seq", None),
            P("wt", "seq", None),
            P("wt", None),
            P("wt", None),
            P("wt", None),
            P("wt", None),
            P("wt", None),
            P("wt", None),
            P("wt", None),
            P("wt", None),
        ),
        check_vma=False,
    )
```

profile of v0, /device:TPU:12, one launch (start us, length us, event | category | flops | bytes accessed | tf_op | source)
XLA Modules:
  0.0 1565.6 jit_solution(16223305629226824355)
XLA Ops:
  15.3 35.6 %all-gather.15.cloned.1.call-done = bf16[1024,1024]{1,0:T(8,128)(2,1)} async-done(((bf16[64,1024]{1,0:T(8,128)(2,1)}), bf16[1024,1024]{1,0:T(8,128)(2,1)}) %all-gather.15.cloned.1.call-update) | async-done | bytes 2097168 | tf_op jit(solution)/shard_map/all_gather | solution.py:110
  56.1 37.1 %all-gather.13.cloned.1.call-done = bf16[1024,1024]{1,0:T(8,128)(2,1)} async-done(((bf16[64,1024]{1,0:T(8,128)(2,1)}), bf16[1024,1024]{1,0:T(8,128)(2,1)}) %all-gather.13.cloned.1.call-update) | async-done | bytes 2097168 | tf_op jit(solution)/shard_map/all_gather | solution.py:109
  98.5 37.1 %all-gather.11.cloned.1.call-done = bf16[1024,1024]{1,0:T(8,128)(2,1)} async-done(((bf16[64,1024]{1,0:T(8,128)(2,1)}), bf16[1024,1024]{1,0:T(8,128)(2,1)}) %all-gather.11.cloned.1.call-update) | async-done | bytes 2097168 | tf_op jit(solution)/shard_map/all_gather | solution.py:108
  141.5 36.3 %all-gather.9.cloned.1.call-done = bf16[1024,1024]{1,0:T(8,128)(2,1)} async-done(((bf16[64,1024]{1,0:T(8,128)(2,1)}), bf16[1024,1024]{1,0:T(8,128)(2,1)}) %all-gather.9.cloned.1.call-update) | async-done | bytes 2097168 | tf_op jit(solution)/shard_map/all_gather | solution.py:107
  189.5 15.1 copy.266
  218.8 86.1 %all-to-all-done = bf16[4,1024,1024]{1,0,2:T(4,128)(2,1)} async-done(((bf16[4,1024,1024]{1,0,2:T(4,128)(2,1)}), bf16[4,1024,1024]{1,0,2:T(4,128)(2,1)}, u32[]{:S(2)}, u32[]{:S(2)}) %all-to-all-start) | async-done | bytes 8388640 | tf_op jit(solution)/shard_map/all_to_all | solution.py:124
  369.3 61.0 %while.42 = (s32[]{:T(128)}, f32[4,256,128]{2,1,0:T(8,128)S(1)}, f32[4,512,4,128]{1,3,2,0:T(8,128)}, f32[4,4,256,128]{3,2,1,0:T(8,128)}, f32[4]{0:T(128)S(1)}, /...) while((s32[]{:T(128)}, f32[4,256,128]{2,1,0:T(8,128)S(1)}, ...), condition=%wide.region_5.6_spmd.clone.clone.clone.clone, body=%wide.region_4.5_spmd.clone.clone.clone.sunk.clone | while | flops 2422476800 | bytes 16552681 | solution.py:169
  480.0 21.2 %all-to-all-done.1 = bf16[2,1024,512]{1,2,0:T(8,128)(2,1)} async-done(((bf16[2,1024,512]{1,2,0:T(8,128)(2,1)}), bf16[2,1024,512]{1,2,0:T(8,128)(2,1)}, u32[]{:S(2)}, u32[]{:S(2)}) %all-to-all-start.1) | async-done | bytes 2097184 | tf_op jit(solution)/shard_map/all_to_all | solution.py:177
  520.6 12.0 fusion.155
  532.6 16.0 %multiply_convert_fusion = (bf16[1024,2816]{1,0:T(8,128)(2,1)}, f32[1024,2816]{1,0:T(8,128)}) fusion(f32[1024,2816]{1,0:T(8,128)} %fusion.155, bf16[1024,1024]{0,1:T(8,128)(2,1)S(1)} %copy-done.31, bf16[1024,2816]{1,0:T(8,128)(2,1)} %all-gather.19.cloned.1.call-done), kind=kOutput, calls=%fused_computation.104 | convolution fusion | flops 5911347200 | bytes 36700160 | tf_op jit(solution)/shard_map/dot_general | solution.py:26
  560.0 14.8 multiply_reduce_fusion.1
  654.9 152.1 %while.43 = (s32[]{:T(128)}, f32[4,256,128]{2,1,0:T(8,128)}, f32[4,512,4,256]{3,1,0,2:T(8,128)}, f32[4,512,4,256]{3,1,0,2:T(8,128)}, bf16[4,512,4,128]{1,3,2,0:T...) while((s32[]{:T(128)}, f32[4,256,128]{2,1,0:T(8,128)}, ...), condition=%wide.region_11.12_spmd.clone.clone.clone.clone, body=%wide.region_10.11_spmd.clone.clone.clone.sunk.clone | while | flops 5382344704 | bytes 83939856 | solution.py:247
  837.4 14.5 copy.300
  865.6 85.0 %all-to-all-done.3 = bf16[4,2048,512]{2,0,1:T(4,128)(2,1)} async-done(((bf16[4,2048,512]{2,0,1:T(4,128)(2,1)}), bf16[4,2048,512]{2,0,1:T(4,128)(2,1)}, u32[]{:S(2)}, u32[]{:S(2)}) %all-to-all-start.3) | async-done | bytes 8388640 | tf_op jit(solution)/shard_map/all_to_all | solution.py:266
  1011.0 14.4 convolution_convert_fusion.2
  1025.5 14.3 convolution_convert_fusion.1
  1051.3 11.8 fusion.126
  1082.6 20.9 %reduce-scatter.11.cloned.1.call-done = bf16[64,1024]{1,0:T(8,128)(2,1)} async-done(((bf16[1024,1024]{1,0:T(8,128)(2,1)}), bf16[64,1024]{1,0:T(8,128)(2,1)}) %reduce-scatter.11.cloned.1.call-update) | async-done | bytes 131088 | tf_op jit(solution)/shard_map/reduce_scatter | solution.py:292
  1103.5 64.6 %reduce-scatter.13.cloned.1.call-done = bf16[64,1024]{1,0:T(8,128)(2,1)} async-done(((bf16[1024,1024]{1,0:T(8,128)(2,1)}), bf16[64,1024]{1,0:T(8,128)(2,1)}) %reduce-scatter.13.cloned.1.call-update) | async-done | bytes 131088 | tf_op jit(solution)/shard_map/reduce_scatter | solution.py:295
  1168.2 64.3 %reduce-scatter.15.cloned.1.call-done = bf16[64,1024]{1,0:T(8,128)(2,1)} async-done(((bf16[1024,1024]{1,0:T(8,128)(2,1)}), bf16[64,1024]{1,0:T(8,128)(2,1)}) %reduce-scatter.15.cloned.1.call-update) | async-done | bytes 131088 | tf_op jit(solution)/shard_map/reduce_scatter | solution.py:298
  1232.5 84.3 %reduce-scatter.19.cloned.1.call-done = bf16[64,2816]{1,0:T(8,128)(2,1)} async-done(((bf16[1024,2816]{1,0:T(8,128)(2,1)}), bf16[64,2816]{1,0:T(8,128)(2,1)}) %reduce-scatter.19.cloned.1.call-update) | async-done | bytes 360464 | tf_op jit(solution)/shard_map/reduce_scatter | solution.py:304
  1316.8 85.0 %reduce-scatter.21.cloned.1.call-done = bf16[64,2816]{1,0:T(8,128)(2,1)} async-done(((bf16[1024,2816]{1,0:T(8,128)(2,1)}), bf16[64,2816]{1,0:T(8,128)(2,1)}) %reduce-scatter.21.cloned.1.call-update) | async-done | bytes 360464 | tf_op jit(solution)/shard_map/reduce_scatter | solution.py:307
  1401.8 85.0 %reduce-scatter.23.cloned.1.call-done = bf16[176,1024]{1,0:T(8,128)(2,1)} async-done(((bf16[2816,1024]{1,0:T(8,128)(2,1)}), bf16[176,1024]{1,0:T(8,128)(2,1)}) %reduce-scatter.23.cloned.1.call-update) | async-done | bytes 360464 | tf_op jit(solution)/shard_map/reduce_scatter | solution.py:310
  1502.0 43.7 %all-reduce.3.cloned.1.call-done = (bf16[64,1024]{1,0:T(8,128)(2,1)}, bf16[64,1024]{1,0:T(8,128)(2,1)}, bf16[64,1024]{1,0:T(8,128)(2,1)}, bf16[64,1024]{1,0:T(8,...) async-done(((bf16[64,1024]{1,0:T(8,128)(2,1)}, bf16[64,1024]{1,0:T(8,128)(2,1)}, ...) | async-done | bytes 1736720 | tf_op jit(solution)/shard_map/psum | solution.py:315
  (419 shorter events, 650.4 us)
Async XLA Ops:
  7.2 43.7 %all-gather.15.cloned.1.call-start = ((), (), s32[]{:S(2)}) async-start(), calls=%async_computation.15 | async-start | bytes 2228224 | tf_op jit(solution)/shard_map/all_gather | solution.py:110
  7.9 85.3 %all-gather.13.cloned.1.call-start = ((), (), s32[]{:S(2)}) async-start(), calls=%async_computation.14 | async-start | bytes 2228224 | tf_op jit(solution)/shard_map/all_gather | solution.py:109
  8.7 126.9 %all-gather.11.cloned.1.call-start = ((), (), s32[]{:S(2)}) async-start(), calls=%async_computation.13 | async-start | bytes 2228224 | tf_op jit(solution)/shard_map/all_gather | solution.py:108
  9.4 168.4 %all-gather.9.cloned.1.call-start = ((), (), s32[]{:S(2)}) async-start(), calls=%async_computation.12 | async-start | bytes 2228224 | tf_op jit(solution)/shard_map/all_gather | solution.py:107
  10.0 470.0 %all-gather.17.cloned.1.call-start = ((), (), s32[]{:S(2)}) async-start(), calls=%async_computation.16 | async-start | bytes 2228224 | tf_op jit(solution)/shard_map/all_gather | solution.py:179
  10.6 499.5 %all-gather.23.cloned.1.call-start = ((), (), s32[]{:S(2)}) async-start(), calls=%async_computation.19 | async-start | bytes 6127616 | tf_op jit(solution)/shard_map/all_gather | solution.py:182
  11.1 509.5 %all-gather.21.cloned.1.call-start = ((), (), s32[]{:S(2)}) async-start(), calls=%async_computation.18 | async-start | bytes 6127616 | tf_op jit(solution)/shard_map/all_gather | solution.py:181
  14.8 163.0 %copy-start.10 = (bf16[1,1024,1024]{1,2,0:T(8,128)(2,1)}, bf16[1,1024,1024]{1,2,0:T(8,128)(2,1)S(1)}, u32[]{:S(2)}) copy-start(bf16[1,1024,1024]{1,2,0:T(8,128)(2,1)S(1)} %copy.265) | copy-start | bytes 6291460
  15.3 162.5 %copy-start.41 = (f32[1024]{0:T(1024)}, f32[1024]{0:T(1024)S(1)}, u32[]{:S(2)}) copy-start(f32[1024]{0:T(1024)S(1)} %add_rsqrt_fusion.2) | copy-start | bytes 12292
  204.6 100.3 %all-to-all-start = ((bf16[4,1024,1024]{1,0,2:T(4,128)(2,1)}), bf16[4,1024,1024]{1,0,2:T(4,128)(2,1)}, u32[]{:S(2)}, u32[]{:S(2)}) async-start(bf16[4,1024,1024]{1,0,2:T(4,128)(2,1)} %copy.266), calls=%async_computation | async-start | bytes 16777216 | tf_op jit(solution)/shard_map/all_to_all | solution.py:124
  211.8 320.8 %all-gather.19.cloned.1.call-start = ((), (), s32[]{:S(2)}) async-start(), calls=%async_computation.17 | async-start | bytes 6127616 | tf_op jit(solution)/shard_map/all_gather | solution.py:180
  213.5 101.1 %copy-start.43 = (f32[128]{0:T(128)}, f32[128]{0:T(128)S(1)}, u32[]{:S(2)}) copy-start(f32[128]{0:T(128)S(1)} %multiply_power_fusion) | copy-start | bytes 1540
  471.1 30.1 %all-to-all-start.1 = ((bf16[2,1024,512]{1,2,0:T(8,128)(2,1)}), bf16[2,1024,512]{1,2,0:T(8,128)(2,1)}, u32[]{:S(2)}, u32[]{:S(2)}) async-start(bf16[2,1024,512]{1,2,0:T(8,128)(2,1)} %fusion.125), calls=%async_computation.1 | async-start | bytes 4194304 | tf_op jit(solution)/shard_map/all_to_all | solution.py:177
  581.4 33.1 %all-to-all-start.2 = ((bf16[1024,2,512]{2,0,1:T(8,128)(2,1)}), bf16[1024,2,512]{2,0,1:T(8,128)(2,1)S(1)}, u32[]{:S(2)}, u32[]{:S(2)}) async-start(bf16[1024,2,512]{2,0,1:T(8,128)(2,1)} %copy.281), calls=%async_computation.2 | async-start | bytes 4194304 | tf_op jit(solution)/shard_map/all_to_all | solution.py:203
  851.9 98.7 %all-to-all-start.3 = ((bf16[4,2048,512]{2,0,1:T(4,128)(2,1)}), bf16[4,2048,512]{2,0,1:T(4,128)(2,1)}, u32[]{:S(2)}, u32[]{:S(2)}) async-start(bf16[4,2048,512]{2,0,1:T(4,128)(2,1)} %copy.300), calls=%async_computation.3 | async-start | bytes 16777216 | tf_op jit(solution)/shard_map/all_to_all | solution.py:266
  858.9 223.7 %reduce-scatter.17.cloned.1.call-start = ((), (), s32[]{:S(2)}) async-start(), calls=%async_computation.24 | async-start | bytes 2228224 | tf_op jit(solution)/shard_map/reduce_scatter | solution.py:301
  865.6 217.0 %reduce-scatter.9.cloned.1.call-start = ((), (), s32[]{:S(2)}) async-start(), calls=%async_computation.20 | async-start | bytes 2228224 | tf_op jit(solution)/shard_map/reduce_scatter | solution.py:289
  977.5 126.1 %reduce-scatter.11.cloned.1.call-start = ((), (), s32[]{:S(2)}) async-start(), calls=%async_computation.21 | async-start | bytes 2228224 | tf_op jit(solution)/shard_map/reduce_scatter | solution.py:292
  992.0 176.1 %reduce-scatter.13.cloned.1.call-start = ((), (), s32[]{:S(2)}) async-start(), calls=%async_computation.22 | async-start | bytes 2228224 | tf_op jit(solution)/shard_map/reduce_scatter | solution.py:295
  1001.4 231.0 %reduce-scatter.15.cloned.1.call-start = ((), (), s32[]{:S(2)}) async-start(), calls=%async_computation.23 | async-start | bytes 2228224 | tf_op jit(solution)/shard_map/reduce_scatter | solution.py:298
  1011.0 305.8 %reduce-scatter.19.cloned.1.call-start = ((), (), s32[]{:S(2)}) async-start(), calls=%async_computation.25 | async-start | bytes 6127616 | tf_op jit(solution)/shard_map/reduce_scatter | solution.py:304
  1025.5 376.3 %reduce-scatter.21.cloned.1.call-start = ((), (), s32[]{:S(2)}) async-start(), calls=%async_computation.26 | async-start | bytes 6127616 | tf_op jit(solution)/shard_map/reduce_scatter | solution.py:307
  1039.9 447.0 %reduce-scatter.23.cloned.1.call-start = ((), (), s32[]{:S(2)}) async-start(), calls=%async_computation.27 | async-start | bytes 6127616 | tf_op jit(solution)/shard_map/reduce_scatter | solution.py:310
  1051.0 494.7 %all-reduce.3.cloned.1.call-start = ((), (), s32[]{:S(2)}) async-start(), calls=%async_computation.28 | async-start | bytes 3473408 | tf_op jit(solution)/shard_map/psum | solution.py:315
  (76 other events, 360.9 us)
Sparse Core Ops, SparseCore 0:
  10.2 40.6 all-gather.14
  53.0 40.1 all-gather.12
  95.4 40.1 all-gather.10
  137.6 40.1 all-gather.8
  179.8 40.1 all-gather.16
  222.1 58.8 all-gather.22
  283.3 57.6 all-gather.20
  343.3 57.6 all-gather.18
  865.7 62.8 reduce-scatter.16
  977.6 61.5 reduce-scatter.8
  1043.0 60.5 reduce-scatter.10
  1107.6 60.5 reduce-scatter.12
  1171.9 60.5 reduce-scatter.14
  1236.7 80.0 reduce-scatter.18
  1321.0 80.7 reduce-scatter.20
  1406.1 80.7 reduce-scatter.22
  1489.6 56.0 all-reduce.2
where the time goes:
time: 1580 us; the launch traced here: 1570 us
  waiting for transfers between devices  791 us (50%)
  matrix products  318 us (20%)
  local copies, waits for them, and re-layouts  294 us (19%)
  other arithmetic  121 us (8%)
  starting transfers between devices  24.8 us (2%)
    all_to_all x1, waiting for transfers between devices, body(): lax.all_to_all(outgoing, 'seq', split_axis=2, concat_axis=1, tiled=True)  86.1 us
    reduce_scatter x1, waiting for transfers between devices, body(): lax.psum_scatter(grad_down.astype(jnp.bfloat16), 'wt', scatter_dimension=...  85 us
    reduce_scatter x1, waiting for transfers between devices, body(): lax.psum_scatter(grad_second.astype(jnp.bfloat16), 'wt', scatter_dimensio...  85 us
    all_to_all x1, waiting for transfers between devices, body(): lax.all_to_all(back_stack, 'seq', split_axis=1, concat_axis=2, tiled=True)  85 us
    reduce_scatter x1, waiting for transfers between devices, body(): lax.psum_scatter(grad_first.astype(jnp.bfloat16), 'wt', scatter_dimension...  84.3 us
    dot_general x8, matrix products, matmul(): return jnp.dot(left, right, preferred_element_type=jnp.float32)  65.2 us
    reduce_scatter x1, waiting for transfers between devices, body(): lax.psum_scatter(grad_value.astype(jnp.bfloat16), 'wt', scatter_dimension...  64.6 us
    dot_general x8, matrix products, transposed_left(): lax.dot_general(left, right, (((0,), (0,)), ((), ())), preferred_element_...  64.3 us
  transfers between devices with their start and end apart: 21, of which 14 were waited for; matrix products, arithmetic and copies ran while one was open for 27% of the time, Pallas kernels for 0%

commit v1 on v0

v1 whole, which is shorter than its diff:
```python
import jax
import jax.numpy as jnp
from jax import lax
from jax.experimental import pallas as pl
from jax.experimental.pallas import tpu as pltpu
from jax.sharding import PartitionSpec as P

H = 8
HD = 128
CH = 256
TILE = 256
MIN_LEN = 1024
VMEM_LIMIT = 60 << 20

epsilon = 1e-06
head_floor = 1.0
bf16 = jnp.bfloat16
f32 = jnp.float32


def nn(left, right):
    return jnp.dot(left, right, preferred_element_type=f32)


def nt(left, right):
    return lax.dot_general(left, right, (((1,), (1,)), ((), ())), preferred_element_type=f32)


def tn(left, right):
    return lax.dot_general(left, right, (((0,), (0,)), ((), ())), preferred_element_type=f32)


def struct(shape, dtype):
    return jax.ShapeDtypeStruct(shape, dtype)


def fixed(shape):
    zeros = (0,) * len(shape)
    return pl.BlockSpec(shape, lambda i: zeros, pipeline_mode=pl.Buffered(1))


def columns(rows, width):
    return pl.BlockSpec((rows, width), lambda i: (0, i))


def row_tiles(height, cols):
    return pl.BlockSpec((height, cols), lambda i: (i, 0))


def smem():
    return pl.BlockSpec(memory_space=pltpu.SMEM)


def params():
    return pltpu.CompilerParams(vmem_limit_bytes=VMEM_LIMIT)


def cost(flops, moved):
    return pl.CostEstimate(flops=flops, bytes_accessed=moved, transcendentals=0)


def decay_in_of(rate):
    row = lax.broadcasted_iota(jnp.int32, (CH, HD), 0).astype(f32)
    return jnp.exp(-rate * (row + 1.0))


def decay_out_of(rate):
    row = lax.broadcasted_iota(jnp.int32, (CH, HD), 0).astype(f32)
    return jnp.exp(-rate * (CH - 1.0 - row))


def double(table):
    return jnp.concatenate([table, table], axis=1)


def rotated(heads, cosine, sine):
    return jnp.concatenate([heads * cosine, heads * sine], axis=1)


def swish(raw):
    return raw * jax.nn.sigmoid(raw)


def swish_slope(raw):
    sig = jax.nn.sigmoid(raw)
    return sig * (1.0 + raw * (1.0 - sig))


def head_columns(s):
    return slice(s * HD, (s + 1) * HD)


def key_value_kernel(rates, across, a, wk, wv, cosine, sine, kraw_out, v_out, state_out):
    step = pl.program_id(0)
    rows = a.shape[0]
    kraw = nn(a[...], wk[...])
    v_out[...] = nn(a[...], wv[...]).astype(bf16)
    kraw_out[...] = kraw.astype(bf16)
    for s in range(TILE // HD):
        head = step * (TILE // HD) + s
        cols = head_columns(s)
        tail = double(decay_out_of(rates[head]))
        state = jnp.zeros((HD, 2 * HD), f32)
        for c in range(rows // CH):
            span = slice(c * CH, (c + 1) * CH)
            key = swish(kraw[span, cols])
            faded = rotated(key, cosine[span, :], sine[span, :]) * tail
            state = across[head] * state + tn(v_out[span, cols], faded.astype(bf16))
        state_out[s] = state


def key_value(rates, across, a, wk, wv, cosine, sine):
    rows, depth = a.shape
    width = wk.shape[1]
    return pl.pallas_call(
        key_value_kernel,
        grid=(width // TILE,),
        in_specs=[
            smem(),
            smem(),
            fixed((rows, depth)),
            columns(depth, TILE),
            columns(depth, TILE),
            fixed((rows, HD)),
            fixed((rows, HD)),
        ],
        out_specs=[
            columns(rows, TILE),
            columns(rows, TILE),
            pl.BlockSpec((TILE // HD, HD, 2 * HD), lambda i: (i, 0, 0)),
        ],
        out_shape=[
            struct((rows, width), bf16),
            struct((rows, width), bf16),
            struct((H, HD, 2 * HD), f32),
        ],
        compiler_params=params(),
        cost_estimate=cost(4 * rows * depth * width, 2 * (3 * rows * depth + 2 * depth * width)),
        name="key_value",
    )(rates, across, a, wk, wv, cosine, sine)


def mix_kernel(
    rates, across, a, wq, wg, kraw, v, cosine, sine, state_in, qraw_out, u_out, o_out, gated_out
):
    step = pl.program_id(0)
    rows = a.shape[0]
    qraw = nn(a[...], wq[...])
    qraw_out[...] = qraw.astype(bf16)
    u_out[...] = nn(a[...], wg[...]).astype(bf16)
    row = lax.broadcasted_iota(jnp.int32, (CH, CH), 0)
    col = lax.broadcasted_iota(jnp.int32, (CH, CH), 1)
    distance = (row - col).astype(f32)
    for s in range(TILE // HD):
        head = step * (TILE // HD) + s
        cols = head_columns(s)
        rate = rates[head]
        tail = double(decay_out_of(rate))
        lead = decay_in_of(rate)
        mask = jnp.where(distance >= 0, jnp.exp(-rate * jnp.maximum(distance, 0.0)), 0.0)
        state = state_in[s]
        for c in range(rows // CH):
            span = slice(c * CH, (c + 1) * CH)
            cos_c, sin_c = cosine[span, :], sine[span, :]
            query = rotated(swish(qraw[span, cols]), cos_c, sin_c).astype(bf16)
            key_float = rotated(swish(kraw[span, cols].astype(f32)), cos_c, sin_c)
            key = key_float.astype(bf16)
            value = v[span, cols]
            weights = (nt(query, key) * mask).astype(bf16)
            o = nn(weights, value) + lead * nt(query, state.astype(bf16))
            state = across[head] * state + tn(value, (key_float * tail).astype(bf16))
            o_out[span, cols] = o.astype(bf16)
            scale = lax.rsqrt(jnp.mean(o * o, axis=1, keepdims=True) + head_floor)
            gated_out[span, cols] = (o * scale * u_out[span, cols].astype(f32)).astype(bf16)


def mix(rates, across, a, wq, wg, kraw, v, cosine, sine, state_in):
    rows, depth = a.shape
    width = wq.shape[1]
    return pl.pallas_call(
        mix_kernel,
        grid=(width // TILE,),
        in_specs=[
            smem(),
            smem(),
            fixed((rows, depth)),
            columns(depth, TILE),
            columns(depth, TILE),
            columns(rows, TILE),
            columns(rows, TILE),
            fixed((rows, HD)),
            fixed((rows, HD)),
            pl.BlockSpec((TILE // HD, HD, 2 * HD), lambda i: (i, 0, 0)),
        ],
        out_specs=[columns(rows, TILE)] * 4,
        out_shape=[struct((rows, width), bf16)] * 4,
        compiler_params=params(),
        cost_estimate=cost(8 * rows * depth * width, 2 * (7 * rows * depth + 2 * depth * width)),
        name="mix",
    )(rates, across, a, wq, wg, kraw, v, cosine, sine, state_in)


def residual_kernel(x, gated, wo, h1_out, bn_out, bnt_out):
    h1 = x[...].astype(f32) + nn(gated[...], wo[...])
    h1_out[...] = h1
    normed = h1 * lax.rsqrt(jnp.mean(h1 * h1, axis=1, keepdims=True) + epsilon)
    low = normed.astype(bf16)
    bn_out[...] = low
    bnt_out[...] = low.T


def residual(x, gated, wo):
    rows, depth = x.shape
    part = 512
    return pl.pallas_call(
        residual_kernel,
        grid=(rows // part,),
        in_specs=[row_tiles(part, depth), row_tiles(part, depth), fixed(wo.shape)],
        out_specs=[row_tiles(part, depth), row_tiles(part, depth), columns(depth, part)],
        out_shape=[
            struct((rows, depth), f32),
            struct((rows, depth), bf16),
            struct((depth, rows), bf16),
        ],
        compiler_params=params(),
        cost_estimate=cost(2 * rows * depth * depth, 14 * rows * depth),
        name="residual",
    )(x, gated, wo)


def feed_kernel(
    h1, bn, bnt, og, w1, w2, wd, g1_out, g2_out, gd_out, y_out, dh1_out, dattn_out, total, dbn
):
    step = pl.program_id(0)

    @pl.when(step == 0)
    def _():
        total[...] = h1[...]
        dbn[...] = jnp.zeros_like(dbn)

    first = nn(bn[...], w1[...])
    second = nn(bn[...], w2[...])
    middle = (first * second).astype(bf16)
    dmid = nt(og[...], wd[...])
    total[...] += nn(middle, wd[...])
    d_first = (dmid * second).astype(bf16)
    d_second = (dmid * first).astype(bf16)
    dbn[...] += nt(d_first, w1[...]) + nt(d_second, w2[...])
    g1_out[...] = nn(bnt[...], d_first).astype(bf16)
    g2_out[...] = nn(bnt[...], d_second).astype(bf16)
    gd_out[...] = tn(middle, og[...]).astype(bf16)

    @pl.when(step == pl.num_programs(0) - 1)
    def _():
        y_out[...] = total[...].astype(bf16)
        hidden = h1[...]
        scale = lax.rsqrt(jnp.mean(hidden * hidden, axis=1, keepdims=True) + epsilon)
        normed = hidden * scale
        incoming = dbn[...]
        dh1 = og[...].astype(f32) + scale * (
            incoming - normed * jnp.mean(normed * incoming, axis=1, keepdims=True)
        )
        dh1_out[...] = dh1
        dattn_out[...] = dh1.astype(bf16)


def feed(h1, bn, bnt, og, w1, w2, wd):
    rows, depth = h1.shape
    hidden = w1.shape[1]
    return pl.pallas_call(
        feed_kernel,
        grid=(hidden // TILE,),
        in_specs=[
            fixed((rows, depth)),
            fixed((rows, depth)),
            fixed((depth, rows)),
            fixed((rows, depth)),
            columns(depth, TILE),
            columns(depth, TILE),
            row_tiles(TILE, depth),
        ],
        out_specs=[
            columns(depth, TILE),
            columns(depth, TILE),
            row_tiles(TILE, depth),
            fixed((rows, depth)),
            fixed((rows, depth)),
            fixed((rows, depth)),
        ],
        out_shape=[
            struct((depth, hidden), bf16),
            struct((depth, hidden), bf16),
            struct((hidden, depth), bf16),
            struct((rows, depth), bf16),
            struct((rows, depth), f32),
            struct((rows, depth), bf16),
        ],
        scratch_shapes=[pltpu.VMEM((rows, depth), f32), pltpu.VMEM((rows, depth), f32)],
        compiler_params=params(),
        cost_estimate=cost(18 * rows * depth * hidden, 12 * depth * hidden + 20 * rows * depth),
        name="feed",
    )(h1, bn, bnt, og, w1, w2, wd)


def gate_back_kernel(
    rates, across, dattn, wo, o_in, u_in, qraw, cosine, sine, du_out, do_out, back_out
):
    step = pl.program_id(0)
    rows = dattn.shape[0]
    dgated = nt(dattn[...], wo[...]).astype(bf16).astype(f32)
    for s in range(TILE // HD):
        head = step * (TILE // HD) + s
        cols = head_columns(s)
        lead = double(decay_in_of(rates[head]))
        back = jnp.zeros((HD, 2 * HD), f32)
        for c in reversed(range(rows // CH)):
            span = slice(c * CH, (c + 1) * CH)
            o = o_in[span, cols].astype(f32)
            scale = lax.rsqrt(jnp.mean(o * o, axis=1, keepdims=True) + head_floor)
            normed = o * scale
            incoming = dgated[span, cols]
            du_out[span, cols] = (incoming * normed).astype(bf16)
            spread = incoming * u_in[span, cols].astype(f32)
            do = scale * (spread - normed * jnp.mean(normed * spread, axis=1, keepdims=True))
            low = do.astype(bf16)
            do_out[span, cols] = low
            query = rotated(
                swish(qraw[span, cols].astype(f32)), cosine[span, :], sine[span, :]
            )
            back = across[head] * back + tn(low, (query * lead).astype(bf16))
        back_out[s] = back


def gate_back(rates, across, dattn, wo, o_in, u_in, qraw, cosine, sine):
    rows, depth = dattn.shape
    return pl.pallas_call(
        gate_back_kernel,
        grid=(depth // TILE,),
        in_specs=[
            smem(),
            smem(),
            fixed((rows, depth)),
            row_tiles(TILE, depth),
            columns(rows, TILE),
            columns(rows, TILE),
            columns(rows, TILE),
            fixed((rows, HD)),
            fixed((rows, HD)),
        ],
        out_specs=[
            columns(rows, TILE),
            columns(rows, TILE),
            pl.BlockSpec((TILE // HD, HD, 2 * HD), lambda i: (i, 0, 0)),
        ],
        out_shape=[
            struct((rows, depth), bf16),
            struct((rows, depth), bf16),
            struct((H, HD, 2 * HD), f32),
        ],
        compiler_params=params(),
        cost_estimate=cost(3 * rows * depth * depth, 16 * rows * depth),
        name="gate_back",
    )(rates, across, dattn, wo, o_in, u_in, qraw, cosine, sine)


def mix_back_kernel(
    rates,
    across,
    qraw,
    kraw,
    v,
    do_in,
    cosine,
    sine,
    state_in,
    back_in,
    dq_out,
    dk_out,
    dv_out,
    query_s,
    key_s,
):
    step = pl.program_id(0)
    rows = qraw.shape[0]
    count = rows // CH
    row = lax.broadcasted_iota(jnp.int32, (CH, CH), 0)
    col = lax.broadcasted_iota(jnp.int32, (CH, CH), 1)
    distance = (row - col).astype(f32)
    for s in range(TILE // HD):
        head = step * (TILE // HD) + s
        cols = head_columns(s)
        rate = rates[head]
        lead = double(decay_in_of(rate))
        tail = double(decay_out_of(rate))
        mask = jnp.where(distance >= 0, jnp.exp(-rate * jnp.maximum(distance, 0.0)), 0.0)
        mask_t = jnp.where(distance <= 0, jnp.exp(rate * jnp.minimum(distance, 0.0)), 0.0)
        state = state_in[s]
        states = []
        for c in range(count):
            span = slice(c * CH, (c + 1) * CH)
            key_float = rotated(
                swish(kraw[span, cols].astype(f32)), cosine[span, :], sine[span, :]
            )
            key_s[span, :] = key_float.astype(bf16)
            states.append(state.astype(bf16))
            if c < count - 1:
                state = across[head] * state + tn(v[span, cols], (key_float * tail).astype(bf16))
        back = back_in[s]
        for c in reversed(range(count)):
            span = slice(c * CH, (c + 1) * CH)
            cos_c, sin_c = cosine[span, :], sine[span, :]
            query_raw = qraw[span, cols].astype(f32)
            query_float = rotated(swish(query_raw), cos_c, sin_c)
            query = query_float.astype(bf16)
            key = key_s[span, :]
            value = v[span, cols]
            do = do_in[span, cols]
            back_low = back.astype(bf16)
            weights_t = (nt(key, query) * mask_t).astype(bf16)
            dscore = (nt(do, value) * mask).astype(bf16)
            dscore_t = (nt(value, do) * mask_t).astype(bf16)
            dqr = nn(dscore, key) + lead * nn(do, states[c])
            dkr = nn(dscore_t, query) + tail * nn(value, back_low)
            dv = nn(weights_t, do) + tail[:, :HD] * nt(key, back_low)
            back = across[head] * back + tn(do, (query_float * lead).astype(bf16))
            dq = dqr[:, :HD] * cos_c + dqr[:, HD:] * sin_c
            dk = dkr[:, :HD] * cos_c + dkr[:, HD:] * sin_c
            dq_out[span, cols] = (dq * swish_slope(query_raw)).astype(bf16)
            dk_out[span, cols] = (dk * swish_slope(kraw[span, cols].astype(f32))).astype(bf16)
            dv_out[span, cols] = dv.astype(bf16)


def mix_back(rates, across, qraw, kraw, v, do_in, cosine, sine, state_in, back_in):
    rows, width = qraw.shape
    heads = pl.BlockSpec((TILE // HD, HD, 2 * HD), lambda i: (i, 0, 0))
    return pl.pallas_call(
        mix_back_kernel,
        grid=(width // TILE,),
        in_specs=[
            smem(),
            smem(),
            columns(rows, TILE),
            columns(rows, TILE),
            columns(rows, TILE),
            columns(rows, TILE),
            fixed((rows, HD)),
            fixed((rows, HD)),
            heads,
            heads,
        ],
        out_specs=[columns(rows, TILE)] * 3,
        out_shape=[struct((rows, width), bf16)] * 3,
        scratch_shapes=[pltpu.VMEM((rows, 2 * HD), bf16), pltpu.VMEM((rows, 2 * HD), bf16)],
        compiler_params=params(),
        cost_estimate=cost(4 * rows * width * width, 16 * rows * width),
        name="mix_back",
    )(rates, across, qraw, kraw, v, do_in, cosine, sine, state_in, back_in)


def weight_grads_kernel(left_t, *refs):
    half = len(refs) // 2
    for incoming, out in zip(refs[:half], refs[half:]):
        out[...] = nn(left_t[...], incoming[...]).astype(bf16)


def weight_grads(left_t, *incoming):
    depth, rows = left_t.shape
    count = len(incoming)
    width = incoming[0].shape[1]
    return pl.pallas_call(
        weight_grads_kernel,
        grid=(width // TILE,),
        in_specs=[fixed((depth, rows))] + [columns(rows, TILE)] * count,
        out_specs=[columns(depth, TILE)] * count,
        out_shape=[struct((depth, width), bf16)] * count,
        compiler_params=params(),
        cost_estimate=cost(
            2 * count * rows * depth * width, 2 * count * (rows + depth) * width
        ),
        name="weight_grads",
    )(left_t, *incoming)


def input_back_kernel(x, dh1, dq, dk, dv, du, wq, wk, wv, wg, out, total):
    step = pl.program_id(0)
    part = nt(dq[...], wq[...]) + nt(dk[...], wk[...]) + nt(dv[...], wv[...]) + nt(du[...], wg[...])

    @pl.when(step == 0)
    def _():
        total[...] = part

    @pl.when(step > 0)
    def _():
        total[...] += part

    @pl.when(step == pl.num_programs(0) - 1)
    def _():
        hidden = x[...].astype(f32)
        scale = lax.rsqrt(jnp.mean(hidden * hidden, axis=1, keepdims=True) + epsilon)
        normed = hidden * scale
        incoming = total[...]
        out[...] = (
            dh1[...]
            + scale * (incoming - normed * jnp.mean(normed * incoming, axis=1, keepdims=True))
        ).astype(bf16)


def input_back(x, dh1, grads, weights):
    rows, depth = x.shape
    width = weights[0].shape[1]
    return pl.pallas_call(
        input_back_kernel,
        grid=(width // TILE,),
        in_specs=[fixed((rows, depth)), fixed((rows, depth))]
        + [columns(rows, TILE)] * 4
        + [columns(depth, TILE)] * 4,
        out_specs=fixed((rows, depth)),
        out_shape=struct((rows, depth), bf16),
        scratch_shapes=[pltpu.VMEM((rows, depth), f32)],
        compiler_params=params(),
        cost_estimate=cost(8 * rows * depth * width, 8 * rows * depth + 16 * width * depth),
        name="input_back",
    )(x, dh1, *grads, *weights)


def body(
    activations,
    w_query,
    w_key,
    w_value,
    w_gate,
    w_out,
    w_first,
    w_second,
    w_down,
    decay_rate,
    seq_lengths,
    out_grad,
):
    seq_count = lax.axis_size("seq")
    seq_index = lax.axis_index("seq")
    x = activations[0]
    og = out_grad[0]
    rows = x.shape[0]
    assert MIN_LEN % rows == 0

    def gathered(w):
        return lax.all_gather(w, "wt", axis=0, tiled=True)

    full_key, full_value = gathered(w_key), gathered(w_value)
    full_query, full_gate = gathered(w_query), gathered(w_gate)
    full_out, full_first = gathered(w_out), gathered(w_first)
    full_second, full_down = gathered(w_second), gathered(w_down)

    lengths = seq_lengths[0]
    starts = jnp.cumsum(lengths) - lengths
    begin = seq_index * rows
    begun = (starts <= begin) & (lengths > 0)
    first_token = jnp.max(jnp.where(begun, starts, 0))
    keep = jnp.where(begin == first_token, 0.0, 1.0).astype(f32)
    position = (begin - first_token + jnp.arange(rows, dtype=jnp.int32)).astype(f32)
    frequency = 10000.0 ** (-jnp.arange(HD, dtype=f32) / HD)
    angles = position[:, None] * frequency[None, :]
    cosine, sine = jnp.cos(angles), jnp.sin(angles)
    across = jnp.exp(-decay_rate * CH)
    whole = jnp.exp(-decay_rate * rows)[:, None, None]

    x_float = x.astype(f32)
    a = (
        x_float * lax.rsqrt(jnp.mean(x_float * x_float, axis=-1, keepdims=True) + epsilon)
    ).astype(bf16)
    a_t = a.T

    kraw, v, own_state = key_value(decay_rate, across, a, full_key, full_value, cosine, sine)
    ahead = [(i, i + 1) for i in range(seq_count - 1)]
    state_in = jnp.zeros_like(own_state)
    for _ in range(seq_count - 1):
        sent = (whole * state_in + own_state).astype(bf16)
        state_in = keep * lax.ppermute(sent, "seq", ahead).astype(f32)

    qraw, u, o, gated = mix(
        decay_rate, across, a, full_query, full_gate, kraw, v, cosine, sine, state_in
    )
    h1, bn, bn_t = residual(x, gated, full_out)
    g_first, g_second, g_down, layer_out, dh1, dattn = feed(
        h1, bn, bn_t, og, full_first, full_second, full_down
    )
    du, do, own_back = gate_back(
        decay_rate, across, dattn, full_out, o, u, qraw, cosine, sine
    )
    behind = [(i + 1, i) for i in range(seq_count - 1)]
    back_in = jnp.zeros_like(own_back)
    for _ in range(seq_count - 1):
        sent = (keep * (whole * back_in + own_back)).astype(bf16)
        back_in = lax.ppermute(sent, "seq", behind).astype(f32)
    (g_out,) = weight_grads(gated.T, dattn)
    dq, dk, dv = mix_back(
        decay_rate, across, qraw, kraw, v, do, cosine, sine, state_in, back_in
    )
    g_query, g_key, g_value, g_gate = weight_grads(a_t, dq, dk, dv, du)
    input_grad = input_back(
        x, dh1, (dq, dk, dv, du), (full_query, full_key, full_value, full_gate)
    )

    def owned(g):
        return lax.psum_scatter(g, "wt", scatter_dimension=0, tiled=True)

    shares = [
        owned(g)
        for g in (g_query, g_key, g_value, g_gate, g_out, g_first, g_second, g_down)
    ]
    totals = [lax.psum(share, "seq").astype(f32) for share in shares]
    return (layer_out[None], input_grad[None], *totals)


def solution(mesh):
    weight = P("wt", None)
    tokens = P("wt", "seq", None)
    return jax.shard_map(
        body,
        mesh=mesh,
        in_specs=(tokens,) + (weight,) * 8 + (P(), weight, tokens),
        out_specs=(tokens, tokens) + (weight,) * 8,
        check_vma=False,
    )
```

time: 1580 us -> 1130 us (0.72)
  matrix products: 318 us -> 0 us
  local copies, waits for them, and re-layouts: 294 us -> 10.8 us
  Pallas kernels: 0 us -> 167 us
  waiting for transfers between devices: 791 us -> 899 us
  other arithmetic: 121 us -> 25.9 us
  starting transfers between devices: 24.8 us -> 6.02 us
    dot_general x68 -> x0, matrix products: 318 us -> none  [the longest x8 65.2 us: matmul(): return jnp.dot(left, right, preferred_element_type=jnp.float32)]
    all_to_all x4 -> x0, waiting for transfers between devices: 192 us -> none  [the longest x1 86.1 us: body(): lax.all_to_all(outgoing, 'seq', split_axis=2, concat_axis=1, tiled=True)]
    all_gather x8, waiting for transfers between devices: 146 us -> 318 us  [gathered(): return lax.all_gather(w, 'wt', axis=0, tiled=True)]
    pallas_call x0 -> x9, Pallas kernels: none -> 167 us  [the longest x1 67.1 us: feed(): pl.pallas_call(feed_kernel, grid=(hidden // TILE,), in_specs=[fixed((rows...]
    reduce_scatter x8, waiting for transfers between devices: 404 us -> 509 us  [owned(): return lax.psum_scatter(g, 'wt', scatter_dimension=0, tiled=True)]
    another operation x9 -> x0, local copies, waits for them, and re-layouts: 54.9 us -> none  [the longest x3 20.6 us: body(): jnp.stack([grad_query_h, grad_key_h, grad_vheads.reshape(head_shape), gra...]
    convert_element_type x10 -> x1, local copies, waits for them, and re-layouts: 51.5 us -> 3.94 us  [body(): a = (x_float * lax.rsqrt(jnp.mean(x_float * x_float, axis=-1, keepdims=Tr...]
    dynamic_slice x32 -> x0, local copies, waits for them, and re-layouts: 40.6 us -> none  [body(): lax.scan(forward_block, zero_state, (blocked(query_rot), blocked(key_rot)...]
  transfers between devices with their start and end apart: 21 -> 19, of which waited for: 14 -> 18; matrix products, arithmetic and copies ran while one was open for 27% -> 2% of each run, Pallas kernels for 0% -> 8%
where the time goes in v1:
time: 1130 us; the launch traced here: 1120 us
  waiting for transfers between devices  899 us (80%)
  Pallas kernels  167 us (15%)
  other arithmetic  25.9 us (2%)
  between operations  15.4 us (1%)
    reduce_scatter x8, waiting for transfers between devices, owned(): return lax.psum_scatter(g, 'wt', scatter_dimension=0, tiled=True)  509 us
    all_gather x8, waiting for transfers between devices, gathered(): return lax.all_gather(w, 'wt', axis=0, tiled=True)  318 us
    pallas_call x1, Pallas kernels, feed(): pl.pallas_call(feed_kernel, grid=(hidden // TILE,), in_specs=[fixed((rows...  67.1 us
    psum x1, waiting for transfers between devices, body(): totals = [lax.psum(share, 'seq').astype(f32) for share in shares]  40.1 us
  transfers between devices with their start and end apart: 19, of which 18 were waited for; matrix products, arithmetic and copies ran while one was open for 2% of the time, Pallas kernels for 8%

profile of v1, /device:TPU:12, one launch (start us, length us, event | category | flops | bytes accessed | tf_op | source)
XLA Modules:
  0.0 1124.3 jit_solution(9117914653992705569)
XLA Ops:
  28.2 22.6 %all-gather.13.cloned.1.call-done.wk = bf16[1024,1024]{1,0:T(8,128)(2,1)} async-done(((bf16[64,1024]{1,0:T(8,128)(2,1)}), bf16[1024,1024]{1,0:T(8,128)(2,1)}) %all-gather.13.cloned.1.call-update) | async-done | bytes 2097168 | tf_op jit(solution)/shard_map/all_gather | solution.py:548
  50.8 42.4 %all-gather.15.cloned.1.call-done.wv = bf16[1024,1024]{1,0:T(8,128)(2,1)} async-done(((bf16[64,1024]{1,0:T(8,128)(2,1)}), bf16[1024,1024]{1,0:T(8,128)(2,1)}) %all-gather.15.cloned.1.call-update) | async-done | bytes 2097168 | tf_op jit(solution)/shard_map/all_gather | solution.py:548
  108.6 10.7 collective-permute-done
  120.4 15.2 %all-gather.9.cloned.1.call-done.wq = bf16[1024,1024]{1,0:T(8,128)(2,1)} async-done(((bf16[64,1024]{1,0:T(8,128)(2,1)}), bf16[1024,1024]{1,0:T(8,128)(2,1)}) %all-gather.9.cloned.1.call-update) | async-done | bytes 2097168 | tf_op jit(solution)/shard_map/all_gather | solution.py:548
  135.6 42.2 %all-gather.11.cloned.1.call-done.wg = bf16[1024,1024]{1,0:T(8,128)(2,1)} async-done(((bf16[64,1024]{1,0:T(8,128)(2,1)}), bf16[1024,1024]{1,0:T(8,128)(2,1)}) %all-gather.11.cloned.1.call-update) | async-done | bytes 2097168 | tf_op jit(solution)/shard_map/all_gather | solution.py:548
  177.8 16.3 %mix.1 = (bf16[1024,1024]{1,0:T(8,128)(2,1)}, bf16[1024,1024]{1,0:T(8,128)(2,1)}, bf16[1024,1024]{1,0:T(8,128)(2,1)}, bf16[1024,1024]{1,0:T(8,128)(2,1)}) custom-call(f32[8]{0:T(128)} %rates.7, f32[8]{0:T(128)} %get-tuple-element.73.across, bf16[1024,1024]{1,0:T(8,128)(2,1)} %copy.24.a, bf16[1024,1024]{1,0:T(8,128)(2,1)} %all-gather.9.cloned.1.call-done.wq, ...), custom_call_target="tpu_custom_call" | custom-call | flops 8589934592 | bytes 18874368 | tf_op jit(solution)/shard_map/mix/pallas_call | solution.py:180
  198.0 22.0 %all-gather.17.cloned.1.call-done.wo = bf16[1024,1024]{1,0:T(8,128)(2,1)} async-done(((bf16[64,1024]{1,0:T(8,128)(2,1)}), bf16[1024,1024]{1,0:T(8,128)(2,1)}) %all-gather.17.cloned.1.call-update) | async-done | bytes 2097168 | tf_op jit(solution)/shard_map/all_gather | solution.py:548
  227.3 53.6 %all-gather.19.cloned.1.call-done.w1 = bf16[1024,2816]{1,0:T(8,128)(2,1)} async-done(((bf16[64,2816]{1,0:T(8,128)(2,1)}), bf16[1024,2816]{1,0:T(8,128)(2,1)}) %all-gather.19.cloned.1.call-update) | async-done | bytes 5767184 | tf_op jit(solution)/shard_map/all_gather | solution.py:548
  281.0 60.0 %all-gather.21.cloned.1.call-done.w2 = bf16[1024,2816]{1,0:T(8,128)(2,1)} async-done(((bf16[64,2816]{1,0:T(8,128)(2,1)}), bf16[1024,2816]{1,0:T(8,128)(2,1)}) %all-gather.21.cloned.1.call-update) | async-done | bytes 5767184 | tf_op jit(solution)/shard_map/all_gather | solution.py:548
  340.9 60.0 %all-gather.23.cloned.1.call-done.wd = bf16[2816,1024]{1,0:T(8,128)(2,1)} async-done(((bf16[176,1024]{1,0:T(8,128)(2,1)}), bf16[2816,1024]{1,0:T(8,128)(2,1)}) %all-gather.23.cloned.1.call-update) | async-done | bytes 5767184 | tf_op jit(solution)/shard_map/all_gather | solution.py:548
  400.9 67.1 %feed.1 = (bf16[1024,2816]{1,0:T(8,128)(2,1)}, bf16[1024,2816]{1,0:T(8,128)(2,1)}, bf16[2816,1024]{1,0:T(8,128)(2,1)}, bf16[1024,1024]{1,0:T(8,128)(2,1)}, f32[1...) custom-call(f32[1024,1024]{1,0:T(8,128)} %get-tuple-element.40.h1, bf16[1024,1024]{1,0:T(8,128)(2,1)} %get-tuple-element.41.bn, ...), custom_call_target="tpu_custom_call" | custom-call | flops 53150220288 | bytes 55574528 | tf_op jit(solution)/shard_map/feed/pallas_call | solution.py:270
  474.3 10.9 gate_back.1
  489.9 12.8 %collective-permute-done.1 = bf16[8,128,256]{2,1,0:T(8,128)(2,1)S(1)} collective-permute-done((bf16[8,128,256]{2,1,0:T(8,128)(2,1)S(1)}, bf16[8,128,256]{2,1,0:T(8,128)(2,1)S(1)}, u32[]{:S(2)}, u32[]{:S(2)}) %collective-permute-start.1) | collective-permute-done | bytes 524320 | tf_op jit(solution)/shard_map/ppermute | solution.py:595
  503.8 18.1 %mix_back.1 = (bf16[1024,1024]{1,0:T(8,128)(2,1)}, bf16[1024,1024]{1,0:T(8,128)(2,1)}, bf16[1024,1024]{1,0:T(8,128)(2,1)}) custom-call(f32[8]{0:T(128)} %rates.7, f32[8]{0:T(128)} %get-tuple-element.73.across, bf16[1024,1024]{1,0:T(8,128)(2,1)} %get-tuple-element.45.qraw, bf16[1024,1024]{1,0:T(8,128)(2,1)} %get-tuple-element.36.kraw, ...), custom_call_target="tpu_custom_call" | custom-call | flops 4294967296 | bytes 16777216 | tf_op jit(solution)/shard_map/mix_back/pallas_call | solution.py:436
  521.9 13.3 %weight_grads.2 = (bf16[1024,1024]{1,0:T(8,128)(2,1)}, bf16[1024,1024]{1,0:T(8,128)(2,1)}, bf16[1024,1024]{1,0:T(8,128)(2,1)}, bf16[1024,1024]{1,0:T(8,128)(2,1)}) custom-call(bf16[1024,1024]{1,0:T(8,128)(2,1)} %fusion.3.left_t, bf16[1024,1024]{1,0:T(8,128)(2,1)} %get-tuple-element.51.dq.refs_0_, bf16[1024,1024]{1,0:T(8,128)(2,1)} %get-tuple-element.52.dk.refs_1_, ...), custom_call_target="tpu_custom_call" | custom-call | flops 8589934592 | bytes 16777216 | tf_op jit(solution)/shard_map/weight_grads/pallas_call | solution.py:470
  539.3 61.1 %reduce-scatter.9.cloned.1.call-done = bf16[64,1024]{1,0:T(8,128)(2,1)} async-done(((bf16[1024,1024]{1,0:T(8,128)(2,1)}), bf16[64,1024]{1,0:T(8,128)(2,1)}) %reduce-scatter.9.cloned.1.call-update) | async-done | bytes 131088 | tf_op jit(solution)/shard_map/reduce_scatter | solution.py:606
  600.4 64.3 %reduce-scatter.11.cloned.1.call-done = bf16[64,1024]{1,0:T(8,128)(2,1)} async-done(((bf16[1024,1024]{1,0:T(8,128)(2,1)}), bf16[64,1024]{1,0:T(8,128)(2,1)}) %reduce-scatter.11.cloned.1.call-update) | async-done | bytes 131088 | tf_op jit(solution)/shard_map/reduce_scatter | solution.py:606
  664.6 64.7 %reduce-scatter.13.cloned.1.call-done = bf16[64,1024]{1,0:T(8,128)(2,1)} async-done(((bf16[1024,1024]{1,0:T(8,128)(2,1)}), bf16[64,1024]{1,0:T(8,128)(2,1)}) %reduce-scatter.13.cloned.1.call-update) | async-done | bytes 131088 | tf_op jit(solution)/shard_map/reduce_scatter | solution.py:606
  729.3 64.2 %reduce-scatter.15.cloned.1.call-done = bf16[64,1024]{1,0:T(8,128)(2,1)} async-done(((bf16[1024,1024]{1,0:T(8,128)(2,1)}), bf16[64,1024]{1,0:T(8,128)(2,1)}) %reduce-scatter.15.cloned.1.call-update) | async-done | bytes 131088 | tf_op jit(solution)/shard_map/reduce_scatter | solution.py:606
  793.6 84.4 %reduce-scatter.19.cloned.1.call-done = bf16[64,2816]{1,0:T(8,128)(2,1)} async-done(((bf16[1024,2816]{1,0:T(8,128)(2,1)}), bf16[64,2816]{1,0:T(8,128)(2,1)}) %reduce-scatter.19.cloned.1.call-update) | async-done | bytes 360464 | tf_op jit(solution)/shard_map/reduce_scatter | solution.py:606
  878.0 85.0 %reduce-scatter.21.cloned.1.call-done = bf16[64,2816]{1,0:T(8,128)(2,1)} async-done(((bf16[1024,2816]{1,0:T(8,128)(2,1)}), bf16[64,2816]{1,0:T(8,128)(2,1)}) %reduce-scatter.21.cloned.1.call-update) | async-done | bytes 360464 | tf_op jit(solution)/shard_map/reduce_scatter | solution.py:606
  963.0 85.0 %reduce-scatter.23.cloned.1.call-done = bf16[176,1024]{1,0:T(8,128)(2,1)} async-done(((bf16[2816,1024]{1,0:T(8,128)(2,1)}), bf16[176,1024]{1,0:T(8,128)(2,1)}) %reduce-scatter.23.cloned.1.call-update) | async-done | bytes 360464 | tf_op jit(solution)/shard_map/reduce_scatter | solution.py:606
  1048.0 18.7 %input_back.1 = bf16[1024,1024]{1,0:T(8,128)(2,1)} custom-call(bf16[1024,1024]{1,0:T(8,128)(2,1)} %bitcast.22, f32[1024,1024]{1,0:T(8,128)} %get-tuple-element.44.dh1, bf16[1024,1024]{1,0:T(8,128)(2,1)} %get-tuple-element.51.dq.refs_0_, bf16[1024,1024]{1,0:T(8,128)(2,1)} %get-tuple-element.52.dk.refs_1_, bf16[1024,1024]{1,0:T(8,128)(2,1)} %get-tuple-element.53.dv.refs_2_, ...), custom_call_target="tpu_custom_call" | custom-call | flops 8589934592 | bytes 25165824 | tf_op jit(solution)/shard_map/input_back/pallas_call | solution.py:511
  1066.7 40.1 %all-reduce.3.cloned.1.call-done = (bf16[64,1024]{1,0:T(8,128)(2,1)}, bf16[64,1024]{1,0:T(8,128)(2,1)}, bf16[64,1024]{1,0:T(8,128)(2,1)}, bf16[64,1024]{1,0:T(8,...) async-done(((bf16[64,1024]{1,0:T(8,128)(2,1)}, bf16[64,1024]{1,0:T(8,128)(2,1)}, ...) | async-done | bytes 1736720 | tf_op jit(solution)/shard_map/psum | solution.py:612
  (73 shorter events, 74.4 us)
Async XLA Ops:
  7.2 43.7 %all-gather.13.cloned.1.call-start = ((), (), s32[]{:S(2)}) async-start(), calls=%async_computation.10 | async-start | bytes 2228224 | tf_op jit(solution)/shard_map/all_gather | solution.py:548
  7.9 85.3 %all-gather.15.cloned.1.call-start = ((), (), s32[]{:S(2)}) async-start(), calls=%async_computation.11 | async-start | bytes 2228224 | tf_op jit(solution)/shard_map/all_gather | solution.py:548
  8.7 126.9 %all-gather.9.cloned.1.call-start = ((), (), s32[]{:S(2)}) async-start(), calls=%async_computation.8 | async-start | bytes 2228224 | tf_op jit(solution)/shard_map/all_gather | solution.py:548
  9.4 168.4 %all-gather.11.cloned.1.call-start = ((), (), s32[]{:S(2)}) async-start(), calls=%async_computation.9 | async-start | bytes 2228224 | tf_op jit(solution)/shard_map/all_gather | solution.py:548
  10.0 210.0 %all-gather.17.cloned.1.call-start = ((), (), s32[]{:S(2)}) async-start(), calls=%async_computation.12 | async-start | bytes 2228224 | tf_op jit(solution)/shard_map/all_gather | solution.py:548
  10.6 270.4 %all-gather.19.cloned.1.call-start = ((), (), s32[]{:S(2)}) async-start(), calls=%async_computation.13 | async-start | bytes 6127616 | tf_op jit(solution)/shard_map/all_gather | solution.py:548
  11.1 329.8 %all-gather.21.cloned.1.call-start = ((), (), s32[]{:S(2)}) async-start(), calls=%async_computation.14 | async-start | bytes 6127616 | tf_op jit(solution)/shard_map/all_gather | solution.py:548
  11.9 389.0 %all-gather.23.cloned.1.call-start = ((), (), s32[]{:S(2)}) async-start(), calls=%async_computation.15 | async-start | bytes 6127616 | tf_op jit(solution)/shard_map/all_gather | solution.py:548
  12.6 526.6 %reduce-scatter.17.cloned.1.call-start = ((), (), s32[]{:S(2)}) async-start(), calls=%async_computation.20 | async-start | bytes 2228224 | tf_op jit(solution)/shard_map/reduce_scatter | solution.py:606
  20.7 4.0 copy-start.3
  104.3 15.0 %collective-permute-start = (bf16[8,128,256]{2,1,0:T(8,128)(2,1)S(1)}, bf16[8,128,256]{2,1,0:T(8,128)(2,1)S(1)}, u32[]{:S(2)}, u32[]{:S(2)}) collective-permute-start(bf16[8,128,256]{2,1,0:T(8,128)(2,1)S(1)} %add_convert_fusion), channel_id=1, source_target_pairs={{0,16},{1,17},{2,18},{3,19},{4,20},{5,21},{6,22},{7,23},{8,24},{9,... | collective-permute-start | bytes 1572872 | tf_op jit(solution)/shard_map/ppermute | solution.py:579
  474.1 126.3 %reduce-scatter.9.cloned.1.call-start = ((), (), s32[]{:S(2)}) async-start(), calls=%async_computation.16 | async-start | bytes 2228224 | tf_op jit(solution)/shard_map/reduce_scatter | solution.py:606
  486.7 16.0 %collective-permute-start.1 = (bf16[8,128,256]{2,1,0:T(8,128)(2,1)S(1)}, bf16[8,128,256]{2,1,0:T(8,128)(2,1)S(1)}, u32[]{:S(2)}, u32[]{:S(2)}) collective-permute-start(bf16[8,128,256]{2,1,0:T(8,128)(2,1)S(1)} %multiply_convert_fusion), channel_id=1, source_target_pairs={{16,0},{17,1},{18,2},{19,3},{20,4},{21,5},{22,6},{23,7},{24,8},{25... | collective-permute-start | bytes 1572872 | tf_op jit(solution)/shard_map/ppermute | solution.py:595
  535.1 129.5 %reduce-scatter.11.cloned.1.call-start = ((), (), s32[]{:S(2)}) async-start(), calls=%async_computation.17 | async-start | bytes 2228224 | tf_op jit(solution)/shard_map/reduce_scatter | solution.py:606
  535.9 193.5 %reduce-scatter.13.cloned.1.call-start = ((), (), s32[]{:S(2)}) async-start(), calls=%async_computation.18 | async-start | bytes 2228224 | tf_op jit(solution)/shard_map/reduce_scatter | solution.py:606
  536.5 257.1 %reduce-scatter.15.cloned.1.call-start = ((), (), s32[]{:S(2)}) async-start(), calls=%async_computation.19 | async-start | bytes 2228224 | tf_op jit(solution)/shard_map/reduce_scatter | solution.py:606
  537.2 340.8 %reduce-scatter.19.cloned.1.call-start = ((), (), s32[]{:S(2)}) async-start(), calls=%async_computation.21 | async-start | bytes 6127616 | tf_op jit(solution)/shard_map/reduce_scatter | solution.py:606
  537.8 425.2 %reduce-scatter.21.cloned.1.call-start = ((), (), s32[]{:S(2)}) async-start(), calls=%async_computation.22 | async-start | bytes 6127616 | tf_op jit(solution)/shard_map/reduce_scatter | solution.py:606
  538.4 509.6 %reduce-scatter.23.cloned.1.call-start = ((), (), s32[]{:S(2)}) async-start(), calls=%async_computation.23 | async-start | bytes 6127616 | tf_op jit(solution)/shard_map/reduce_scatter | solution.py:606
  538.9 567.9 %all-reduce.3.cloned.1.call-start = ((), (), s32[]{:S(2)}) async-start(), calls=%async_computation.24 | async-start | bytes 3473408 | tf_op jit(solution)/shard_map/psum | solution.py:612
  1106.8 8.2 copy-start.2
  1106.8 9.1 copy-start.1
  1106.8 10.0 copy-start
Sparse Core Ops, SparseCore 0:
  10.2 40.6 all-gather.12
  53.0 40.1 all-gather.14
  95.4 40.1 all-gather.8
  137.6 40.1 all-gather.10
  179.8 40.1 all-gather.16
  222.1 58.7 all-gather.18
  283.3 57.6 all-gather.20
  343.2 57.6 all-gather.22
  474.2 60.9 reduce-scatter.16
  539.8 60.5 reduce-scatter.8
  604.1 60.4 reduce-scatter.10
  668.7 60.5 reduce-scatter.12
  733.1 60.4 reduce-scatter.14
  797.8 80.1 reduce-scatter.18
  882.3 80.7 reduce-scatter.20
  967.3 80.7 reduce-scatter.22
  1050.8 56.0 all-reduce.2

commit v2 on v1

v2 whole, which is shorter than its diff:
```python
import jax
import jax.numpy as jnp
from jax import lax
from jax.experimental import pallas as pl
from jax.experimental.pallas import tpu as pltpu
from jax.sharding import PartitionSpec as P

H = 8
HD = 128
CH = 256
TILE = 256
HALF = 128
SHARDS = 16
MIN_LEN = 1024
VMEM_LIMIT = 60 << 20

epsilon = 1e-06
head_floor = 1.0
bf16 = jnp.bfloat16
f32 = jnp.float32


def nn(left, right):
    return jnp.dot(left, right, preferred_element_type=f32)


def nt(left, right):
    return lax.dot_general(left, right, (((1,), (1,)), ((), ())), preferred_element_type=f32)


def tn(left, right):
    return lax.dot_general(left, right, (((0,), (0,)), ((), ())), preferred_element_type=f32)


def struct(shape, dtype):
    return jax.ShapeDtypeStruct(shape, dtype)


def fixed(shape):
    zeros = (0,) * len(shape)
    return pl.BlockSpec(shape, lambda i: zeros, pipeline_mode=pl.Buffered(1))


def columns(rows, width):
    return pl.BlockSpec((rows, width), lambda i: (0, i))


def row_tiles(height, cols):
    return pl.BlockSpec((height, cols), lambda i: (i, 0))


def smem():
    return pl.BlockSpec(memory_space=pltpu.SMEM)


def params():
    return pltpu.CompilerParams(vmem_limit_bytes=VMEM_LIMIT)


def cost(flops, moved):
    return pl.CostEstimate(flops=flops, bytes_accessed=moved, transcendentals=0)


class Gathered:
    def __init__(self, first, second, order):
        self.first, self.second, self.order = first, second, order

    def specs(self, height, index, chips=8):
        def of(core):
            if chips == 8:
                return pl.BlockSpec((8, 1, height, TILE), lambda i: (0, core, index(i), 0))
            return pl.BlockSpec((chips, 1, height, TILE), lambda i: (i, core, index(i), 0))

        return [of(0), of(self.first.shape[1] - 1)]

    def arrays(self):
        return [self.first, self.second]


def join(order, first, second, held, rows=slice(None)):
    held[:, order, rows, :] = first[:, 0]
    held[:, 1 - order, rows, :] = second[:, 0]


def emit(coords, stage, own, other, rows, order):
    z0, y0, c0, x0 = coords[0], coords[1], coords[2], coords[3]
    for x in range(2):
        x_rel = x + x0 - 2 * x * x0
        cols = slice(x * HALF, (x + 1) * HALF)
        for y_rel in range(2):
            y = y_rel + y0 - 2 * y_rel * y0
            for z_rel in range(4):
                z = lax.rem(z0 + z_rel, 4)
                shard = z * 4 + y * 2
                lead = (x_rel, y_rel) if order == "xy" else (y_rel, x_rel)
                own[(*lead, z_rel, rows)] = stage[shard + c0, :, cols]
                other[(*lead, z_rel, rows)] = stage[shard + 1 - c0, :, cols]


def decay_in_of(rate):
    row = lax.broadcasted_iota(jnp.int32, (CH, HD), 0).astype(f32)
    return jnp.exp(-rate * (row + 1.0))


def decay_out_of(rate):
    row = lax.broadcasted_iota(jnp.int32, (CH, HD), 0).astype(f32)
    return jnp.exp(-rate * (CH - 1.0 - row))


def double(table):
    return jnp.concatenate([table, table], axis=1)


def rotated(heads, cosine, sine):
    return jnp.concatenate([heads * cosine, heads * sine], axis=1)


def swish(raw):
    return raw * jax.nn.sigmoid(raw)


def swish_slope(raw):
    sig = jax.nn.sigmoid(raw)
    return sig * (1.0 + raw * (1.0 - sig))


def head_columns(s):
    return slice(s * HD, (s + 1) * HD)


def head_states():
    return pl.BlockSpec((TILE // HD, HD, 2 * HD), lambda i: (i, 0, 0))


def prepare_kernel(x, a_out, at_out):
    value = x[...].astype(f32)
    low = (value * lax.rsqrt(jnp.mean(value * value, axis=1, keepdims=True) + epsilon)).astype(bf16)
    a_out[...] = low
    at_out[...] = low.T


def prepare(x):
    rows, depth = x.shape
    part = 512
    return pl.pallas_call(
        prepare_kernel,
        grid=(rows // part,),
        in_specs=[row_tiles(part, depth)],
        out_specs=[row_tiles(part, depth), columns(depth, part)],
        out_shape=[struct((rows, depth), bf16), struct((depth, rows), bf16)],
        compiler_params=params(),
        cost_estimate=cost(8 * rows * depth, 6 * rows * depth),
        name="prepare",
    )(x)


def key_value_kernel(
    rates, across, order, a, wk0, wk1, wv0, wv1, cosine, sine, kraw_out, v_out, state_out, held
):
    step = pl.program_id(0)
    rows = a.shape[0]
    join(order[0], wk0, wk1, held.at[0])
    join(order[0], wv0, wv1, held.at[1])
    kraw = nn(a[...], held[0].reshape(-1, TILE))
    v_out[...] = nn(a[...], held[1].reshape(-1, TILE)).astype(bf16)
    kraw_out[...] = kraw.astype(bf16)
    for s in range(TILE // HD):
        head = step * (TILE // HD) + s
        cols = head_columns(s)
        tail = double(decay_out_of(rates[head]))
        state = jnp.zeros((HD, 2 * HD), f32)
        for c in range(rows // CH):
            span = slice(c * CH, (c + 1) * CH)
            key = swish(kraw[span, cols])
            faded = rotated(key, cosine[span, :], sine[span, :]) * tail
            state = across[head] * state + tn(v_out[span, cols], faded.astype(bf16))
        state_out[s] = state


def key_value(rates, across, a, keys, values, cosine, sine):
    rows, depth = a.shape
    return pl.pallas_call(
        key_value_kernel,
        grid=(depth // TILE,),
        in_specs=[smem(), smem(), smem(), fixed((rows, depth))]
        + keys.specs(64, lambda i: i)
        + values.specs(64, lambda i: i)
        + [fixed((rows, HD)), fixed((rows, HD))],
        out_specs=[columns(rows, TILE), columns(rows, TILE), head_states()],
        out_shape=[
            struct((rows, depth), bf16),
            struct((rows, depth), bf16),
            struct((H, HD, 2 * HD), f32),
        ],
        scratch_shapes=[pltpu.VMEM((2, 8, 2, 64, TILE), bf16)],
        compiler_params=params(),
        cost_estimate=cost(5 * rows * depth * depth, 10 * rows * depth),
        name="key_value",
    )(rates, across, keys.order, a, *keys.arrays(), *values.arrays(), cosine, sine)


def mix_kernel(
    rates,
    across,
    order,
    a,
    wq0,
    wq1,
    wg0,
    wg1,
    kraw,
    v,
    cosine,
    sine,
    state_in,
    qraw_out,
    u_out,
    o_out,
    gated_out,
    held,
):
    step = pl.program_id(0)
    rows = a.shape[0]
    join(order[0], wq0, wq1, held.at[0])
    join(order[0], wg0, wg1, held.at[1])
    qraw = nn(a[...], held[0].reshape(-1, TILE))
    qraw_out[...] = qraw.astype(bf16)
    u_out[...] = nn(a[...], held[1].reshape(-1, TILE)).astype(bf16)
    row = lax.broadcasted_iota(jnp.int32, (CH, CH), 0)
    col = lax.broadcasted_iota(jnp.int32, (CH, CH), 1)
    distance = (row - col).astype(f32)
    for s in range(TILE // HD):
        head = step * (TILE // HD) + s
        cols = head_columns(s)
        rate = rates[head]
        tail = double(decay_out_of(rate))
        lead = decay_in_of(rate)
        mask = jnp.where(distance >= 0, jnp.exp(-rate * jnp.maximum(distance, 0.0)), 0.0)
        state = state_in[s]
        for c in range(rows // CH):
            span = slice(c * CH, (c + 1) * CH)
            cos_c, sin_c = cosine[span, :], sine[span, :]
            query = rotated(swish(qraw[span, cols]), cos_c, sin_c).astype(bf16)
            key_float = rotated(swish(kraw[span, cols].astype(f32)), cos_c, sin_c)
            key = key_float.astype(bf16)
            value = v[span, cols]
            weights = (nt(query, key) * mask).astype(bf16)
            o = nn(weights, value) + lead * nt(query, state.astype(bf16))
            state = across[head] * state + tn(value, (key_float * tail).astype(bf16))
            o_out[span, cols] = o.astype(bf16)
            scale = lax.rsqrt(jnp.mean(o * o, axis=1, keepdims=True) + head_floor)
            gated_out[span, cols] = (o * scale * u_out[span, cols].astype(f32)).astype(bf16)


def mix(rates, across, a, queries, gates, kraw, v, cosine, sine, state_in):
    rows, depth = a.shape
    return pl.pallas_call(
        mix_kernel,
        grid=(depth // TILE,),
        in_specs=[smem(), smem(), smem(), fixed((rows, depth))]
        + queries.specs(64, lambda i: i)
        + gates.specs(64, lambda i: i)
        + [
            columns(rows, TILE),
            columns(rows, TILE),
            fixed((rows, HD)),
            fixed((rows, HD)),
            head_states(),
        ],
        out_specs=[columns(rows, TILE)] * 4,
        out_shape=[struct((rows, depth), bf16)] * 4,
        scratch_shapes=[pltpu.VMEM((2, 8, 2, 64, TILE), bf16)],
        compiler_params=params(),
        cost_estimate=cost(8 * rows * depth * depth, 18 * rows * depth),
        name="mix",
    )(
        rates,
        across,
        queries.order,
        a,
        *queries.arrays(),
        *gates.arrays(),
        kraw,
        v,
        cosine,
        sine,
        state_in,
    )


def residual_kernel(order, x, gated, lo0, lo1, hi0, hi1, h1_out, bn_out, bnt_out, held, h1):
    join(order[0], lo0, lo1, held, slice(0, 128))
    join(order[0], hi0, hi1, held, slice(128, 256))
    for b in range(4):
        cols = slice(b * TILE, (b + 1) * TILE)
        weight = held[:, :, b * 64 : (b + 1) * 64, :].reshape(-1, TILE)
        h1[:, cols] = x[:, cols].astype(f32) + nn(gated[...], weight)
    value = h1[...]
    h1_out[...] = value
    normed = value * lax.rsqrt(jnp.mean(value * value, axis=1, keepdims=True) + epsilon)
    low = normed.astype(bf16)
    bn_out[...] = low
    bnt_out[...] = low.T


def residual(x, gated, out_lo, out_hi):
    rows, depth = x.shape
    part = 512
    return pl.pallas_call(
        residual_kernel,
        grid=(rows // part,),
        in_specs=[smem(), row_tiles(part, depth), row_tiles(part, depth)]
        + out_lo.specs(128, lambda i: 2)
        + out_hi.specs(128, lambda i: 2),
        out_specs=[row_tiles(part, depth), row_tiles(part, depth), columns(depth, part)],
        out_shape=[
            struct((rows, depth), f32),
            struct((rows, depth), bf16),
            struct((depth, rows), bf16),
        ],
        scratch_shapes=[
            pltpu.VMEM((8, 2, 256, TILE), bf16),
            pltpu.VMEM((part, depth), f32),
        ],
        compiler_params=params(),
        cost_estimate=cost(2 * rows * depth * depth, 14 * rows * depth),
        name="residual",
    )(out_lo.order, x, gated, *out_lo.arrays(), *out_hi.arrays())


def feed_tile(bn, bnt, og, held, down, stage, total, dbn):
    w1 = held[:, :, 0:64, :].reshape(-1, TILE)
    w2 = held[:, :, 64:128, :].reshape(-1, TILE)
    for b in range(4):
        rows = slice(128 + 16 * b, 144 + 16 * b)
        down[:, b * TILE : (b + 1) * TILE] = held[:, :, rows, :].reshape(TILE, TILE)
    first = nn(bn[...], w1)
    second = nn(bn[...], w2)
    middle = (first * second).astype(bf16)
    dmid = nt(og[...], down[...])
    total[...] += nn(middle, down[...])
    d_first = (dmid * second).astype(bf16)
    d_second = (dmid * first).astype(bf16)
    dbn[...] += nt(d_first, w1) + nt(d_second, w2)
    stage[:, 0:64, :] = nn(bnt[...], d_first).astype(bf16).reshape(SHARDS, 64, TILE)
    stage[:, 64:128, :] = nn(bnt[...], d_second).astype(bf16).reshape(SHARDS, 64, TILE)
    g_down = tn(middle, og[...]).astype(bf16)
    for b in range(4):
        rows = slice(128 + 16 * b, 144 + 16 * b)
        stage[:, rows, :] = g_down[:, b * TILE : (b + 1) * TILE].reshape(SHARDS, 16, TILE)


def feed_start_kernel(bn, bnt, og, w, g_out, y_out, dbn_out, down, total, dbn):
    step = pl.program_id(0)

    @pl.when(step == 0)
    def _():
        total[...] = jnp.zeros_like(total)
        dbn[...] = jnp.zeros_like(dbn)

    feed_tile(bn, bnt, og, w, down, g_out, total, dbn)

    @pl.when(step == pl.num_programs(0) - 1)
    def _():
        y_out[...] = total[...].astype(bf16)
        dbn_out[...] = dbn[...].astype(bf16)


def feed_start(bn, bnt, og, weights, base, tiles):
    rows, depth = bn.shape
    return pl.pallas_call(
        feed_start_kernel,
        grid=(tiles,),
        in_specs=[
            fixed((rows, depth)),
            fixed((depth, rows)),
            fixed((rows, depth)),
            pl.BlockSpec((8, 2, 192, TILE), lambda i: (0, 0, base + i, 0)),
        ],
        out_specs=[
            pl.BlockSpec((SHARDS, 192, TILE), lambda i: (0, i, 0)),
            fixed((rows, depth)),
            fixed((rows, depth)),
        ],
        out_shape=[
            struct((SHARDS, tiles * 192, TILE), bf16),
            struct((rows, depth), bf16),
            struct((rows, depth), bf16),
        ],
        scratch_shapes=[
            pltpu.VMEM((TILE, depth), bf16),
            pltpu.VMEM((rows, depth), f32),
            pltpu.VMEM((rows, depth), f32),
        ],
        compiler_params=params(),
        cost_estimate=cost(
            18 * rows * depth * tiles * TILE, 12 * depth * tiles * TILE + 10 * rows * depth
        ),
        name="feed_start",
    )(bn, bnt, og, weights)


def feed_end_kernel(
    coords,
    h1,
    bn,
    bnt,
    og,
    y_part,
    dbn_part,
    w,
    own_out,
    other_out,
    y_out,
    dh1_out,
    dattn_out,
    down,
    stage,
    total,
    dbn,
):
    step = pl.program_id(0)

    @pl.when(step == 0)
    def _():
        total[...] = h1[...] + y_part[...].astype(f32)
        dbn[...] = dbn_part[...].astype(f32)

    feed_tile(bn, bnt, og, w, down, stage, total, dbn)
    emit(coords, stage, own_out, other_out, slice(0, 192), "xy")

    @pl.when(step == pl.num_programs(0) - 1)
    def _():
        y_out[...] = total[...].astype(bf16)
        hidden = h1[...]
        scale = lax.rsqrt(jnp.mean(hidden * hidden, axis=1, keepdims=True) + epsilon)
        normed = hidden * scale
        incoming = dbn[...]
        dh1 = og[...].astype(f32) + scale * (
            incoming - normed * jnp.mean(normed * incoming, axis=1, keepdims=True)
        )
        dh1_out[...] = dh1
        dattn_out[...] = dh1.astype(bf16)


def grad_block(height):
    return pl.BlockSpec((2, 2, 4, height, HALF), lambda i: (0, 0, 0, i, 0))


def feed_end(coords, h1, bn, bnt, og, y_part, dbn_part, weights, base, tiles):
    rows, depth = bn.shape
    grads = struct((2, 2, 4, tiles * 192, HALF), bf16)
    return pl.pallas_call(
        feed_end_kernel,
        grid=(tiles,),
        in_specs=[
            smem(),
            fixed((rows, depth)),
            fixed((rows, depth)),
            fixed((depth, rows)),
            fixed((rows, depth)),
            fixed((rows, depth)),
            fixed((rows, depth)),
            pl.BlockSpec((8, 2, 192, TILE), lambda i: (0, 0, base + i, 0)),
        ],
        out_specs=[
            grad_block(192),
            grad_block(192),
            fixed((rows, depth)),
            fixed((rows, depth)),
            fixed((rows, depth)),
        ],
        out_shape=[
            grads,
            grads,
            struct((rows, depth), bf16),
            struct((rows, depth), f32),
            struct((rows, depth), bf16),
        ],
        scratch_shapes=[
            pltpu.VMEM((TILE, depth), bf16),
            pltpu.VMEM((SHARDS, 192, TILE), bf16),
            pltpu.VMEM((rows, depth), f32),
            pltpu.VMEM((rows, depth), f32),
        ],
        compiler_params=params(),
        cost_estimate=cost(
            18 * rows * depth * tiles * TILE, 12 * depth * tiles * TILE + 20 * rows * depth
        ),
        name="feed_end",
    )(coords, h1, bn, bnt, og, y_part, dbn_part, weights)


def gate_back_kernel(
    rates,
    across,
    order,
    dattn,
    lo0,
    lo1,
    hi0,
    hi1,
    o_in,
    u_in,
    qraw,
    cosine,
    sine,
    du_out,
    do_out,
    back_out,
    held,
):
    step = pl.program_id(0)
    rows = dattn.shape[0]
    join(order[0], lo0, lo1, held, slice(0, 128))
    join(order[0], hi0, hi1, held, slice(128, 256))
    dgated = jnp.zeros((rows, TILE), f32)
    for b in range(4):
        weight = held[:, :, b * 64 : (b + 1) * 64, :].reshape(TILE, TILE)
        dgated = dgated + nt(dattn[:, b * TILE : (b + 1) * TILE], weight)
    dgated = dgated.astype(bf16).astype(f32)
    for s in range(TILE // HD):
        head = step * (TILE // HD) + s
        cols = head_columns(s)
        lead = double(decay_in_of(rates[head]))
        back = jnp.zeros((HD, 2 * HD), f32)
        for c in reversed(range(rows // CH)):
            span = slice(c * CH, (c + 1) * CH)
            o = o_in[span, cols].astype(f32)
            scale = lax.rsqrt(jnp.mean(o * o, axis=1, keepdims=True) + head_floor)
            normed = o * scale
            incoming = dgated[span, cols]
            du_out[span, cols] = (incoming * normed).astype(bf16)
            spread = incoming * u_in[span, cols].astype(f32)
            do = scale * (spread - normed * jnp.mean(normed * spread, axis=1, keepdims=True))
            low = do.astype(bf16)
            do_out[span, cols] = low
            query = rotated(swish(qraw[span, cols].astype(f32)), cosine[span, :], sine[span, :])
            back = across[head] * back + tn(low, (query * lead).astype(bf16))
        back_out[s] = back


def gate_back(rates, across, dattn, out_lo, out_hi, o_in, u_in, qraw, cosine, sine):
    rows, depth = dattn.shape
    return pl.pallas_call(
        gate_back_kernel,
        grid=(depth // TILE,),
        in_specs=[smem(), smem(), smem(), fixed((rows, depth))]
        + out_lo.specs(128, lambda i: 2, chips=2)
        + out_hi.specs(128, lambda i: 2, chips=2)
        + [
            columns(rows, TILE),
            columns(rows, TILE),
            columns(rows, TILE),
            fixed((rows, HD)),
            fixed((rows, HD)),
        ],
        out_specs=[columns(rows, TILE), columns(rows, TILE), head_states()],
        out_shape=[
            struct((rows, depth), bf16),
            struct((rows, depth), bf16),
            struct((H, HD, 2 * HD), f32),
        ],
        scratch_shapes=[pltpu.VMEM((2, 2, 256, TILE), bf16)],
        compiler_params=params(),
        cost_estimate=cost(3 * rows * depth * depth, 16 * rows * depth),
        name="gate_back",
    )(
        rates,
        across,
        out_lo.order,
        dattn,
        *out_lo.arrays(),
        *out_hi.arrays(),
        o_in,
        u_in,
        qraw,
        cosine,
        sine,
    )


def out_gate_grads_kernel(
    coords, a_t, du, gated, dattn, own_out, other_out, stage, stage_out
):
    step = pl.program_id(0)
    z0, y0, c0, x0 = coords[0], coords[1], coords[2], coords[3]
    stage[...] = nn(a_t[...], du[...]).astype(bf16).reshape(SHARDS, 64, TILE)
    rows = pl.ds(pl.multiple_of(256 + step * 64, 64), 64)
    emit(coords, stage, own_out, other_out, rows, "yx")
    g = tn(gated[...], dattn[...]).astype(bf16)
    z_rel = lax.rem(step + 4 - z0, 4)
    for b in range(4):
        stage_out[b] = g[:, b * TILE : (b + 1) * TILE].reshape(4, 64, TILE)
        rows = slice(b * 64, (b + 1) * 64)
        for x in range(2):
            x_rel = x + x0 - 2 * x * x0
            cols = slice(x * HALF, (x + 1) * HALF)
            for y_rel in range(2):
                y = y_rel + y0 - 2 * y_rel * y0
                own_out[y_rel, x_rel, z_rel, rows, :] = stage_out[b, 2 * y + c0, :, cols]
                other_out[y_rel, x_rel, z_rel, rows, :] = stage_out[
                    b, 2 * y + 1 - c0, :, cols
                ]


def out_gate_grads(coords, a_t, du, gated, dattn):
    depth, rows = a_t.shape
    grads = struct((2, 2, 4, 512, HALF), bf16)
    return pl.pallas_call(
        out_gate_grads_kernel,
        grid=(depth // TILE,),
        in_specs=[
            smem(),
            fixed((depth, rows)),
            columns(rows, TILE),
            columns(rows, TILE),
            fixed((rows, depth)),
        ],
        out_specs=[fixed(grads.shape), fixed(grads.shape)],
        out_shape=[grads, grads],
        scratch_shapes=[
            pltpu.VMEM((SHARDS, 64, TILE), bf16),
            pltpu.VMEM((4, 4, 64, TILE), bf16),
        ],
        compiler_params=params(),
        cost_estimate=cost(4 * rows * depth * depth, 12 * rows * depth),
        name="out_gate_grads",
    )(coords, a_t, du, gated, dattn)


def mix_back_kernel(
    rates,
    across,
    qraw,
    kraw,
    v,
    do_in,
    cosine,
    sine,
    state_in,
    back_in,
    dq_out,
    dk_out,
    dv_out,
    key_s,
):
    step = pl.program_id(0)
    rows = qraw.shape[0]
    count = rows // CH
    row = lax.broadcasted_iota(jnp.int32, (CH, CH), 0)
    col = lax.broadcasted_iota(jnp.int32, (CH, CH), 1)
    distance = (row - col).astype(f32)
    for s in range(TILE // HD):
        head = step * (TILE // HD) + s
        cols = head_columns(s)
        rate = rates[head]
        lead = double(decay_in_of(rate))
        tail = double(decay_out_of(rate))
        mask = jnp.where(distance >= 0, jnp.exp(-rate * jnp.maximum(distance, 0.0)), 0.0)
        mask_t = jnp.where(distance <= 0, jnp.exp(rate * jnp.minimum(distance, 0.0)), 0.0)
        state = state_in[s]
        states = []
        for c in range(count):
            span = slice(c * CH, (c + 1) * CH)
            key_float = rotated(
                swish(kraw[span, cols].astype(f32)), cosine[span, :], sine[span, :]
            )
            key_s[span, :] = key_float.astype(bf16)
            states.append(state.astype(bf16))
            if c < count - 1:
                state = across[head] * state + tn(v[span, cols], (key_float * tail).astype(bf16))
        back = back_in[s]
        for c in reversed(range(count)):
            span = slice(c * CH, (c + 1) * CH)
            cos_c, sin_c = cosine[span, :], sine[span, :]
            query_raw = qraw[span, cols].astype(f32)
            query_float = rotated(swish(query_raw), cos_c, sin_c)
            query = query_float.astype(bf16)
            key = key_s[span, :]
            value = v[span, cols]
            do = do_in[span, cols]
            back_low = back.astype(bf16)
            weights_t = (nt(key, query) * mask_t).astype(bf16)
            dscore = (nt(do, value) * mask).astype(bf16)
            dscore_t = (nt(value, do) * mask_t).astype(bf16)
            dqr = nn(dscore, key) + lead * nn(do, states[c])
            dkr = nn(dscore_t, query) + tail * nn(value, back_low)
            dv = nn(weights_t, do) + tail[:, :HD] * nt(key, back_low)
            back = across[head] * back + tn(do, (query_float * lead).astype(bf16))
            dq = dqr[:, :HD] * cos_c + dqr[:, HD:] * sin_c
            dk = dkr[:, :HD] * cos_c + dkr[:, HD:] * sin_c
            dq_out[span, cols] = (dq * swish_slope(query_raw)).astype(bf16)
            dk_out[span, cols] = (dk * swish_slope(kraw[span, cols].astype(f32))).astype(bf16)
            dv_out[span, cols] = dv.astype(bf16)


def mix_back(rates, across, qraw, kraw, v, do_in, cosine, sine, state_in, back_in):
    rows, width = qraw.shape
    return pl.pallas_call(
        mix_back_kernel,
        grid=(width // TILE,),
        in_specs=[smem(), smem()]
        + [columns(rows, TILE)] * 4
        + [fixed((rows, HD)), fixed((rows, HD)), head_states(), head_states()],
        out_specs=[columns(rows, TILE)] * 3,
        out_shape=[struct((rows, width), bf16)] * 3,
        scratch_shapes=[pltpu.VMEM((rows, 2 * HD), bf16)],
        compiler_params=params(),
        cost_estimate=cost(8 * rows * width * width, 16 * rows * width),
        name="mix_back",
    )(rates, across, qraw, kraw, v, do_in, cosine, sine, state_in, back_in)


def query_grads_kernel(coords, a_t, dq, dk, dv, own_out, other_out, stage):
    for n, incoming in enumerate((dq, dk, dv)):
        stage[:, n * 64 : (n + 1) * 64, :] = (
            nn(a_t[...], incoming[...]).astype(bf16).reshape(SHARDS, 64, TILE)
        )
    emit(coords, stage, own_out, other_out, slice(0, 192), "xy")


def query_grads(coords, a_t, dq, dk, dv):
    depth, rows = a_t.shape
    grads = struct((2, 2, 4, 3 * 256, HALF), bf16)
    return pl.pallas_call(
        query_grads_kernel,
        grid=(depth // TILE,),
        in_specs=[smem(), fixed((depth, rows))] + [columns(rows, TILE)] * 3,
        out_specs=[grad_block(192), grad_block(192)],
        out_shape=[grads, grads],
        scratch_shapes=[pltpu.VMEM((SHARDS, 192, TILE), bf16)],
        compiler_params=params(),
        cost_estimate=cost(6 * rows * depth * depth, 14 * rows * depth),
        name="query_grads",
    )(coords, a_t, dq, dk, dv)


def input_back_kernel(order, x, dh1, dq, dk, dv, du, *refs):
    weights, (out, total, held) = refs[:8], refs[8:]
    step = pl.program_id(0)

    @pl.when(step == 0)
    def _():
        total[...] = jnp.zeros_like(total)

    part = None
    for n, incoming in enumerate((dq, dk, dv, du)):
        join(order[0], weights[2 * n], weights[2 * n + 1], held.at[n])
        term = nt(incoming[...], held[n].reshape(-1, TILE))
        part = term if part is None else part + term
    total[...] += part

    @pl.when(step == pl.num_programs(0) - 1)
    def _():
        hidden = x[...].astype(f32)
        scale = lax.rsqrt(jnp.mean(hidden * hidden, axis=1, keepdims=True) + epsilon)
        normed = hidden * scale
        incoming = total[...]
        out[...] = (
            dh1[...]
            + scale * (incoming - normed * jnp.mean(normed * incoming, axis=1, keepdims=True))
        ).astype(bf16)


def input_back(x, dh1, grads, weights):
    rows, depth = x.shape
    specs, arrays = [], []
    for weight in weights:
        specs += weight.specs(64, lambda i: i)
        arrays += weight.arrays()
    return pl.pallas_call(
        input_back_kernel,
        grid=(depth // TILE,),
        in_specs=[smem(), fixed((rows, depth)), fixed((rows, depth))]
        + [columns(rows, TILE)] * 4
        + specs,
        out_specs=fixed((rows, depth)),
        out_shape=struct((rows, depth), bf16),
        scratch_shapes=[
            pltpu.VMEM((rows, depth), f32),
            pltpu.VMEM((4, 8, 2, 64, TILE), bf16),
        ],
        compiler_params=params(),
        cost_estimate=cost(8 * rows * depth * depth, 24 * rows * depth),
        name="input_back",
    )(weights[0].order, x, dh1, *grads, *arrays)


def square_blocks(w, shards):
    return w.reshape(shards, 64, 4, TILE).transpose(0, 2, 1, 3).reshape(shards, 256, TILE)


def square_back(blocks, shards):
    return blocks.reshape(shards, 4, 64, TILE).transpose(0, 2, 1, 3).reshape(shards * 64, 1024)


def feed_blocks(first, second, down, shards):
    hidden = first.shape[1]
    tiles = hidden // TILE

    def wide(w):
        return w.reshape(shards, 64, SHARDS, tiles, 16).transpose(0, 3, 1, 2, 4).reshape(
            shards, tiles, 64, TILE
        )

    low = down.reshape(shards, tiles, 16, 4, TILE).transpose(0, 1, 3, 2, 4)
    return jnp.concatenate(
        [wide(first), wide(second), low.reshape(shards, tiles, 64, TILE)], axis=2
    ).reshape(shards, tiles * 192, TILE)


def feed_back(blocks, shards):
    tiles = blocks.shape[1] // 192
    blocks = blocks.reshape(shards, tiles, 192, TILE)

    def wide(part):
        return part.reshape(shards, tiles, 64, SHARDS, 16).transpose(0, 2, 3, 1, 4).reshape(
            shards * 64, tiles * TILE
        )

    low = blocks[:, :, 128:].reshape(shards, tiles, 4, 16, TILE).transpose(0, 1, 3, 2, 4)
    return wide(blocks[:, :, :64]), wide(blocks[:, :, 64:128]), low.reshape(-1, 1024)


class Grid:
    def __init__(self):
        index = lax.axis_index("wt")
        self.z, self.y, self.core = index // 4, (index // 2) % 2, index % 2
        self.x = lax.axis_index("seq")

    def coords(self):
        return jnp.stack([self.z, self.y, self.core, self.x]).astype(jnp.int32)

    def over(self, axis, value):
        if axis == "x":
            return lax.ppermute(value, "seq", [(0, 1), (1, 0)])
        step = {"y": 2, "core": 1}[axis]
        return lax.ppermute(value, "wt", [(i, i ^ step) for i in range(SHARDS)])

    def shift_z(self, value, k):
        return lax.ppermute(value, "wt", [(i, (i + 4 * k) % SHARDS) for i in range(SHARDS)])

    def in_order(self, flag, own, received, axis):
        near = jnp.concatenate([own, received], axis=axis)
        far = jnp.concatenate([received, own], axis=axis)
        return jnp.where(flag == 0, near, far)

    def gather(self, y_first, x_first):
        split = y_first.shape[0]
        both = jnp.concatenate([y_first, x_first], axis=0)
        own = lax.dynamic_slice_in_dim(both, self.x * HALF, HALF, axis=1)
        parts = [own] + [self.shift_z(own, k) for k in (1, 2, 3)]
        ring = jnp.stack(parts[::-1] + parts[::-1])
        ring = lax.dynamic_slice_in_dim(ring, (3 - self.z) % 4, 4, axis=0)
        one, two = ring[:, None, :split], ring[:, None, split:]
        one_y, two_x = self.over("y", one), self.over("x", two)
        one = self.in_order(self.y, one, one_y, 1)
        two = self.in_order(self.x, two, two_x, 3)
        one_x, two_y = self.over("x", one), self.over("y", two)
        one = self.in_order(self.x, one, one_x, 3).reshape(8, 1, -1, TILE)
        two = self.in_order(self.y, two, two_y, 1).reshape(8, 1, -1, TILE)
        order = self.core.astype(jnp.int32)[None]
        return (
            Gathered(one, self.over("core", one), order),
            Gathered(two, self.over("core", two), order),
        )

    def scatter(self, own, other, first, second):
        got = self.over("core", other)
        far = (own[1].astype(f32) + got[1].astype(f32)).astype(bf16)
        got_first = self.over(first, far)
        near = own[0].astype(f32) + got[0].astype(f32) + got_first.astype(f32)
        got_second = self.over(second, near[1].astype(bf16))
        total = near[0] + got_second.astype(f32)
        result = total[0]
        for k in (1, 2, 3):
            result = result + self.shift_z(total[k].astype(bf16), k).astype(f32)
        return result.astype(bf16)

    def both_halves(self, half):
        return self.in_order(self.x, half, self.over("x", half), 1)


class Plain:
    def coords(self):
        return jnp.zeros((4,), jnp.int32)


def natural(own, other, order):
    both = jnp.stack([own, other])
    x_axis, y_axis = (1, 2) if order == "xy" else (2, 1)
    both = both.transpose(3, y_axis, 0, 4, x_axis, 5)
    return both.reshape(SHARDS, own.shape[3], TILE)


def body(
    activations,
    w_query,
    w_key,
    w_value,
    w_gate,
    w_out,
    w_first,
    w_second,
    w_down,
    decay_rate,
    seq_lengths,
    out_grad,
):
    seq_count = lax.axis_size("seq")
    seq_index = lax.axis_index("seq")
    direct = seq_count == 2 and lax.axis_size("wt") == SHARDS
    x = activations[0]
    og = out_grad[0]
    rows = x.shape[0]
    assert MIN_LEN % rows == 0

    if direct:
        grid = Grid()
        key_block, value_block, query_block, gate_block, out_block = (
            square_blocks(w, 1)[0] for w in (w_key, w_value, w_query, w_gate, w_out)
        )
        feed_block = feed_blocks(w_first, w_second, w_down, 1)[0]
        feed_weights = lax.all_gather(feed_block, "wt", axis=0, tiled=True)
        feed_weights = feed_weights.reshape(8, 2, -1, TILE)
        keys, values = grid.gather(key_block, value_block)
        queries, gates = grid.gather(
            jnp.concatenate([query_block, out_block[:128]]),
            jnp.concatenate([gate_block, out_block[128:]]),
        )
    else:
        grid = Plain()
        full_key, full_value, full_query, full_gate, full_out = (
            square_blocks(lax.all_gather(w, "wt", axis=0, tiled=True), SHARDS)
            for w in (w_key, w_value, w_query, w_gate, w_out)
        )
        feed_weights = feed_blocks(
            *(lax.all_gather(w, "wt", axis=0, tiled=True) for w in (w_first, w_second, w_down)),
            SHARDS,
        ).reshape(8, 2, -1, TILE)

        def held(block):
            block = block.reshape(8, 2, -1, TILE)
            return Gathered(block, block, jnp.zeros((1,), jnp.int32))

        keys, values = held(full_key), held(full_value)
        queries = held(jnp.concatenate([full_query, full_out[:, :128]], axis=1))
        gates = held(jnp.concatenate([full_gate, full_out[:, 128:]], axis=1))
    coords = grid.coords()

    lengths = seq_lengths[0]
    starts = jnp.cumsum(lengths) - lengths
    begin = seq_index * rows
    begun = (starts <= begin) & (lengths > 0)
    first_token = jnp.max(jnp.where(begun, starts, 0))
    keep = jnp.where(begin == first_token, 0.0, 1.0).astype(f32)
    position = (begin - first_token + jnp.arange(rows, dtype=jnp.int32)).astype(f32)
    frequency = 10000.0 ** (-jnp.arange(HD, dtype=f32) / HD)
    angles = position[:, None] * frequency[None, :]
    cosine, sine = jnp.cos(angles), jnp.sin(angles)
    across = jnp.exp(-decay_rate * CH)
    whole = jnp.exp(-decay_rate * rows)[:, None, None]

    a, a_t = prepare(x)
    kraw, v, own_state = key_value(decay_rate, across, a, keys, values, cosine, sine)
    ahead = [(i, i + 1) for i in range(seq_count - 1)]
    state_in = jnp.zeros_like(own_state)
    for _ in range(seq_count - 1):
        sent = (whole * state_in + own_state).astype(bf16)
        state_in = keep * lax.ppermute(sent, "seq", ahead).astype(f32)

    qraw, u, o, gated = mix(
        decay_rate, across, a, queries, gates, kraw, v, cosine, sine, state_in
    )
    h1, bn, bn_t = residual(x, gated, queries, gates)
    tiles = w_first.shape[1] // TILE
    early = (tiles + 1) // 2
    g_early, y_part, dbn_part = feed_start(bn, bn_t, og, feed_weights, 0, early)
    if direct:
        early_share = lax.psum_scatter(
            g_early.reshape(SHARDS, -1, TILE), "wt", scatter_dimension=0, tiled=True
        )[0]
    own_late, other_late, layer_out, dh1, dattn = feed_end(
        coords, h1, bn, bn_t, og, y_part, dbn_part, feed_weights, early, tiles - early
    )
    du, do, own_back = gate_back(
        decay_rate, across, dattn, queries, gates, o, u, qraw, cosine, sine
    )
    behind = [(i + 1, i) for i in range(seq_count - 1)]
    back_in = jnp.zeros_like(own_back)
    for _ in range(seq_count - 1):
        sent = (keep * (whole * back_in + own_back)).astype(bf16)
        back_in = lax.ppermute(sent, "seq", behind).astype(f32)
    own_og, other_og = out_gate_grads(coords, a_t, du, gated, dattn)
    dq, dk, dv = mix_back(
        decay_rate, across, qraw, kraw, v, do, cosine, sine, state_in, back_in
    )
    own_qkv, other_qkv = query_grads(coords, a_t, dq, dk, dv)
    input_grad = input_back(x, dh1, (dq, dk, dv, du), (queries, keys, values, gates))

    if direct:
        early_total = early_share.astype(f32) + grid.over("x", early_share).astype(f32)
        late_total = grid.both_halves(grid.scatter(own_late, other_late, "x", "y")).astype(f32)
        og_total = grid.both_halves(grid.scatter(own_og, other_og, "y", "x")).astype(f32)
        qkv_total = grid.both_halves(grid.scatter(own_qkv, other_qkv, "x", "y")).astype(f32)
        feed_total = jnp.concatenate([early_total, late_total])[None]
        og_total, qkv_total = og_total[None], qkv_total[None]
        shards = 1
    else:
        feed_total = jnp.concatenate([g_early, natural(own_late, other_late, "xy")], axis=1)
        og_total = natural(own_og, other_og, "yx")
        qkv_total = natural(own_qkv, other_qkv, "xy")
        shards = SHARDS
    qkv_total = qkv_total.reshape(shards, 4, 3, 64, TILE)
    squares = [qkv_total[:, :, n] for n in range(3)] + [og_total[:, 256:], og_total[:, :256]]
    totals = [square_back(g, shards) for g in squares] + list(feed_back(feed_total, shards))
    if not direct:
        totals = [
            lax.psum(lax.psum_scatter(g, "wt", scatter_dimension=0, tiled=True), "seq").astype(f32)
            for g in totals
        ]
    return (layer_out[None], input_grad[None], *totals)


def solution(mesh):
    weight = P("wt", None)
    tokens = P("wt", "seq", None)
    return jax.shard_map(
        body,
        mesh=mesh,
        in_specs=(tokens,) + (weight,) * 8 + (P(), weight, tokens),
        out_specs=(tokens, tokens) + (weight,) * 8,
        check_vma=False,
    )
```

time: 1130 us -> 544 us (0.48)
  waiting for transfers between devices: 899 us -> 174 us
  starting transfers between devices: 6.02 us -> 97.3 us
  Pallas kernels: 167 us -> 185 us
  local copies, waits for them, and re-layouts: 10.8 us -> 25 us
  other arithmetic: 25.9 us -> 37.6 us
    reduce_scatter x8 -> x1, waiting for transfers between devices: 509 us -> 0.02 us  [body(): lax.psum_scatter(g_early.reshape(SHARDS, -1, TILE), 'wt', scatter_dimensi...]
    all_gather x8 -> x1, waiting for transfers between devices: 318 us -> 0.01 us  [body(): feed_weights = lax.all_gather(feed_block, 'wt', axis=0, tiled=True)]
    ppermute x0 -> x40, waiting for transfers between devices: none -> 162 us  [the longest x15 54.8 us: shift_z(): lax.ppermute(value, 'wt', [(i, (i + 4 * k) % SHARDS) for i in range(SHARD...]
    ppermute x0 -> x40, starting transfers between devices: none -> 92.3 us  [the longest x15 70.9 us: shift_z(): lax.ppermute(value, 'wt', [(i, (i + 4 * k) % SHARDS) for i in range(SHARD...]
    psum x1 -> x0, waiting for transfers between devices: 40.1 us -> none  [body(): totals = [lax.psum(share, 'seq').astype(f32) for share in shares]]
    pallas_call x7 -> x9, Pallas kernels: 138 us -> 155 us  [the longest x1 39.2 us: feed_end(): pl.pallas_call(feed_end_kernel, grid=(tiles,), in_specs=[smem(), fixed((r...]
  transfers between devices with their start and end apart: 19 -> 44, of which waited for: 18 -> 19; matrix products, arithmetic and copies ran while one was open for 2% -> 9% of each run, Pallas kernels for 8% -> 28%
where the time goes in v2:
time: 544 us; the launch traced here: 536 us
  Pallas kernels  185 us (34%)
  waiting for transfers between devices  174 us (32%)
  starting transfers between devices  97.3 us (18%)
  other arithmetic  37.6 us (7%)
  local copies, waits for them, and re-layouts  25 us (5%)
  between operations  16.6 us (3%)
    ppermute x15, starting transfers between devices, shift_z(): lax.ppermute(value, 'wt', [(i, (i + 4 * k) % SHARDS) for i in range(SHARD...  70.9 us
    ppermute x15, waiting for transfers between devices, shift_z(): lax.ppermute(value, 'wt', [(i, (i + 4 * k) % SHARDS) for i in range(SHARD...  54.8 us
    ppermute x11, waiting for transfers between devices, over(): return lax.ppermute(value, 'seq', [(0, 1), (1, 0)])  54.4 us
    ppermute x14, waiting for transfers between devices, over(): return lax.ppermute(value, 'wt', [(i, i ^ step) for i in range(SHARDS)])  52.5 us
    pallas_call x1, Pallas kernels, feed_end(): pl.pallas_call(feed_end_kernel, grid=(tiles,), in_specs=[smem(), fixed((r...  39.2 us
    pallas_call x1, Pallas kernels, feed_start(): pl.pallas_call(feed_start_kernel, grid=(tiles,), in_specs=[fixed((rows, d...  37.3 us
    pallas_call x1, Pallas kernels, mix_back(): pl.pallas_call(mix_back_kernel, grid=(width // TILE,), in_specs=[smem(),...  18.3 us
    pallas_call x1, Pallas kernels, input_back(): pl.pallas_call(input_back_kernel, grid=(depth // TILE,), in_specs=[smem()...  17.7 us
  transfers between devices with their start and end apart: 44, of which 19 were waited for; matrix products, arithmetic and copies ran while one was open for 9% of the time, Pallas kernels for 28%

profile of v2, /device:TPU:12, one launch (start us, length us, event | category | flops | bytes accessed | tf_op | source)
XLA Modules:
  0.0 536.1 jit_solution(694731074574444074)
XLA Ops:
  24.6 4.5 collective-permute-done.10
  29.1 9.1 %collective-permute-done.11 = bf16[512,128]{1,0:T(8,128)(2,1)S(1)} collective-permute-done((bf16[512,128]{1,0:T(8,128)(2,1)S(1)}, bf16[512,128]{1,0:T(8,128)(2,1)S(1)}, u32[]{:S(2)}, u32[]{:S(2)}) %collective-permute-start.11) | collective-permute-done | bytes 131104 | tf_op jit(solution)/shard_map/ppermute | solution.py:842
  44.1 7.9 %collective-permute-done.1 = bf16[768,128]{1,0:T(8,128)(2,1)S(1)} collective-permute-done((bf16[768,128]{1,0:T(8,128)(2,1)S(1)}, bf16[768,128]{1,0:T(8,128)(2,1)S(1)}, u32[]{:S(2)}, u32[]{:S(2)}) %collective-permute-start.1) | collective-permute-done | bytes 196640 | tf_op jit(solution)/shard_map/ppermute | solution.py:842
  52.1 7.5 %collective-permute-done.2 = bf16[768,128]{1,0:T(8,128)(2,1)S(1)} collective-permute-done((bf16[768,128]{1,0:T(8,128)(2,1)S(1)}, bf16[768,128]{1,0:T(8,128)(2,1)S(1)}, u32[]{:S(2)}, u32[]{:S(2)}) %collective-permute-start.2) | collective-permute-done | bytes 196640 | tf_op jit(solution)/shard_map/ppermute | solution.py:842
  64.6 7.5 %collective-permute-done.6 = bf16[4,1,384,128]{3,2,1,0:T(8,128)(2,1)} collective-permute-done((bf16[4,1,384,128]{3,2,1,0:T(8,128)(2,1)S(1)}, bf16[4,1,384,128]{3,2,1,0:T(8,128)(2,1)}, u32[]{:S(2)}, u32[]{:S(2)}) %collective-permute-start.6) | collective-permute-done | bytes 393248 | tf_op jit(solution)/shard_map/ppermute | solution.py:837
  75.7 9.1 %collective-permute-done.16 = bf16[4,1,256,256]{3,2,1,0:T(8,128)(2,1)} collective-permute-done((bf16[4,1,256,256]{3,2,1,0:T(8,128)(2,1)S(1)}, bf16[4,1,256,256]{3,2,1,0:T(8,128)(2,1)}, u32[]{:S(2)}, u32[]{:S(2)}) %collective-permute-start.16) | collective-permute-done | bytes 524320 | tf_op jit(solution)/shard_map/ppermute | solution.py:839
  106.4 10.3 %key_value.1 = (bf16[1024,1024]{1,0:T(8,128)(2,1)}, bf16[1024,1024]{1,0:T(8,128)(2,1)}, f32[8,128,256]{2,1,0:T(8,128)}) custom-call(f32[8]{0:T(128)} %rates.7, f32[8]{0:T(128)} %get-tuple-element.122.across, s32[1]{0:T(128)} %bitcast.2.order, bf16[1024,1024]{1,0:T(8,128)(2,1)} %get-tuple-element.40.a, ...), custom_call_target="tpu_custom_call" | custom-call | flops 5368709120 | bytes 10485760 | tf_op jit(solution)/shard_map/key_value/pallas_call | solution.py:182
  123.8 9.5 %collective-permute-done.18 = bf16[8,128,256]{2,1,0:T(8,128)(2,1)} collective-permute-done((bf16[8,128,256]{2,1,0:T(8,128)(2,1)}, bf16[8,128,256]{2,1,0:T(8,128)(2,1)}, u32[]{:S(2)}, u32[]{:S(2)}) %collective-permute-start.18) | collective-permute-done | bytes 524320 | tf_op jit(solution)/shard_map/ppermute | solution.py:971
  135.4 16.1 %mix.1 = (bf16[1024,1024]{1,0:T(8,128)(2,1)}, bf16[1024,1024]{1,0:T(8,128)(2,1)}, bf16[1024,1024]{1,0:T(8,128)(2,1)}, bf16[1024,1024]{1,0:T(8,128)(2,1)}) custom-call(f32[8]{0:T(128)} %rates.7, f32[8]{0:T(128)} %get-tuple-element.122.across, s32[1]{0:T(128)} %bitcast.2.order, bf16[1024,1024]{1,0:T(8,128)(2,1)} %get-tuple-element.40.a, ...), custom_call_target="tpu_custom_call" | custom-call | flops 8589934592 | bytes 18874368 | tf_op jit(solution)/shard_map/mix/pallas_call | solution.py:257
  151.5 7.8 %residual.1 = (f32[1024,1024]{1,0:T(8,128)}, bf16[1024,1024]{1,0:T(8,128)(2,1)}, bf16[1024,1024]{1,0:T(8,128)(2,1)}) custom-call(s32[1]{0:T(128)} %bitcast.2.order, bf16[1024,1024]{1,0:T(8,128)(2,1)} %bitcast.219, bf16[1024,1024]{1,0:T(8,128)(2,1)} %get-tuple-element.44.gated, bf16[8,1,384,256]{3,2,1,0:T(8,128)(2,1)} %copy-done.1, ...), custom_call_target="tpu_custom_call" | custom-call | flops 2147483648 | bytes 14680064 | tf_op jit(solution)/shard_map/residual/pallas_call | solution.py:309
  159.3 37.3 %feed_start.1 = (bf16[16,1152,256]{2,1,0:T(8,128)(2,1)}, bf16[1024,1024]{1,0:T(8,128)(2,1)}, bf16[1024,1024]{1,0:T(8,128)(2,1)}) custom-call(bf16[1024,1024]{1,0:T(8,128)(2,1)} %get-tuple-element.46.bn, bf16[1024,1024]{1,0:T(8,128)(2,1)} %get-tuple-element.47.bnt, bf16[1024,1024]{1,0:T(8,128)(2,1)} %bitcast.269, bf16[8,2,2112,256]{3,2,1,0:T(8,128)(2,1)} %bitcast.267), custom_call_target="tpu_custom_call" | custom-call | flops 28991029248 | bytes 29360128 | tf_op jit(solution)/shard_map/feed_start/pallas_call | solution.py:371
  196.6 39.2 %feed_end.1 = (bf16[2,2,4,960,128]{4,3,2,1,0:T(8,128)(2,1)}, bf16[2,2,4,960,128]{4,3,2,1,0:T(8,128)(2,1)}, bf16[1024,1024]{1,0:T(8,128)(2,1)}, f32[1024,1024]{1,0:T(8,128)}, bf16[1024,1024]{1,0:T(8,128)(2,1)}) custom-call(s32[4]{0:T(128)} %pad_add_fusion.coords, f32[1024,1024]{1,0:T(8,128)} %get-tuple-element.45.h1, ...), custom_call_target="tpu_custom_call" | custom-call | flops 24159191040 | bytes 36700160 | tf_op jit(solution)/shard_map/feed_end/pallas_call | solution.py:453
  235.8 11.8 %gate_back.1 = (bf16[1024,1024]{1,0:T(8,128)(2,1)}, bf16[1024,1024]{1,0:T(8,128)(2,1)}, f32[8,128,256]{2,1,0:T(8,128)}) custom-call(f32[8]{0:T(128)} %rates.7, f32[8]{0:T(128)} %get-tuple-element.122.across, s32[1]{0:T(128)} %bitcast.2.order, bf16[1024,1024]{1,0:T(8,128)(2,1)} %get-tuple-element.53.dattn, bf16[8,1,384,256]{3,2,1,0:T(8,128)(2,1)} %copy-done.1, ...), custom_call_target="tpu_custom_call" | custom-call | flops 3221225472 | bytes 16777216 | tf_op jit(solution)/shard_map/gate_back/pallas_call | solution.py:545
  251.2 11.0 %out_gate_grads.1 = (bf16[2,2,4,512,128]{4,3,2,1,0:T(8,128)(2,1)}, bf16[2,2,4,512,128]{4,3,2,1,0:T(8,128)(2,1)}) custom-call(s32[4]{0:T(128)} %pad_add_fusion.coords, bf16[1024,1024]{1,0:T(8,128)(2,1)} %get-tuple-element.62.a_t, bf16[1024,1024]{1,0:T(8,128)(2,1)} %get-tuple-element.61.du, bf16[1024,1024]{1,0:T(8,128)(2,1)} %get-tuple-element.44.gated, ...), custom_call_target="tpu_custom_call" | custom-call | flops 4294967296 | bytes 12582912 | tf_op jit(solution)/shard_map/out_gate_grads/pallas_call | solution.py:610
  267.8 18.3 %mix_back.1 = (bf16[1024,1024]{1,0:T(8,128)(2,1)}, bf16[1024,1024]{1,0:T(8,128)(2,1)}, bf16[1024,1024]{1,0:T(8,128)(2,1)}) custom-call(f32[8]{0:T(128)} %rates.7, f32[8]{0:T(128)} %get-tuple-element.122.across, bf16[1024,1024]{1,0:T(8,128)(2,1)} %get-tuple-element.52.qraw, bf16[1024,1024]{1,0:T(8,128)(2,1)} %get-tuple-element.41.kraw, ...), custom_call_target="tpu_custom_call" | custom-call | flops 8589934592 | bytes 16777216 | tf_op jit(solution)/shard_map/mix_back/pallas_call | solution.py:700
  286.2 12.1 %query_grads.1 = (bf16[2,2,4,768,128]{4,3,2,1,0:T(8,128)(2,1)}, bf16[2,2,4,768,128]{4,3,2,1,0:T(8,128)(2,1)}) custom-call(s32[4]{0:T(128)} %pad_add_fusion.coords, bf16[1024,1024]{1,0:T(8,128)(2,1)} %get-tuple-element.62.a_t, bf16[1024,1024]{1,0:T(8,128)(2,1)} %get-tuple-element.58.dq, bf16[1024,1024]{1,0:T(8,128)(2,1)} %get-tuple-element.59.dk, ...), custom_call_target="tpu_custom_call" | custom-call | flops 6442450944 | bytes 14680064 | tf_op jit(solution)/shard_map/query_grads/pallas_call | solution.py:726
  301.2 33.6 %collective-permute-done.28 = bf16[2,4,512,128]{3,2,1,0:T(8,128)(2,1)S(1)} collective-permute-done((bf16[2,4,512,128]{3,2,1,0:T(8,128)(2,1)S(1)}, bf16[2,4,512,128]{3,2,1,0:T(8,128)(2,1)S(1)}, u32[]{:S(2)}, u32[]{:S(2)}) %collective-permute-start.28) | collective-permute-done | bytes 1048608 | tf_op jit(solution)/shard_map/ppermute | solution.py:839
  342.5 43.0 %collective-permute-done.29 = bf16[4,512,128]{2,1,0:T(8,128)(2,1)S(1)} collective-permute-done((bf16[4,512,128]{2,1,0:T(8,128)(2,1)S(1)}, bf16[4,512,128]{2,1,0:T(8,128)(2,1)S(1)}, u32[]{:S(2)}, u32[]{:S(2)}) %collective-permute-start.29) | collective-permute-done | bytes 524320 | tf_op jit(solution)/shard_map/ppermute | solution.py:837
  387.8 30.4 %collective-permute-start.31 = (bf16[512,128]{1,0:T(8,128)(2,1)S(1)}, bf16[512,128]{1,0:T(8,128)(2,1)S(1)}, u32[]{:S(2)}, u32[]{:S(2)}) collective-permute-start(bf16[512,128]{1,0:T(8,128)(2,1)S(1)} %get-tuple-element.116), channel_id=1, source_target_pairs={{0,8},{1,9},{2,10},{3,11},{4,12},{5,13},{6,14},{7,15},{8,0},{9,1},... | collective-permute-start | bytes 393224 | tf_op jit(solution)/shard_map/ppermute | solution.py:842
  432.7 6.5 %collective-permute-done.22 = bf16[4,768,128]{2,1,0:T(8,128)(2,1)S(1)} collective-permute-done((bf16[4,768,128]{2,1,0:T(8,128)(2,1)S(1)}, bf16[4,768,128]{2,1,0:T(8,128)(2,1)S(1)}, u32[]{:S(2)}, u32[]{:S(2)}) %collective-permute-start.22) | collective-permute-done | bytes 786464 | tf_op jit(solution)/shard_map/ppermute | solution.py:839
  443.6 22.2 %collective-permute-start.24 = (bf16[768,128]{1,0:T(8,128)(2,1)}, bf16[768,128]{1,0:T(8,128)(2,1)}, u32[]{:S(2)}, u32[]{:S(2)}) collective-permute-start(bf16[768,128]{1,0:T(8,128)(2,1)} %get-tuple-element.111), channel_id=1, source_target_pairs={{0,8},{1,9},{2,10},{3,11},{4,12},{5,13},{6,14},{7,15},{8,0},{9,1},... | collective-permute-start | bytes 589832 | tf_op jit(solution)/shard_map/ppermute | solution.py:842
  465.8 17.7 %input_back.1 = bf16[1024,1024]{1,0:T(8,128)(2,1)} custom-call(s32[1]{0:T(128)} %bitcast.2.order, bf16[1024,1024]{1,0:T(8,128)(2,1)} %bitcast.220, f32[1024,1024]{1,0:T(8,128)} %get-tuple-element.51.dh1, bf16[1024,1024]{1,0:T(8,128)(2,1)} %get-tuple-element.58.dq, bf16[1024,1024]{1,0:T(8,128)(2,1)} %get-tuple-element.59.dk, ...), custom_call_target="tpu_custom_call" | custom-call | flops 8589934592 | bytes 25165824 | tf_op jit(solution)/shard_map/input_back/pallas_call | solution.py:772
  496.8 11.0 %collective-permute-done.38 = bf16[960,128]{1,0:T(8,128)(2,1)S(1)} collective-permute-done((bf16[960,128]{1,0:T(8,128)(2,1)S(1)}, bf16[960,128]{1,0:T(8,128)(2,1)S(1)}, u32[]{:S(2)}, u32[]{:S(2)}) %collective-permute-start.38) | collective-permute-done | bytes 245792 | tf_op jit(solution)/shard_map/ppermute | solution.py:842
  516.9 3.9 collective-permute-done.41
  (221 shorter events, 132.2 us)
Async XLA Ops:
  7.2 152.1 %all-gather.2.cloned.1.call-start = ((), (), s32[]{:S(2)}) async-start(), calls=%async_computation.1 | async-start | bytes 18382848 | tf_op jit(solution)/shard_map/all_gather | solution.py:925
  14.4 481.8 %reduce-scatter.2.cloned.1.call-start = ((), (), s32[]{:S(2)}) async-start(), calls=%async_computation.2 | async-start | bytes 10027008 | tf_op jit(solution)/shard_map/reduce_scatter | solution.py:981
  20.8 31.2 %collective-permute-start.1 = (bf16[768,128]{1,0:T(8,128)(2,1)S(1)}, bf16[768,128]{1,0:T(8,128)(2,1)S(1)}, u32[]{:S(2)}, u32[]{:S(2)}) collective-permute-start(bf16[768,128]{1,0:T(8,128)(2,1)S(1)} %fusion.26), channel_id=1, source_target_pairs={{0,8},{1,9},{2,10},{3,11},{4,12},{5,13},{6,14},{7,15},{8,0},{9,1},... | collective-permute-start | bytes 589832 | tf_op jit(solution)/shard_map/ppermute | solution.py:842
  22.3 37.3 %collective-permute-start.2 = (bf16[768,128]{1,0:T(8,128)(2,1)S(1)}, bf16[768,128]{1,0:T(8,128)(2,1)S(1)}, u32[]{:S(2)}, u32[]{:S(2)}) collective-permute-start(bf16[768,128]{1,0:T(8,128)(2,1)S(1)} %fusion.26), channel_id=1, source_target_pairs={{0,4},{1,5},{2,6},{3,7},{4,8},{5,9},{6,10},{7,11},{8,12},{9,13},{1... | collective-permute-start | bytes 589832 | tf_op jit(solution)/shard_map/ppermute | solution.py:842
  38.4 23.5 %collective-permute-start.15 = (bf16[4,1,256,128]{3,2,1,0:T(8,128)(2,1)S(1)}, bf16[4,1,256,128]{3,2,1,0:T(8,128)(2,1)S(1)}, u32[]{:S(2)}, u32[]{:S(2)}) collective-permute-start(bf16[4,1,256,128]{3,2,1,0:T(8,128)(2,1)S(1)} %get-tuple-element.101), channel_id=1, source_target_pairs={{0,16},{16,0},{1,17},{17,1},{2,18},{18,2},{3,19},{19,3},{4,20},{20... | collective-permute-start | bytes 786440 | tf_op jit(solution)/shard_map/ppermute | solution.py:837
  39.9 23.8 %collective-permute-start.12 = (bf16[4,1,256,128]{3,2,0,1:T(8,128)(2,1)S(1)}, bf16[4,1,256,128]{3,2,0,1:T(8,128)(2,1)S(1)}, u32[]{:S(2)}, u32[]{:S(2)}) collective-permute-start(bf16[4,1,256,128]{3,2,0,1:T(8,128)(2,1)S(1)} %get-tuple-element.102), channel_id=1, source_target_pairs={{0,2},{1,3},{2,0},{3,1},{4,6},{5,7},{6,4},{7,5},{8,10},{9,11},{10,... | collective-permute-start | bytes 786440 | tf_op jit(solution)/shard_map/ppermute | solution.py:839
  73.5 24.4 %collective-permute-start.7 = (bf16[4,1,384,256]{3,2,1,0:T(8,128)(2,1)S(1)}, bf16[4,1,384,256]{3,2,1,0:T(8,128)(2,1)}, u32[]{:S(2)}, u32[]{:S(2)}) collective-permute-start(bf16[4,1,384,256]{3,2,1,0:T(8,128)(2,1)S(1)} %maximum_select_fusion.5), channel_id=1, source_target_pairs={{0,2},{1,3},{2,0},{3,1},{4,6},{5,7},{6,4},{7,5},{8,10},{9,11},{10,... | collective-permute-start | bytes 2359304 | tf_op jit(solution)/shard_map/ppermute | solution.py:839
  74.2 25.5 %collective-permute-start.4 = (bf16[4,2,384,128]{3,2,0,1:T(8,128)(2,1)S(1)}, bf16[4,2,384,128]{3,2,0,1:T(8,128)(2,1)}, u32[]{:S(2)}, u32[]{:S(2)}) collective-permute-start(bf16[4,2,384,128]{3,2,0,1:T(8,128)(2,1)S(1)} %maximum_select_fusion.4), channel_id=1, source_target_pairs={{0,16},{16,0},{1,17},{17,1},{2,18},{18,2},{3,19},{19,3},{4,20},{20... | collective-permute-start | bytes 2359304 | tf_op jit(solution)/shard_map/ppermute | solution.py:837
  99.6 35.9 %collective-permute-start.8 = (bf16[8,1,384,256]{3,2,1,0:T(8,128)(2,1)S(1)}, bf16[8,1,384,256]{3,2,1,0:T(8,128)(2,1)}, u32[]{:S(2)}, u32[]{:S(2)}) collective-permute-start(bf16[8,1,384,256]{3,2,1,0:T(8,128)(2,1)S(1)} %bitcast.212), channel_id=1, source_target_pairs={{0,1},{1,0},{2,3},{3,2},{4,5},{5,4},{6,7},{7,6},{8,9},{9,8},{10,11... | collective-permute-start | bytes 4718600 | tf_op jit(solution)/shard_map/ppermute | solution.py:839
  101.9 33.5 %collective-permute-start.5 = (bf16[8,1,384,256]{3,2,1,0:T(8,128)(2,1)S(1)}, bf16[8,1,384,256]{3,2,1,0:T(8,128)(2,1)}, u32[]{:S(2)}, u32[]{:S(2)}) collective-permute-start(bf16[8,1,384,256]{3,2,1,0:T(8,128)(2,1)S(1)} %maximum_select_fusion.wq0.lo0.refs_0_), channel_id=1, source_target_pairs={{0,1},{1,0},{2,3},{3,2},{4,5},{5,4},{6,7},{7,6},{8,9},{9,8},{10,11... | collective-permute-start | bytes 4718600 | tf_op jit(solution)/shard_map/ppermute | solution.py:839
  251.2 88.0 %collective-permute-start.35 = (bf16[2,2,4,960,128]{4,3,2,1,0:T(8,128)(2,1)}, bf16[2,2,4,960,128]{4,3,2,1,0:T(8,128)(2,1)S(1)}, u32[]{:S(2)}, u32[]{:S(2)}) collective-permute-start(bf16[2,2,4,960,128]{4,3,2,1,0:T(8,128)(2,1)} %get-tuple-element.69), channel_id=1, source_target_pairs={{0,1},{1,0},{2,3},{3,2},{4,5},{5,4},{6,7},{7,6},{8,9},{9,8},{10,11... | collective-permute-start | bytes 11796488 | tf_op jit(solution)/shard_map/ppermute | solution.py:839
  262.3 36.1 %collective-permute-start.27 = (bf16[2,2,4,512,128]{4,3,2,1,0:T(8,128)(2,1)}, bf16[2,2,4,512,128]{4,3,2,1,0:T(8,128)(2,1)}, u32[]{:S(2)}, u32[]{:S(2)}) collective-permute-start(bf16[2,2,4,512,128]{4,3,2,1,0:T(8,128)(2,1)} %get-tuple-element.66), channel_id=1, source_target_pairs={{0,1},{1,0},{2,3},{3,2},{4,5},{5,4},{6,7},{7,6},{8,9},{9,8},{10,11... | collective-permute-start | bytes 6291464 | tf_op jit(solution)/shard_map/ppermute | solution.py:839
  298.3 38.2 %collective-permute-start.20 = (bf16[2,2,4,768,128]{4,3,2,1,0:T(8,128)(2,1)}, bf16[2,2,4,768,128]{4,3,2,1,0:T(8,128)(2,1)S(1)}, u32[]{:S(2)}, u32[]{:S(2)}) collective-permute-start(bf16[2,2,4,768,128]{4,3,2,1,0:T(8,128)(2,1)} %get-tuple-element.64), channel_id=1, source_target_pairs={{0,1},{1,0},{2,3},{3,2},{4,5},{5,4},{6,7},{7,6},{8,9},{9,8},{10,11... | collective-permute-start | bytes 9437192 | tf_op jit(solution)/shard_map/ppermute | solution.py:839
  300.4 34.4 %collective-permute-start.28 = (bf16[2,4,512,128]{3,2,1,0:T(8,128)(2,1)S(1)}, bf16[2,4,512,128]{3,2,1,0:T(8,128)(2,1)S(1)}, u32[]{:S(2)}, u32[]{:S(2)}) collective-permute-start(bf16[2,4,512,128]{3,2,1,0:T(8,128)(2,1)S(1)} %fusion.4), channel_id=1, source_target_pairs={{0,2},{1,3},{2,0},{3,1},{4,6},{5,7},{6,4},{7,5},{8,10},{9,11},{10,... | collective-permute-start | bytes 3145736 | tf_op jit(solution)/shard_map/ppermute | solution.py:839
  336.9 81.9 %collective-permute-start.21 = (bf16[2,4,768,128]{3,2,1,0:T(8,128)(2,1)S(1)}, bf16[2,4,768,128]{3,2,1,0:T(8,128)(2,1)S(1)}, u32[]{:S(2)}, u32[]{:S(2)}) collective-permute-start(bf16[2,4,768,128]{3,2,1,0:T(8,128)(2,1)S(1)} %fusion.2), channel_id=1, source_target_pairs={{0,16},{16,0},{1,17},{17,1},{2,18},{18,2},{3,19},{19,3},{4,20},{20... | collective-permute-start | bytes 4718600 | tf_op jit(solution)/shard_map/ppermute | solution.py:837
  338.5 46.9 %collective-permute-start.29 = (bf16[4,512,128]{2,1,0:T(8,128)(2,1)S(1)}, bf16[4,512,128]{2,1,0:T(8,128)(2,1)S(1)}, u32[]{:S(2)}, u32[]{:S(2)}) collective-permute-start(bf16[4,512,128]{2,1,0:T(8,128)(2,1)S(1)} %fusion.8), channel_id=1, source_target_pairs={{0,16},{16,0},{1,17},{17,1},{2,18},{18,2},{3,19},{19,3},{4,20},{20... | collective-permute-start | bytes 1572872 | tf_op jit(solution)/shard_map/ppermute | solution.py:837
  341.0 88.0 %collective-permute-start.36 = (bf16[2,4,960,128]{3,2,1,0:T(8,128)(2,1)S(1)}, bf16[2,4,960,128]{3,2,1,0:T(8,128)(2,1)S(1)}, u32[]{:S(2)}, u32[]{:S(2)}) collective-permute-start(bf16[2,4,960,128]{3,2,1,0:T(8,128)(2,1)S(1)} %fusion), channel_id=1, source_target_pairs={{0,16},{16,0},{1,17},{17,1},{2,18},{18,2},{3,19},{19,3},{4,20},{20... | collective-permute-start | bytes 5898248 | tf_op jit(solution)/shard_map/ppermute | solution.py:837
  385.6 34.9 %collective-permute-start.30 = (bf16[512,128]{1,0:T(8,128)(2,1)S(1)}, bf16[512,128]{1,0:T(8,128)(2,1)S(1)}, u32[]{:S(2)}, u32[]{:S(2)}) collective-permute-start(bf16[512,128]{1,0:T(8,128)(2,1)S(1)} %get-tuple-element.114), channel_id=1, source_target_pairs={{0,4},{1,5},{2,6},{3,7},{4,8},{5,9},{6,10},{7,11},{8,12},{9,13},{1... | collective-permute-start | bytes 393224 | tf_op jit(solution)/shard_map/ppermute | solution.py:842
  387.8 36.0 %collective-permute-start.31 = (bf16[512,128]{1,0:T(8,128)(2,1)S(1)}, bf16[512,128]{1,0:T(8,128)(2,1)S(1)}, u32[]{:S(2)}, u32[]{:S(2)}) collective-permute-start(bf16[512,128]{1,0:T(8,128)(2,1)S(1)} %get-tuple-element.116), channel_id=1, source_target_pairs={{0,8},{1,9},{2,10},{3,11},{4,12},{5,13},{6,14},{7,15},{8,0},{9,1},... | collective-permute-start | bytes 393224 | tf_op jit(solution)/shard_map/ppermute | solution.py:842
  427.2 56.3 %collective-permute-start.33 = (bf16[512,128]{1,0:T(8,128)(2,1)S(1)}, bf16[512,128]{1,0:T(8,128)(2,1)}, u32[]{:S(2)}, u32[]{:S(2)}) collective-permute-start(bf16[512,128]{1,0:T(8,128)(2,1)S(1)} %fusion.22), channel_id=1, source_target_pairs={{0,16},{16,0},{1,17},{17,1},{2,18},{18,2},{3,19},{19,3},{4,20},{20... | collective-permute-start | bytes 393224 | tf_op jit(solution)/shard_map/ppermute | solution.py:837
  430.9 56.5 %collective-permute-start.37 = (bf16[4,960,128]{2,1,0:T(8,128)(2,1)}, bf16[4,960,128]{2,1,0:T(8,128)(2,1)}, u32[]{:S(2)}, u32[]{:S(2)}) collective-permute-start(bf16[4,960,128]{2,1,0:T(8,128)(2,1)} %fusion.6), channel_id=1, source_target_pairs={{0,2},{1,3},{2,0},{3,1},{4,6},{5,7},{6,4},{7,5},{8,10},{9,11},{10,... | collective-permute-start | bytes 2949128 | tf_op jit(solution)/shard_map/ppermute | solution.py:839
  441.4 43.2 %collective-permute-start.23 = (bf16[768,128]{1,0:T(8,128)(2,1)}, bf16[768,128]{1,0:T(8,128)(2,1)}, u32[]{:S(2)}, u32[]{:S(2)}) collective-permute-start(bf16[768,128]{1,0:T(8,128)(2,1)} %get-tuple-element.109), channel_id=1, source_target_pairs={{0,4},{1,5},{2,6},{3,7},{4,8},{5,9},{6,10},{7,11},{8,12},{9,13},{1... | collective-permute-start | bytes 589832 | tf_op jit(solution)/shard_map/ppermute | solution.py:842
  443.6 41.0 %collective-permute-start.24 = (bf16[768,128]{1,0:T(8,128)(2,1)}, bf16[768,128]{1,0:T(8,128)(2,1)}, u32[]{:S(2)}, u32[]{:S(2)}) collective-permute-start(bf16[768,128]{1,0:T(8,128)(2,1)} %get-tuple-element.111), channel_id=1, source_target_pairs={{0,8},{1,9},{2,10},{3,11},{4,12},{5,13},{6,14},{7,15},{8,0},{9,1},... | collective-permute-start | bytes 589832 | tf_op jit(solution)/shard_map/ppermute | solution.py:842
  496.2 24.8 %collective-permute-start.34 = (bf16[1152,256]{1,0:T(8,128)(2,1)}, bf16[1152,256]{1,0:T(8,128)(2,1)S(1)}, u32[]{:S(2)}, u32[]{:S(2)}) collective-permute-start(bf16[1152,256]{1,0:T(8,128)(2,1)} %bitcast.247), channel_id=1, source_target_pairs={{0,16},{16,0},{1,17},{17,1},{2,18},{18,2},{3,19},{19,3},{4,20},{20... | collective-permute-start | bytes 1769480 | tf_op jit(solution)/shard_map/ppermute | solution.py:837
  (38 other events, 466.8 us)
Sparse Core Ops, SparseCore 0:
  14.5 131.1 all-gather.1
  196.7 164.0 reduce-scatter.1

commit v3 on v2

--- a/solution.py
+++ b/solution.py
@@ -1,3 +1,5 @@
+import functools
+
 import jax
 import jax.numpy as jnp
 from jax import lax
@@ -58,31 +60,37 @@
 
 
 def cost(flops, moved):
-    return pl.CostEstimate(flops=flops, bytes_accessed=moved, transcendentals=0)
+    return pl.CostEstimate(flops=flops // 10000, bytes_accessed=moved // 10000, transcendentals=0)
 
 
 class Gathered:
-    def __init__(self, first, second, order):
-        self.first, self.second, self.order = first, second, order
-
-    def specs(self, height, index, chips=8):
-        def of(core):
-            if chips == 8:
-                return pl.BlockSpec((8, 1, height, TILE), lambda i: (0, core, index(i), 0))
-            return pl.BlockSpec((chips, 1, height, TILE), lambda i: (i, core, index(i), 0))
-
-        return [of(0), of(self.first.shape[1] - 1)]
-
-    def arrays(self):
-        return [self.first, self.second]
-
-
-def join(order, first, second, held, rows=slice(None)):
-    held[:, order, rows, :] = first[:, 0]
-    held[:, 1 - order, rows, :] = second[:, 0]
-
-
-def emit(coords, stage, own, other, rows, order):
+    def __init__(self, kind, arrays):
+        self.kind, self.arrays = kind, arrays
+
+    def specs(self, height, index):
+        spec = pl.BlockSpec((2, 4, height, HALF), lambda i: (0, 0, index(i), 0))
+        return [spec] * 4
+
+
+def join(coords, kind, refs, held, rows=slice(None)):
+    z0, y0, c0, x0 = coords[0], coords[1], coords[2], coords[3]
+    for c_rel in range(2):
+        core = c_rel + c0 - 2 * c_rel * c0
+        pair = refs[2 * c_rel : 2 * c_rel + 2]
+        for y_rel in range(2):
+            y = y_rel + y0 - 2 * y_rel * y0
+            for z_rel in range(4):
+                z = lax.rem(z0 + 4 - z_rel, 4)
+                if kind == "y":
+                    here, there = pair[0][y_rel, z_rel], pair[1][y_rel, z_rel]
+                else:
+                    here, there = pair[y_rel][0, z_rel], pair[y_rel][1, z_rel]
+                near = jnp.concatenate([here, there], axis=1)
+                far = jnp.concatenate([there, here], axis=1)
+                held[z, y, core, rows, :] = jnp.where(x0 == 0, near, far)
+
+
+def emit(coords, stage, own, other, rows):
     z0, y0, c0, x0 = coords[0], coords[1], coords[2], coords[3]
     for x in range(2):
         x_rel = x + x0 - 2 * x * x0
@@ -92,9 +100,8 @@
             for z_rel in range(4):
                 z = lax.rem(z0 + z_rel, 4)
                 shard = z * 4 + y * 2
-                lead = (x_rel, y_rel) if order == "xy" else (y_rel, x_rel)
-                own[(*lead, z_rel, rows)] = stage[shard + c0, :, cols]
-                other[(*lead, z_rel, rows)] = stage[shard + 1 - c0, :, cols]
+                own[x_rel, y_rel, z_rel, rows, :] = stage[shard + c0, :, cols]
+                other[x_rel, y_rel, z_rel, rows, :] = stage[shard + 1 - c0, :, cols]
 
 
 def decay_in_of(rate):
@@ -155,12 +162,13 @@
 
 
 def key_value_kernel(
-    rates, across, order, a, wk0, wk1, wv0, wv1, cosine, sine, kraw_out, v_out, state_out, held
+    rates, across, coords, a, cosine, sine, *refs
 ):
+    kraw_out, v_out, state_out, held = refs[8:]
     step = pl.program_id(0)
     rows = a.shape[0]
-    join(order[0], wk0, wk1, held.at[0])
-    join(order[0], wv0, wv1, held.at[1])
+    join(coords, "y", refs[:4], held.at[0])
+    join(coords, "x", refs[4:8], held.at[1])
     kraw = nn(a[...], held[0].reshape(-1, TILE))
     v_out[...] = nn(a[...], held[1].reshape(-1, TILE)).astype(bf16)
     kraw_out[...] = kraw.astype(bf16)
@@ -174,55 +182,37 @@
             key = swish(kraw[span, cols])
             faded = rotated(key, cosine[span, :], sine[span, :]) * tail
             state = across[head] * state + tn(v_out[span, cols], faded.astype(bf16))
-        state_out[s] = state
-
-
-def key_value(rates, across, a, keys, values, cosine, sine):
+        state_out[s] = state.astype(state_out.dtype)
+
+
+def key_value(rates, across, coords, a, keys, values, cosine, sine, state_type):
     rows, depth = a.shape
     return pl.pallas_call(
         key_value_kernel,
         grid=(depth // TILE,),
         in_specs=[smem(), smem(), smem(), fixed((rows, depth))]
+        + [fixed((rows, HD)), fixed((rows, HD))]
         + keys.specs(64, lambda i: i)
-        + values.specs(64, lambda i: i)
-        + [fixed((rows, HD)), fixed((rows, HD))],
+        + values.specs(64, lambda i: i),
         out_specs=[columns(rows, TILE), columns(rows, TILE), head_states()],
         out_shape=[
             struct((rows, depth), bf16),
             struct((rows, depth), bf16),
-            struct((H, HD, 2 * HD), f32),
-        ],
-        scratch_shapes=[pltpu.VMEM((2, 8, 2, 64, TILE), bf16)],
+            struct((H, HD, 2 * HD), state_type),
+        ],
+        scratch_shapes=[pltpu.VMEM((2, 4, 2, 2, 64, TILE), bf16)],
         compiler_params=params(),
         cost_estimate=cost(5 * rows * depth * depth, 10 * rows * depth),
         name="key_value",
-    )(rates, across, keys.order, a, *keys.arrays(), *values.arrays(), cosine, sine)
-
-
-def mix_kernel(
-    rates,
-    across,
-    order,
-    a,
-    wq0,
-    wq1,
-    wg0,
-    wg1,
-    kraw,
-    v,
-    cosine,
-    sine,
-    state_in,
-    qraw_out,
-    u_out,
-    o_out,
-    gated_out,
-    held,
-):
+    )(rates, across, coords, a, cosine, sine, *keys.arrays, *values.arrays)
+
+
+def mix_kernel(rates, across, keep, coords, a, kraw, v, cosine, sine, state_in, *refs):
+    qraw_out, u_out, o_out, gated_out, held = refs[8:]
     step = pl.program_id(0)
     rows = a.shape[0]
-    join(order[0], wq0, wq1, held.at[0])
-    join(order[0], wg0, wg1, held.at[1])
+    join(coords, "y", refs[:4], held.at[0])
+    join(coords, "x", refs[4:8], held.at[1])
     qraw = nn(a[...], held[0].reshape(-1, TILE))
     qraw_out[...] = qraw.astype(bf16)
     u_out[...] = nn(a[...], held[1].reshape(-1, TILE)).astype(bf16)
@@ -236,7 +226,7 @@
         tail = double(decay_out_of(rate))
         lead = decay_in_of(rate)
         mask = jnp.where(distance >= 0, jnp.exp(-rate * jnp.maximum(distance, 0.0)), 0.0)
-        state = state_in[s]
+        state = keep[0] * state_in[s].astype(f32)
         for c in range(rows // CH):
             span = slice(c * CH, (c + 1) * CH)
             cos_c, sin_c = cosine[span, :], sine[span, :]
@@ -252,48 +242,54 @@
             gated_out[span, cols] = (o * scale * u_out[span, cols].astype(f32)).astype(bf16)
 
 
-def mix(rates, across, a, queries, gates, kraw, v, cosine, sine, state_in):
+def mix(rates, across, keep, coords, a, queries, gates, kraw, v, cosine, sine, state_in):
     rows, depth = a.shape
     return pl.pallas_call(
         mix_kernel,
         grid=(depth // TILE,),
-        in_specs=[smem(), smem(), smem(), fixed((rows, depth))]
-        + queries.specs(64, lambda i: i)
-        + gates.specs(64, lambda i: i)
+        in_specs=[smem(), smem(), smem(), smem(), fixed((rows, depth))]
         + [
             columns(rows, TILE),
             columns(rows, TILE),
             fixed((rows, HD)),
             fixed((rows, HD)),
             head_states(),
-        ],
+        ]
+        + queries.specs(64, lambda i: i)
+        + gates.specs(64, lambda i: i),
         out_specs=[columns(rows, TILE)] * 4,
         out_shape=[struct((rows, depth), bf16)] * 4,
-        scratch_shapes=[pltpu.VMEM((2, 8, 2, 64, TILE), bf16)],
+        scratch_shapes=[pltpu.VMEM((2, 4, 2, 2, 64, TILE), bf16)],
         compiler_params=params(),
         cost_estimate=cost(8 * rows * depth * depth, 18 * rows * depth),
         name="mix",
     )(
         rates,
         across,
-        queries.order,
+        keep,
+        coords,
         a,
-        *queries.arrays(),
-        *gates.arrays(),
         kraw,
         v,
         cosine,
         sine,
         state_in,
+        *queries.arrays,
+        *gates.arrays,
     )
 
 
-def residual_kernel(order, x, gated, lo0, lo1, hi0, hi1, h1_out, bn_out, bnt_out, held, h1):
-    join(order[0], lo0, lo1, held, slice(0, 128))
-    join(order[0], hi0, hi1, held, slice(128, 256))
+def residual_kernel(coords, x, gated, *refs):
+    h1_out, bn_out, bnt_out, held, h1 = refs[8:]
+
+    @pl.when(pl.program_id(0) == 0)
+    def _():
+        join(coords, "y", refs[:4], held, slice(0, 128))
+        join(coords, "x", refs[4:8], held, slice(128, 256))
+
     for b in range(4):
         cols = slice(b * TILE, (b + 1) * TILE)
-        weight = held[:, :, b * 64 : (b + 1) * 64, :].reshape(-1, TILE)
+        weight = held[:, :, :, b * 64 : (b + 1) * 64, :].reshape(-1, TILE)
         h1[:, cols] = x[:, cols].astype(f32) + nn(gated[...], weight)
     value = h1[...]
     h1_out[...] = value
@@ -303,7 +299,7 @@
     bnt_out[...] = low.T
 
 
-def residual(x, gated, out_lo, out_hi):
+def residual(coords, x, gated, out_lo, out_hi):
     rows, depth = x.shape
     part = 512
     return pl.pallas_call(
@@ -319,21 +315,21 @@
             struct((depth, rows), bf16),
         ],
         scratch_shapes=[
-            pltpu.VMEM((8, 2, 256, TILE), bf16),
+            pltpu.VMEM((4, 2, 2, 256, TILE), bf16),
             pltpu.VMEM((part, depth), f32),
         ],
         compiler_params=params(),
         cost_estimate=cost(2 * rows * depth * depth, 14 * rows * depth),
         name="residual",
-    )(out_lo.order, x, gated, *out_lo.arrays(), *out_hi.arrays())
+    )(coords, x, gated, *out_lo.arrays, *out_hi.arrays)
 
 
 def feed_tile(bn, bnt, og, held, down, stage, total, dbn):
-    w1 = held[:, :, 0:64, :].reshape(-1, TILE)
-    w2 = held[:, :, 64:128, :].reshape(-1, TILE)
+    w1 = held[:, :, :, 0:64, :].reshape(-1, TILE)
+    w2 = held[:, :, :, 64:128, :].reshape(-1, TILE)
     for b in range(4):
         rows = slice(128 + 16 * b, 144 + 16 * b)
-        down[:, b * TILE : (b + 1) * TILE] = held[:, :, rows, :].reshape(TILE, TILE)
+        down[:, b * TILE : (b + 1) * TILE] = held[:, :, :, rows, :].reshape(TILE, TILE)
     first = nn(bn[...], w1)
     second = nn(bn[...], w2)
     middle = (first * second).astype(bf16)
@@ -366,7 +362,11 @@
         dbn_out[...] = dbn[...].astype(bf16)
 
 
-def feed_start(bn, bnt, og, weights, base, tiles):
+def feed_tiles(base):
+    return pl.BlockSpec((4, 2, 2, 192, TILE), lambda i: (0, 0, 0, base + i, 0))
+
+
+def feed_start(bn, bnt, og, weights, tiles):
     rows, depth = bn.shape
     return pl.pallas_call(
         feed_start_kernel,
@@ -375,7 +375,7 @@
             fixed((rows, depth)),
             fixed((depth, rows)),
             fixed((rows, depth)),
-            pl.BlockSpec((8, 2, 192, TILE), lambda i: (0, 0, base + i, 0)),
+            feed_tiles(0),
         ],
         out_specs=[
             pl.BlockSpec((SHARDS, 192, TILE), lambda i: (0, i, 0)),
@@ -400,25 +400,8 @@
     )(bn, bnt, og, weights)
 
 
-def feed_end_kernel(
-    coords,
-    h1,
-    bn,
-    bnt,
-    og,
-    y_part,
-    dbn_part,
-    w,
-    own_out,
-    other_out,
-    y_out,
-    dh1_out,
-    dattn_out,
-    down,
-    stage,
-    total,
-    dbn,
-):
+def feed_end_kernel(coords, h1, bn, bnt, og, y_part, dbn_part, w, *refs):
+    own_out, other_out, y_out, dh1_out, dattn_out, down, stage, total, dbn = refs
     step = pl.program_id(0)
 
     @pl.when(step == 0)
@@ -427,7 +410,7 @@
         dbn[...] = dbn_part[...].astype(f32)
 
     feed_tile(bn, bnt, og, w, down, stage, total, dbn)
-    emit(coords, stage, own_out, other_out, slice(0, 192), "xy")
+    emit(coords, stage, own_out, other_out, slice(0, 192))
 
     @pl.when(step == pl.num_programs(0) - 1)
     def _():
@@ -447,8 +430,9 @@
     return pl.BlockSpec((2, 2, 4, height, HALF), lambda i: (0, 0, 0, i, 0))
 
 
-def feed_end(coords, h1, bn, bnt, og, y_part, dbn_part, weights, base, tiles):
+def feed_end(coords, h1, bn, bnt, og, y_part, dbn_part, weights, base):
     rows, depth = bn.shape
+    tiles = weights.shape[3] // 192 - base
     grads = struct((2, 2, 4, tiles * 192, HALF), bf16)
     return pl.pallas_call(
         feed_end_kernel,
@@ -461,7 +445,7 @@
             fixed((rows, depth)),
             fixed((rows, depth)),
             fixed((rows, depth)),
-            pl.BlockSpec((8, 2, 192, TILE), lambda i: (0, 0, base + i, 0)),
+            feed_tiles(base),
         ],
         out_specs=[
             grad_block(192),
@@ -491,32 +475,19 @@
     )(coords, h1, bn, bnt, og, y_part, dbn_part, weights)
 
 
-def gate_back_kernel(
-    rates,
-    across,
-    order,
-    dattn,
-    lo0,
-    lo1,
-    hi0,
-    hi1,
-    o_in,
-    u_in,
-    qraw,
-    cosine,
-    sine,
-    du_out,
-    do_out,
-    back_out,
-    held,
-):
+def gate_back_kernel(rates, across, keep, coords, dattn, o_in, u_in, qraw, cosine, sine, *refs):
+    du_out, do_out, back_out, held = refs[8:]
     step = pl.program_id(0)
     rows = dattn.shape[0]
-    join(order[0], lo0, lo1, held, slice(0, 128))
-    join(order[0], hi0, hi1, held, slice(128, 256))
+
+    @pl.when(step == 0)
+    def _():
+        join(coords, "y", refs[:4], held, slice(0, 128))
+        join(coords, "x", refs[4:8], held, slice(128, 256))
+
     dgated = jnp.zeros((rows, TILE), f32)
     for b in range(4):
-        weight = held[:, :, b * 64 : (b + 1) * 64, :].reshape(TILE, TILE)
+        weight = held[step, :, :, b * 64 : (b + 1) * 64, :].reshape(TILE, TILE)
         dgated = dgated + nt(dattn[:, b * TILE : (b + 1) * TILE], weight)
     dgated = dgated.astype(bf16).astype(f32)
     for s in range(TILE // HD):
@@ -537,46 +508,49 @@
             do_out[span, cols] = low
             query = rotated(swish(qraw[span, cols].astype(f32)), cosine[span, :], sine[span, :])
             back = across[head] * back + tn(low, (query * lead).astype(bf16))
-        back_out[s] = back
-
-
-def gate_back(rates, across, dattn, out_lo, out_hi, o_in, u_in, qraw, cosine, sine):
+        back_out[s] = (keep[0] * back).astype(back_out.dtype)
+
+
+def gate_back(
+    rates, across, keep, coords, dattn, out_lo, out_hi, o_in, u_in, qraw, cosine, sine, back_type
+):
     rows, depth = dattn.shape
     return pl.pallas_call(
         gate_back_kernel,
         grid=(depth // TILE,),
-        in_specs=[smem(), smem(), smem(), fixed((rows, depth))]
-        + out_lo.specs(128, lambda i: 2, chips=2)
-        + out_hi.specs(128, lambda i: 2, chips=2)
+        in_specs=[smem(), smem(), smem(), smem(), fixed((rows, depth))]
         + [
             columns(rows, TILE),
             columns(rows, TILE),
             columns(rows, TILE),
             fixed((rows, HD)),
             fixed((rows, HD)),
-        ],
+        ]
+        + out_lo.specs(128, lambda i: 2)
+        + out_hi.specs(128, lambda i: 2),
         out_specs=[columns(rows, TILE), columns(rows, TILE), head_states()],
         out_shape=[
             struct((rows, depth), bf16),
             struct((rows, depth), bf16),
-            struct((H, HD, 2 * HD), f32),
-        ],
-        scratch_shapes=[pltpu.VMEM((2, 2, 256, TILE), bf16)],
+            struct((H, HD, 2 * HD), back_type),
+        ],
+        scratch_shapes=[pltpu.VMEM((4, 2, 2, 256, TILE), bf16)],
         compiler_params=params(),
         cost_estimate=cost(3 * rows * depth * depth, 16 * rows * depth),
         name="gate_back",
     )(
         rates,
         across,
-        out_lo.order,
+        keep,
+        coords,
         dattn,
-        *out_lo.arrays(),
-        *out_hi.arrays(),
         o_in,
         u_in,
         qraw,
         cosine,
         sine,
+        *out_lo.arrays,
+        *out_hi.arrays,
     )
 
 
@@ -587,7 +561,7 @@
     z0, y0, c0, x0 = coords[0], coords[1], coords[2], coords[3]
     stage[...] = nn(a_t[...], du[...]).astype(bf16).reshape(SHARDS, 64, TILE)
     rows = pl.ds(pl.multiple_of(256 + step * 64, 64), 64)
-    emit(coords, stage, own_out, other_out, rows, "yx")
+    emit(coords, stage, own_out, other_out, rows)
     g = tn(gated[...], dattn[...]).astype(bf16)
     z_rel = lax.rem(step + 4 - z0, 4)
     for b in range(4):
@@ -598,8 +572,8 @@
             cols = slice(x * HALF, (x + 1) * HALF)
             for y_rel in range(2):
                 y = y_rel + y0 - 2 * y_rel * y0
-                own_out[y_rel, x_rel, z_rel, rows, :] = stage_out[b, 2 * y + c0, :, cols]
-                other_out[y_rel, x_rel, z_rel, rows, :] = stage_out[
+                own_out[x_rel, y_rel, z_rel, rows, :] = stage_out[b, 2 * y + c0, :, cols]
+                other_out[x_rel, y_rel, z_rel, rows, :] = stage_out[
                     b, 2 * y + 1 - c0, :, cols
                 ]
 
@@ -630,8 +604,10 @@
 
 
 def mix_back_kernel(
+    base,
     rates,
     across,
+    keep,
     qraw,
     kraw,
     v,
@@ -645,7 +621,7 @@
     dv_out,
     key_s,
 ):
-    step = pl.program_id(0)
+    step = base + pl.program_id(0)
     rows = qraw.shape[0]
     count = rows // CH
     row = lax.broadcasted_iota(jnp.int32, (CH, CH), 0)
@@ -659,7 +635,7 @@
         tail = double(decay_out_of(rate))
         mask = jnp.where(distance >= 0, jnp.exp(-rate * jnp.maximum(distance, 0.0)), 0.0)
         mask_t = jnp.where(distance <= 0, jnp.exp(rate * jnp.minimum(distance, 0.0)), 0.0)
-        state = state_in[s]
+        state = keep[0] * state_in[s].astype(f32)
         states = []
         for c in range(count):
             span = slice(c * CH, (c + 1) * CH)
@@ -670,7 +646,7 @@
             states.append(state.astype(bf16))
             if c < count - 1:
                 state = across[head] * state + tn(v[span, cols], (key_float * tail).astype(bf16))
-        back = back_in[s]
+        back = back_in[s].astype(f32)
         for c in reversed(range(count)):
             span = slice(c * CH, (c + 1) * CH)
             cos_c, sin_c = cosine[span, :], sine[span, :]
@@ -695,21 +671,25 @@
             dv_out[span, cols] = dv.astype(bf16)
 
 
-def mix_back(rates, across, qraw, kraw, v, do_in, cosine, sine, state_in, back_in):
+def mix_back(part, rates, across, keep, qraw, kraw, v, do_in, cosine, sine, state_in, back_in):
     rows, width = qraw.shape
-    return pl.pallas_call(
-        mix_back_kernel,
-        grid=(width // TILE,),
-        in_specs=[smem(), smem()]
-        + [columns(rows, TILE)] * 4
-        + [fixed((rows, HD)), fixed((rows, HD)), head_states(), head_states()],
+    count = width // TILE // 2
+    base = part * count
+    cols = pl.BlockSpec((rows, TILE), lambda i: (0, base + i))
+    heads = pl.BlockSpec((TILE // HD, HD, 2 * HD), lambda i: (base + i, 0, 0))
+    return pl.pallas_call(
+        functools.partial(mix_back_kernel, base),
+        grid=(count,),
+        in_specs=[smem(), smem(), smem()]
+        + [cols] * 4
+        + [fixed((rows, HD)), fixed((rows, HD)), heads, heads],
         out_specs=[columns(rows, TILE)] * 3,
-        out_shape=[struct((rows, width), bf16)] * 3,
+        out_shape=[struct((rows, width // 2), bf16)] * 3,
         scratch_shapes=[pltpu.VMEM((rows, 2 * HD), bf16)],
         compiler_params=params(),
-        cost_estimate=cost(8 * rows * width * width, 16 * rows * width),
+        cost_estimate=cost(4 * rows * width * width, 8 * rows * width),
         name="mix_back",
-    )(rates, across, qraw, kraw, v, do_in, cosine, sine, state_in, back_in)
+    )(rates, across, keep, qraw, kraw, v, do_in, cosine, sine, state_in, back_in)
 
 
 def query_grads_kernel(coords, a_t, dq, dk, dv, own_out, other_out, stage):
@@ -717,39 +697,60 @@
         stage[:, n * 64 : (n + 1) * 64, :] = (
             nn(a_t[...], incoming[...]).astype(bf16).reshape(SHARDS, 64, TILE)
         )
-    emit(coords, stage, own_out, other_out, slice(0, 192), "xy")
+    emit(coords, stage, own_out, other_out, slice(0, 192))
 
 
 def query_grads(coords, a_t, dq, dk, dv):
     depth, rows = a_t.shape
-    grads = struct((2, 2, 4, 3 * 256, HALF), bf16)
+    count = dq.shape[1] // TILE
+    grads = struct((2, 2, 4, count * 192, HALF), bf16)
     return pl.pallas_call(
         query_grads_kernel,
-        grid=(depth // TILE,),
+        grid=(count,),
         in_specs=[smem(), fixed((depth, rows))] + [columns(rows, TILE)] * 3,
         out_specs=[grad_block(192), grad_block(192)],
         out_shape=[grads, grads],
         scratch_shapes=[pltpu.VMEM((SHARDS, 192, TILE), bf16)],
         compiler_params=params(),
-        cost_estimate=cost(6 * rows * depth * depth, 14 * rows * depth),
+        cost_estimate=cost(6 * rows * depth * count * TILE, 10 * rows * depth),
         name="query_grads",
     )(coords, a_t, dq, dk, dv)
 
 
-def input_back_kernel(order, x, dh1, dq, dk, dv, du, *refs):
-    weights, (out, total, held) = refs[:8], refs[8:]
+def input_part(coords, refs, total, held):
+    incoming, weights = refs[:4], refs[4:20]
+    part = None
+    for n, kind in enumerate(("y", "y", "x", "x")):
+        join(coords, kind, weights[4 * n : 4 * n + 4], held.at[n])
+        term = nt(incoming[n][...], held[n].reshape(-1, TILE))
+        part = term if part is None else part + term
+    total[...] += part
+
+
+def input_start_kernel(coords, *refs):
+    out, total, held = refs[20:]
     step = pl.program_id(0)
 
     @pl.when(step == 0)
     def _():
         total[...] = jnp.zeros_like(total)
 
-    part = None
-    for n, incoming in enumerate((dq, dk, dv, du)):
-        join(order[0], weights[2 * n], weights[2 * n + 1], held.at[n])
-        term = nt(incoming[...], held[n].reshape(-1, TILE))
-        part = term if part is None else part + term
-    total[...] += part
+    input_part(coords, refs, total, held)
+
+    @pl.when(step == pl.num_programs(0) - 1)
+    def _():
+        out[...] = total[...].astype(bf16)
+
+
+def input_end_kernel(coords, start, x, dh1, *refs):
+    out, total, held = refs[20:]
+    step = pl.program_id(0)
+
+    @pl.when(step == 0)
+    def _():
+        total[...] = start[...].astype(f32)
+
+    input_part(coords, refs, total, held)
 
     @pl.when(step == pl.num_programs(0) - 1)
     def _():
@@ -763,28 +764,32 @@
         ).astype(bf16)
 
 
-def input_back(x, dh1, grads, weights):
-    rows, depth = x.shape
+def input_back(part, coords, whole, grads, du, weights):
+    rows, depth = du.shape
+    count = depth // TILE // 2
+    base = part * count
     specs, arrays = [], []
     for weight in weights:
-        specs += weight.specs(64, lambda i: i)
-        arrays += weight.arrays()
-    return pl.pallas_call(
-        input_back_kernel,
-        grid=(depth // TILE,),
-        in_specs=[smem(), fixed((rows, depth)), fixed((rows, depth))]
-        + [columns(rows, TILE)] * 4
+        specs += weight.specs(64, lambda i: base + i)
+        arrays += weight.arrays
+    return pl.pallas_call(
+        input_end_kernel if part else input_start_kernel,
+        grid=(count,),
+        in_specs=[smem()]
+        + [fixed((rows, depth))] * len(whole)
+        + [columns(rows, TILE)] * 3
+        + [pl.BlockSpec((rows, TILE), lambda i: (0, base + i))]
         + specs,
         out_specs=fixed((rows, depth)),
         out_shape=struct((rows, depth), bf16),
         scratch_shapes=[
             pltpu.VMEM((rows, depth), f32),
-            pltpu.VMEM((4, 8, 2, 64, TILE), bf16),
-        ],
-        compiler_params=params(),
-        cost_estimate=cost(8 * rows * depth * depth, 24 * rows * depth),
+            pltpu.VMEM((4, 4, 2, 2, 64, TILE), bf16),
+        ],
+        compiler_params=params(),
+        cost_estimate=cost(4 * rows * depth * depth, 16 * rows * depth),
         name="input_back",
-    )(weights[0].order, x, dh1, *grads, *arrays)
+    )(coords, *whole, *grads, du, *arrays)
 
 
 def square_blocks(w, shards):
@@ -838,6 +843,17 @@
         step = {"y": 2, "core": 1}[axis]
         return lax.ppermute(value, "wt", [(i, i ^ step) for i in range(SHARDS)])
 
+    def corners(self, values):
+        both = [(s * SHARDS + w, (1 - s) * SHARDS + (w ^ 2)) for s in range(2) for w in range(SHARDS)]
+        return [
+            self.over("x", values[0]),
+            self.over("y", values[1]),
+            lax.ppermute(values[2], ("seq", "wt"), both),
+        ]
+
+    def shifts(self, values):
+        return [values[0]] + [self.shift_z(values[k], k) for k in (1, 2, 3)]
+
     def shift_z(self, value, k):
         return lax.ppermute(value, "wt", [(i, (i + 4 * k) % SHARDS) for i in range(SHARDS)])
 
@@ -846,40 +862,130 @@
         far = jnp.concatenate([received, own], axis=axis)
         return jnp.where(flag == 0, near, far)
 
-    def gather(self, y_first, x_first):
-        split = y_first.shape[0]
-        both = jnp.concatenate([y_first, x_first], axis=0)
-        own = lax.dynamic_slice_in_dim(both, self.x * HALF, HALF, axis=1)
-        parts = [own] + [self.shift_z(own, k) for k in (1, 2, 3)]
-        ring = jnp.stack(parts[::-1] + parts[::-1])
-        ring = lax.dynamic_slice_in_dim(ring, (3 - self.z) % 4, 4, axis=0)
-        one, two = ring[:, None, :split], ring[:, None, split:]
-        one_y, two_x = self.over("y", one), self.over("x", two)
-        one = self.in_order(self.y, one, one_y, 1)
-        two = self.in_order(self.x, two, two_x, 3)
-        one_x, two_y = self.over("x", one), self.over("y", two)
-        one = self.in_order(self.x, one, one_x, 3).reshape(8, 1, -1, TILE)
-        two = self.in_order(self.y, two, two_y, 1).reshape(8, 1, -1, TILE)
-        order = self.core.astype(jnp.int32)[None]
-        return (
-            Gathered(one, self.over("core", one), order),
-            Gathered(two, self.over("core", two), order),
-        )
-
-    def scatter(self, own, other, first, second):
-        got = self.over("core", other)
-        far = (own[1].astype(f32) + got[1].astype(f32)).astype(bf16)
-        got_first = self.over(first, far)
-        near = own[0].astype(f32) + got[0].astype(f32) + got_first.astype(f32)
-        got_second = self.over(second, near[1].astype(bf16))
-        total = near[0] + got_second.astype(f32)
-        result = total[0]
-        for k in (1, 2, 3):
-            result = result + self.shift_z(total[k].astype(bf16), k).astype(f32)
-        return result.astype(bf16)
-
-    def both_halves(self, half):
-        return self.in_order(self.x, half, self.over("x", half), 1)
+
+class Gather:
+    def __init__(self, grid, one, two):
+        self.grid, self.split = grid, one.shape[0]
+        both = jnp.concatenate([one, two], axis=0)
+        own = lax.dynamic_slice_in_dim(both, grid.x * HALF, HALF, axis=1)
+        self.got = [own] + [grid.shift_z(own, k) for k in (1, 2, 3)]
+
+    def first(self):
+        both = jnp.stack(self.got)
+        self.one, self.two = both[:, : self.split], both[:, self.split :]
+
+    def first_send(self):
+        self.got = [self.grid.over("y", self.one), self.grid.over("x", self.two)]
+
+    def second(self):
+        self.one = jnp.stack([self.one, self.got[0]])
+        self.two = jnp.stack([self.two, self.got[1]])
+
+    def second_send(self):
+        self.got = [self.grid.over("x", self.one), self.grid.over("y", self.two)]
+
+    def last_send(self):
+        self.one, self.two = [self.one, self.got[0]], [self.two, self.got[1]]
+        self.got = [self.grid.over("core", value) for value in (*self.one, *self.two)]
+
+    def pairs(self):
+        return Gathered("y", [*self.one, *self.got[:2]]), Gathered("x", [*self.two, *self.got[2:]])
+
+
+def far_kernel(count, *refs):
+    owns, gots, outs = refs[:count], refs[count : 2 * count], refs[2 * count :]
+    first = 0
+    for own, got in zip(owns, gots):
+        rows = slice(first, first + own.shape[3])
+        first += own.shape[3]
+        for (x_rel, y_rel), out in zip(((1, 0), (0, 1), (1, 1)), outs):
+            total = own[x_rel, y_rel].astype(f32) + got[x_rel, y_rel].astype(f32)
+            out[:, rows, :] = total.astype(bf16)
+
+
+def far(owns, gots):
+    rows = sum(own.shape[3] for own in owns)
+
+    def spec(array):
+        return pl.BlockSpec((2, 2, 1, array.shape[3], HALF), lambda i: (0, 0, i, 0, 0))
+
+    return pl.pallas_call(
+        functools.partial(far_kernel, len(owns)),
+        grid=(4,),
+        in_specs=[spec(array) for array in (*owns, *gots)],
+        out_specs=[pl.BlockSpec((1, rows, HALF), lambda i: (i, 0, 0))] * 3,
+        out_shape=[struct((4, rows, HALF), bf16)] * 3,
+        compiler_params=params(),
+        cost_estimate=cost(0, 0),
+        name="far",
+    )(*owns, *gots)
+
+
+def near_kernel(count, *refs):
+    owns, gots, received = refs[:count], refs[count : 2 * count], refs[2 * count : 2 * count + 3]
+    outs = refs[2 * count + 3 :]
+    first = 0
+    for own, got in zip(owns, gots):
+        rows = slice(first, first + own.shape[3])
+        first += own.shape[3]
+        for z_rel, out in enumerate(outs):
+            total = own[0, 0, z_rel].astype(f32) + got[0, 0, z_rel].astype(f32)
+            for other in received:
+                total = total + other[z_rel, rows, :].astype(f32)
+            out[rows, :] = total.astype(bf16)
+
+
+def near(owns, gots, received):
+    rows = received[0].shape[1]
+
+    def spec(array):
+        return pl.BlockSpec((1, 1, 4, array.shape[3], HALF), lambda i: (0, 0, 0, 0, 0))
+
+    return pl.pallas_call(
+        functools.partial(near_kernel, len(owns)),
+        grid=(1,),
+        in_specs=[spec(array) for array in (*owns, *gots)] + [fixed((4, rows, HALF))] * 3,
+        out_specs=[fixed((rows, HALF))] * 4,
+        out_shape=[struct((rows, HALF), bf16)] * 4,
+        compiler_params=params(),
+        cost_estimate=cost(0, 0),
+        name="near",
+    )(*owns, *gots, *received)
+
+
+def last_kernel(*refs):
+    *groups, out = refs
+    first = 0
+    for n in range(0, len(groups), 4):
+        rows = slice(first, first + groups[n].shape[0])
+        first += groups[n].shape[0]
+        out[rows, :] = sum(part[...].astype(f32) for part in groups[n : n + 4]).astype(bf16)
+
+
+def last(*groups):
+    arrays = [array for group in groups for array in group]
+    rows = sum(group[0].shape[0] for group in groups)
+    return pl.pallas_call(
+        last_kernel,
+        grid=(1,),
+        in_specs=[fixed(array.shape) for array in arrays],
+        out_specs=fixed((rows, HALF)),
+        out_shape=struct((rows, HALF), bf16),
+        compiler_params=params(),
+        cost_estimate=cost(0, 0),
+        name="last",
+    )(*arrays)
+
+
+class Order:
+    def __init__(self):
+        self.token = None
+
+    def point(self, *values):
+        kept = values if self.token is None else (*values, self.token)
+        done = lax.optimization_barrier(kept)
+        self.token = done[0]
+        return done[: len(values)]
 
 
 class Plain:
@@ -887,10 +993,8 @@
         return jnp.zeros((4,), jnp.int32)
 
 
-def natural(own, other, order):
-    both = jnp.stack([own, other])
-    x_axis, y_axis = (1, 2) if order == "xy" else (2, 1)
-    both = both.transpose(3, y_axis, 0, 4, x_axis, 5)
+def natural(own, other):
+    both = jnp.stack([own, other]).transpose(3, 2, 0, 4, 1, 5)
     return both.reshape(SHARDS, own.shape[3], TILE)
 
 
@@ -915,6 +1019,8 @@
     og = out_grad[0]
     rows = x.shape[0]
     assert MIN_LEN % rows == 0
+    tiles = w_first.shape[1] // TILE
+    early = (tiles + 1) // 2
 
     if direct:
         grid = Grid()
@@ -922,10 +1028,9 @@
             square_blocks(w, 1)[0] for w in (w_key, w_value, w_query, w_gate, w_out)
         )
         feed_block = feed_blocks(w_first, w_second, w_down, 1)[0]
-        feed_weights = lax.all_gather(feed_block, "wt", axis=0, tiled=True)
-        feed_weights = feed_weights.reshape(8, 2, -1, TILE)
-        keys, values = grid.gather(key_block, value_block)
-        queries, gates = grid.gather(
+        kv = Gather(grid, key_block, value_block)
+        qg = Gather(
+            grid,
             jnp.concatenate([query_block, out_block[:128]]),
             jnp.concatenate([gate_block, out_block[128:]]),
         )
@@ -938,15 +1043,17 @@
         feed_weights = feed_blocks(
             *(lax.all_gather(w, "wt", axis=0, tiled=True) for w in (w_first, w_second, w_down)),
             SHARDS,
-        ).reshape(8, 2, -1, TILE)
-
-        def held(block):
-            block = block.reshape(8, 2, -1, TILE)
-            return Gathered(block, block, jnp.zeros((1,), jnp.int32))
-
-        keys, values = held(full_key), held(full_value)
-        queries = held(jnp.concatenate([full_query, full_out[:, :128]], axis=1))
-        gates = held(jnp.concatenate([full_gate, full_out[:, 128:]], axis=1))
+        )
+
+        def held(block, kind):
+            block = block.reshape(4, 2, 2, -1, 2, HALF)[jnp.array([0, 3, 2, 1])]
+            block = block.transpose((2, 4, 1, 0, 3, 5) if kind == "y" else (2, 1, 4, 0, 3, 5))
+            return Gathered(kind, [block[c, p] for c in range(2) for p in range(2)])
+
+        keys, values = held(full_key, "y"), held(full_value, "x")
+        queries = held(jnp.concatenate([full_query, full_out[:, :128]], axis=1), "y")
+        gates = held(jnp.concatenate([full_gate, full_out[:, 128:]], axis=1), "x")
+        feed_weights = feed_weights.reshape(4, 2, 2, -1, TILE)
     coords = grid.coords()
 
     lengths = seq_lengths[0]
@@ -954,7 +1061,7 @@
     begin = seq_index * rows
     begun = (starts <= begin) & (lengths > 0)
     first_token = jnp.max(jnp.where(begun, starts, 0))
-    keep = jnp.where(begin == first_token, 0.0, 1.0).astype(f32)
+    keep = jnp.where(begin == first_token, 0.0, 1.0).astype(f32)[None]
     position = (begin - first_token + jnp.arange(rows, dtype=jnp.int32)).astype(f32)
     frequency = 10000.0 ** (-jnp.arange(HD, dtype=f32) / HD)
     angles = position[:, None] * frequency[None, :]
@@ -963,54 +1070,137 @@
     whole = jnp.exp(-decay_rate * rows)[:, None, None]
 
     a, a_t = prepare(x)
-    kraw, v, own_state = key_value(decay_rate, across, a, keys, values, cosine, sine)
+    if direct:
+        order = Order()
+        *kv.got, a, a_t = order.point(*kv.got, a, a_t)
+        kv.first()
+        kv.one, kv.two, feed_block = order.point(kv.one, kv.two, feed_block)
+        kv.first_send()
+        kv.got = order.point(*kv.got)
+        kv.second()
+        kv.one, kv.two, *qg.got = order.point(kv.one, kv.two, *qg.got)
+        kv.second_send()
+        qg.first()
+        qg.one, qg.two, feed_block = order.point(qg.one, qg.two, feed_block)
+        qg.first_send()
+        feed_weights = lax.all_gather(feed_block, "wt", axis=0, tiled=True)
+        feed_weights = feed_weights.reshape(4, 2, 2, -1, TILE)
+        *kv.got, cosine, sine = order.point(*kv.got, cosine, sine)
+        kv.last_send()
+        kv.got = order.point(*kv.got)
+        keys, values = kv.pairs()
+    kraw, v, own_state = key_value(
+        decay_rate, across, coords, a, keys, values, cosine, sine, bf16 if direct else f32
+    )
     ahead = [(i, i + 1) for i in range(seq_count - 1)]
-    state_in = jnp.zeros_like(own_state)
-    for _ in range(seq_count - 1):
-        sent = (whole * state_in + own_state).astype(bf16)
-        state_in = keep * lax.ppermute(sent, "seq", ahead).astype(f32)
-
+    if direct:
+        own_state, *qg.got = order.point(own_state, *qg.got)
+        state_in = lax.ppermute(own_state, "seq", ahead)
+        qg.second()
+        qg.one, qg.two = order.point(qg.one, qg.two)
+        qg.second_send()
+        state_in, *qg.got = order.point(state_in, *qg.got)
+        qg.last_send()
+        queries, gates = qg.pairs()
+    else:
+        state_in = jnp.zeros_like(own_state)
+        for _ in range(seq_count - 1):
+            sent = (whole * keep * state_in + own_state).astype(bf16)
+            state_in = lax.ppermute(sent, "seq", ahead).astype(f32)
     qraw, u, o, gated = mix(
-        decay_rate, across, a, queries, gates, kraw, v, cosine, sine, state_in
+        decay_rate, across, keep, coords, a, queries, gates, kraw, v, cosine, sine, state_in
     )
-    h1, bn, bn_t = residual(x, gated, queries, gates)
-    tiles = w_first.shape[1] // TILE
-    early = (tiles + 1) // 2
-    g_early, y_part, dbn_part = feed_start(bn, bn_t, og, feed_weights, 0, early)
+    h1, bn, bn_t = residual(coords, x, gated, queries, gates)
+    g_early, y_part, dbn_part = feed_start(bn, bn_t, og, feed_weights, early)
     if direct:
         early_share = lax.psum_scatter(
             g_early.reshape(SHARDS, -1, TILE), "wt", scatter_dimension=0, tiled=True
         )[0]
     own_late, other_late, layer_out, dh1, dattn = feed_end(
-        coords, h1, bn, bn_t, og, y_part, dbn_part, feed_weights, early, tiles - early
+        coords, h1, bn, bn_t, og, y_part, dbn_part, feed_weights, early
     )
-    du, do, own_back = gate_back(
-        decay_rate, across, dattn, queries, gates, o, u, qraw, cosine, sine
-    )
+    back_args = (decay_rate, across, keep, qraw, kraw, v)
+    weights = (queries, keys, values, gates)
     behind = [(i + 1, i) for i in range(seq_count - 1)]
-    back_in = jnp.zeros_like(own_back)
-    for _ in range(seq_count - 1):
-        sent = (keep * (whole * back_in + own_back)).astype(bf16)
-        back_in = lax.ppermute(sent, "seq", behind).astype(f32)
-    own_og, other_og = out_gate_grads(coords, a_t, du, gated, dattn)
-    dq, dk, dv = mix_back(
-        decay_rate, across, qraw, kraw, v, do, cosine, sine, state_in, back_in
-    )
-    own_qkv, other_qkv = query_grads(coords, a_t, dq, dk, dv)
-    input_grad = input_back(x, dh1, (dq, dk, dv, du), (queries, keys, values, gates))
-
+    gate_args = (decay_rate, across, keep, coords, dattn, queries, gates, o, u, qraw, cosine, sine)
     if direct:
-        early_total = early_share.astype(f32) + grid.over("x", early_share).astype(f32)
-        late_total = grid.both_halves(grid.scatter(own_late, other_late, "x", "y")).astype(f32)
-        og_total = grid.both_halves(grid.scatter(own_og, other_og, "y", "x")).astype(f32)
-        qkv_total = grid.both_halves(grid.scatter(own_qkv, other_qkv, "x", "y")).astype(f32)
-        feed_total = jnp.concatenate([early_total, late_total])[None]
-        og_total, qkv_total = og_total[None], qkv_total[None]
+        got_late = grid.over("core", other_late)
+        du, do, own_back = gate_back(*gate_args, bf16)
+        got_late, du, do, own_back = order.point(got_late, du, do, own_back)
+        *sends, own_back, du = order.point(*far([own_late], [got_late]), own_back, du)
+        back_in = lax.ppermute(own_back, "seq", behind)
+        late_got = grid.corners(sends)
+        own_og, other_og = out_gate_grads(coords, a_t, du, gated, dattn)
+        own_og, other_og, back_in = order.point(own_og, other_og, back_in)
+        got_og = grid.over("core", other_og)
+        dq, dk, dv = mix_back(0, *back_args, do, cosine, sine, state_in, back_in)
+        late_got[1], got_og, dq, dk, dv = order.point(late_got[1], got_og, dq, dk, dv)
+        grads_0 = (dq, dk, dv)
+        own_0, other_0 = query_grads(coords, a_t, *grads_0)
+        late_got[0], own_0, other_0, do = order.point(late_got[0], own_0, other_0, do)
+        got_0 = grid.over("core", other_0)
+        dq, dk, dv = mix_back(1, *back_args, do, cosine, sine, state_in, back_in)
+        late_got[2], got_0, dq, dk, dv = order.point(late_got[2], got_0, dq, dk, dv)
+        z_sends = near([own_late], [got_late], late_got)
+        *sends, dq, dk, dv = order.point(
+            *z_sends, *far([own_og, own_0], [got_og, got_0]), dq, dk, dv
+        )
+        middle_got = grid.corners(sends[4:])
+        late_got = grid.shifts(sends[:4])
+        grads_1 = (dq, dk, dv)
+        own_1, other_1 = query_grads(coords, a_t, *grads_1)
+        own_1, other_1, du = order.point(own_1, other_1, du)
+        got_1 = grid.over("core", other_1)
+        partial_sum = input_back(0, coords, (), grads_0, du, weights)
+        middle_got[1], got_1, partial_sum, early_share = order.point(
+            middle_got[1], got_1, partial_sum, early_share
+        )
+        *sends, partial_sum, early_share = order.point(
+            *far([own_1], [got_1]), partial_sum, early_share
+        )
+        end_got = grid.corners(sends)
+        early_other = grid.over("x", early_share)
+        input_grad = input_back(1, coords, (partial_sum, x, dh1), grads_1, du, weights)
+        *rest, input_grad = order.point(middle_got[0], middle_got[2], *late_got[1:], input_grad)
+        middle_got = [rest[0], middle_got[1], rest[1]]
+        late_got = [late_got[0], *rest[2:]]
+        sends = order.point(*near([own_og, own_0], [got_og, got_0], middle_got))
+        middle_got = grid.shifts(sends)
+        end_got = order.point(*end_got)
+        sends = order.point(*near([own_1], [got_1], end_got))
+        end_got = grid.shifts(sends)
+        *middle_got, early_other = order.point(*middle_got, early_other)
+        wide = order.point(last(late_got, middle_got))[0]
+        wide_other = grid.over("x", wide)
+        end_got = order.point(*end_got)
+        narrow = order.point(last(end_got))[0]
+        narrow_other = grid.over("x", narrow)
+        wide_other = order.point(wide_other)[0]
+        early_total = early_share.astype(f32) + early_other.astype(f32)
+        wide = grid.in_order(grid.x, wide, wide_other, 1).astype(f32)
+        narrow = grid.in_order(grid.x, narrow, narrow_other, 1).astype(f32)
+        split = own_late.shape[3]
+        feed_total = jnp.concatenate([early_total, wide[:split]])[None]
+        og_total = wide[None, split : split + 512]
+        qkv_total = jnp.concatenate([wide[split + 512 :], narrow])[None]
         shards = 1
     else:
-        feed_total = jnp.concatenate([g_early, natural(own_late, other_late, "xy")], axis=1)
-        og_total = natural(own_og, other_og, "yx")
-        qkv_total = natural(own_qkv, other_qkv, "xy")
+        du, do, own_back = gate_back(*gate_args, f32)
+        back_in = jnp.zeros_like(own_back)
+        for _ in range(seq_count - 1):
+            sent = (keep * whole * back_in + own_back).astype(bf16)
+            back_in = lax.ppermute(sent, "seq", behind).astype(f32)
+        own_og, other_og = out_gate_grads(coords, a_t, du, gated, dattn)
+        parts = [
+            mix_back(part, *back_args, do, cosine, sine, state_in, back_in) for part in (0, 1)
+        ]
+        partial_sum = input_back(0, coords, (), parts[0], du, weights)
+        input_grad = input_back(1, coords, (partial_sum, x, dh1), parts[1], du, weights)
+        feed_total = jnp.concatenate([g_early, natural(own_late, other_late)], axis=1)
+        og_total = natural(own_og, other_og)
+        qkv_total = jnp.concatenate(
+            [natural(*query_grads(coords, a_t, *part)) for part in parts], axis=1
+        )
         shards = SHARDS
     qkv_total = qkv_total.reshape(shards, 4, 3, 64, TILE)
     squares = [qkv_total[:, :, n] for n in range(3)] + [og_total[:, 256:], og_total[:, :256]]

time: 544 us -> 491 us (0.903)
  Pallas kernels: 185 us -> 226 us
  starting transfers between devices: 97.3 us -> 61.2 us
  waiting for transfers between devices: 174 us -> 139 us
  other arithmetic: 37.6 us -> 10.2 us
    ppermute x15, waiting for transfers between devices: 54.8 us -> 12.3 us  [shift_z(): lax.ppermute(value, 'wt', [(i, (i + 4 * k) % SHARDS) for i in range(SHARD...]
    ppermute x15, starting transfers between devices: 70.9 us -> 29.1 us  [shift_z(): lax.ppermute(value, 'wt', [(i, (i + 4 * k) % SHARDS) for i in range(SHARD...]
    pallas_call x3 -> x14, Pallas kernels: 48.2 us -> 88.7 us  [the longest x2 22.1 us: input_back(): pl.pallas_call(input_end_kernel if part else input_start_kernel, grid=(co...]
    ppermute x11 -> x10, waiting for transfers between devices: 54.4 us -> 17.6 us  [over(): return lax.ppermute(value, 'seq', [(0, 1), (1, 0)])]
    ppermute x2 -> x5, waiting for transfers between devices: 12.6 us -> 39.9 us  [the longest x1 23.6 us: body(): state_in = lax.ppermute(own_state, 'seq', ahead)]
    all_gather x1, waiting for transfers between devices: 0.01 us -> 24.6 us  [body(): feed_weights = lax.all_gather(feed_block, 'wt', axis=0, tiled=True)]
    convert_element_type x12 -> x2, other arithmetic: 13.5 us -> 0.42 us  [the longest x1 0.38 us: body(): wide = grid.in_order(grid.x, wide, wide_other, 1).astype(f32)]
    ppermute x14 -> x19, waiting for transfers between devices: 52.5 us -> 44.2 us  [over(): return lax.ppermute(value, 'wt', [(i, i ^ step) for i in range(SHARDS)])]
  transfers between devices with their start and end apart: 44 -> 51, of which waited for: 19 -> 17; matrix products, arithmetic and copies ran while one was open for 9% -> 3% of each run, Pallas kernels for 28% -> 39%
where the time goes in v3:
time: 491 us; the launch traced here: 482 us
  Pallas kernels  226 us (46%)
  waiting for transfers between devices  139 us (28%)
  starting transfers between devices  61.2 us (12%)
  local copies, waits for them, and re-layouts  29.2 us (6%)
  between operations  16.6 us (3%)
  other arithmetic  10.2 us (2%)
    ppermute x19, waiting for transfers between devices, over(): return lax.ppermute(value, 'wt', [(i, i ^ step) for i in range(SHARDS)])  44.2 us
    pallas_call x1, Pallas kernels, feed_end(): pl.pallas_call(feed_end_kernel, grid=(tiles,), in_specs=[smem(), fixed((r...  39.5 us
    pallas_call x1, Pallas kernels, feed_start(): pl.pallas_call(feed_start_kernel, grid=(tiles,), in_specs=[fixed((rows, d...  37.3 us
    ppermute x15, starting transfers between devices, shift_z(): lax.ppermute(value, 'wt', [(i, (i + 4 * k) % SHARDS) for i in range(SHARD...  29.1 us
    all_gather x1, waiting for transfers between devices, body(): feed_weights = lax.all_gather(feed_block, 'wt', axis=0, tiled=True)  24.6 us
    ppermute x1, waiting for transfers between devices, body(): state_in = lax.ppermute(own_state, 'seq', ahead)  23.6 us
    pallas_call x2, Pallas kernels, input_back(): pl.pallas_call(input_end_kernel if part else input_start_kernel, grid=(co...  22.1 us
    pallas_call x2, Pallas kernels, mix_back(): pl.pallas_call(functools.partial(mix_back_kernel, base), grid=(count,), i...  21.6 us
  transfers between devices with their start and end apart: 51, of which 17 were waited for; matrix products, arithmetic and copies ran while one was open for 3% of the time, Pallas kernels for 39%

profile of v3, /device:TPU:12, one launch (start us, length us, event | category | flops | bytes accessed | tf_op | source)
XLA Modules:
  0.0 481.9 jit_solution(17684784614634137566)
XLA Ops:
  34.3 9.6 %collective-permute-done.7 = bf16[768,128]{1,0:T(8,128)(2,1)S(1)} collective-permute-done((bf16[768,128]{1,0:T(8,128)(2,1)S(1)}, bf16[768,128]{1,0:T(8,128)(2,1)S(1)}, u32[]{:S(2)}, u32[]{:S(2)}) %collective-permute-start.7) | collective-permute-done | bytes 196640 | tf_op jit(solution)/shard_map/ppermute | solution.py:858
  53.3 6.7 %collective-permute-done.9.refs_5_.refs_13_ = bf16[2,4,256,128]{3,2,1,0:T(8,128)(2,1)S(1)} collective-permute-done((bf16[2,4,256,128]{3,2,1,0:T(8,128)(2,1)S(1)}, bf16[2,4,256,128]{3,2,1,0:T(8,128)(2,1)S(1)}, u32[]{:S(2)}, u32[]{:S(2)}) %collective-permute-start.9) | collective-permute-done | bytes 524320 | tf_op jit(solution)/shard_map/ppermute | solution.py:844
  65.5 10.5 %key_value.1 = (bf16[1024,1024]{1,0:T(8,128)(2,1)}, bf16[1024,1024]{1,0:T(8,128)(2,1)}, bf16[8,128,256]{2,1,0:T(8,128)(2,1)}) custom-call(f32[8]{0:T(128)} %rates.9, f32[8]{0:T(128)} %multiply_exponential_fusion.across, s32[4]{0:T(128)} %pad_add_fusion.coords, bf16[1024,1024]{1,0:T(8,128)(2,1)} %get-tuple-element.181.a, ...), custom_call_target="tpu_custom_call" | custom-call | flops 536870 | bytes 1048 | tf_op jit(solution)/shard_map/key_value/pallas_call | solution.py:190
  84.5 23.6 %collective-permute-done.16.state_in = bf16[8,128,256]{2,1,0:T(8,128)(2,1)S(1)} collective-permute-done((bf16[8,128,256]{2,1,0:T(8,128)(2,1)S(1)}, bf16[8,128,256]{2,1,0:T(8,128)(2,1)S(1)}, u32[]{:S(2)}, u32[]{:S(2)}) %collective-permute-start.16) | collective-permute-done | bytes 524320 | tf_op jit(solution)/shard_map/ppermute | solution.py:1098
  112.5 16.5 %mix.1 = (bf16[1024,1024]{1,0:T(8,128)(2,1)}, bf16[1024,1024]{1,0:T(8,128)(2,1)}, bf16[1024,1024]{1,0:T(8,128)(2,1)}, bf16[1024,1024]{1,0:T(8,128)(2,1)}) custom-call(f32[8]{0:T(128)} %rates.9, f32[8]{0:T(128)} %multiply_exponential_fusion.across, f32[1]{0:T(128)} %bitcast.8.keep, s32[4]{0:T(128)} %pad_add_fusion.coords, ...), custom_call_target="tpu_custom_call" | custom-call | flops 858993 | bytes 1887 | tf_op jit(solution)/shard_map/mix/pallas_call | solution.py:247
  129.0 7.7 %residual.1 = (f32[1024,1024]{1,0:T(8,128)}, bf16[1024,1024]{1,0:T(8,128)(2,1)}, bf16[1024,1024]{1,0:T(8,128)(2,1)}) custom-call(s32[4]{0:T(128)} %pad_add_fusion.coords, bf16[1024,1024]{1,0:T(8,128)(2,1)} %bitcast.117, bf16[1024,1024]{1,0:T(8,128)(2,1)} %get-tuple-element.218.gated, bf16[2,4,384,128]{3,2,1,0:T(8,128)(2,1)} %copy-done, ...), custom_call_target="tpu_custom_call" | custom-call | flops 214748 | bytes 1468 | tf_op jit(solution)/shard_map/residual/pallas_call | solution.py:305
  136.7 24.6 %all-gather.2.cloned.1.call-done = bf16[33792,256]{1,0:T(8,128)(2,1)} async-done(((bf16[2112,256]{1,0:T(8,128)(2,1)}), bf16[33792,256]{1,0:T(8,128)(2,1)}) %all-gather.2.cloned.1.call-update) | async-done | bytes 17301520 | tf_op jit(solution)/shard_map/all_gather | solution.py:1086
  161.3 37.3 %feed_start.1 = (bf16[16,1152,256]{2,1,0:T(8,128)(2,1)}, bf16[1024,1024]{1,0:T(8,128)(2,1)}, bf16[1024,1024]{1,0:T(8,128)(2,1)}) custom-call(bf16[1024,1024]{1,0:T(8,128)(2,1)} %get-tuple-element.220.bn, bf16[1024,1024]{1,0:T(8,128)(2,1)} %get-tuple-element.221.bnt, bf16[1024,1024]{1,0:T(8,128)(2,1)} %bitcast.120, bf16[4,2,2,2112,256]{4,3,2,1,0:T(8,128)(2,1)} %bitcast.114), custom_call_target="tpu_custom_call" | custom-call | flops 2899102 | bytes 2936 | tf_op jit(solution)/shard_map/feed_start/pallas_call | solution.py:371
  198.6 39.5 %feed_end.1 = (bf16[2,2,4,960,128]{4,3,2,1,0:T(8,128)(2,1)}, bf16[2,2,4,960,128]{4,3,2,1,0:T(8,128)(2,1)}, bf16[1024,1024]{1,0:T(8,128)(2,1)}, f32[1024,1024]{1,0:T(8,128)}, bf16[1024,1024]{1,0:T(8,128)(2,1)}) custom-call(s32[4]{0:T(128)} %pad_add_fusion.coords, f32[1024,1024]{1,0:T(8,128)} %get-tuple-element.219.h1, ...), custom_call_target="tpu_custom_call" | custom-call | flops 2415919 | bytes 3670 | tf_op jit(solution)/shard_map/feed_end/pallas_call | solution.py:437
  238.4 11.5 %gate_back.1 = (bf16[1024,1024]{1,0:T(8,128)(2,1)}, bf16[1024,1024]{1,0:T(8,128)(2,1)}, bf16[8,128,256]{2,1,0:T(8,128)(2,1)}) custom-call(f32[8]{0:T(128)} %rates.9, f32[8]{0:T(128)} %multiply_exponential_fusion.across, f32[1]{0:T(128)} %bitcast.8.keep, s32[4]{0:T(128)} %pad_add_fusion.coords, bf16[1024,1024]{1,0:T(8,128)(2,1)} %get-tuple-element.228.dattn, ...), custom_call_target="tpu_custom_call" | custom-call | flops 322122 | bytes 1677 | tf_op jit(solution)/shard_map/gate_back/pallas_call | solution.py:518
  251.8 5.3 %far.3 = (bf16[4,960,128]{2,1,0:T(8,128)(2,1)}, bf16[4,960,128]{2,1,0:T(8,128)(2,1)}, bf16[4,960,128]{2,1,0:T(8,128)(2,1)}) custom-call(bf16[2,2,4,960,128]{4,3,2,1,0:T(8,128)(2,1)} %get-tuple-element.226.refs_0_, bf16[2,2,4,960,128]{4,3,2,1,0:T(8,128)(2,1)} %copy-done.4), custom_call_target="tpu_custom_call" | custom-call | tf_op jit(solution)/shard_map/far/pallas_call | solution.py:912
  258.5 10.6 %out_gate_grads.1 = (bf16[2,2,4,512,128]{4,3,2,1,0:T(8,128)(2,1)}, bf16[2,2,4,512,128]{4,3,2,1,0:T(8,128)(2,1)}) custom-call(s32[4]{0:T(128)} %pad_add_fusion.coords, bf16[1024,1024]{1,0:T(8,128)(2,1)} %get-tuple-element.242.a_t, bf16[1024,1024]{1,0:T(8,128)(2,1)} %get-tuple-element.296.du.refs_3_, bf16[1024,1024]{1,0:T(8,128)(2,1)} %get-tuple-element.218.gated, ...), custom_call_target="tpu_custom_call" | custom-call | flops 429496 | bytes 1258 | tf_op jit(solution)/shard_map/out_gate_grads/pallas_call | solution.py:584
  274.7 10.8 %mix_back.2 = (bf16[1024,512]{1,0:T(8,128)(2,1)}, bf16[1024,512]{1,0:T(8,128)(2,1)}, bf16[1024,512]{1,0:T(8,128)(2,1)}) custom-call(f32[8]{0:T(128)} %rates.9, f32[8]{0:T(128)} %multiply_exponential_fusion.across, f32[1]{0:T(128)} %bitcast.8.keep, bf16[1024,1024]{1,0:T(8,128)(2,1)} %get-tuple-element.231.qraw, bf16[1024,1024]{1,0:T(8,128)(2,1)} %get-tuple-element.206.kraw, ...), custom_call_target="tpu_custom_call" | custom-call | flops 429496 | bytes 838 | tf_op jit(solution)/shard_map/mix_back/pallas_call | solution.py:680
  285.4 16.6 %collective-permute-done.25.refs_3_ = bf16[4,960,128]{2,1,0:T(8,128)(2,1)S(1)} collective-permute-done((bf16[4,960,128]{2,1,0:T(8,128)(2,1)}, bf16[4,960,128]{2,1,0:T(8,128)(2,1)S(1)}, u32[]{:S(2)}, u32[]{:S(2)}) %collective-permute-start.25) | collective-permute-done | bytes 983072 | tf_op jit(solution)/shard_map/ppermute | solution.py:844
  302.1 8.9 %query_grads.2 = (bf16[2,2,4,384,128]{4,3,2,1,0:T(8,128)(2,1)}, bf16[2,2,4,384,128]{4,3,2,1,0:T(8,128)(2,1)}) custom-call(s32[4]{0:T(128)} %pad_add_fusion.coords, bf16[1024,1024]{1,0:T(8,128)(2,1)} %get-tuple-element.242.a_t, bf16[1024,512]{1,0:T(8,128)(2,1)} %get-tuple-element.255.dq.refs_0_, bf16[1024,512]{1,0:T(8,128)(2,1)} %get-tuple-element.256.dk.refs_1_, ...), custom_call_target="tpu_custom_call" | custom-call | flops 322122 | bytes 1048 | tf_op jit(solution)/shard_map/query_grads/pallas_call | solution.py:707
  313.5 10.9 %mix_back.3 = (bf16[1024,512]{1,0:T(8,128)(2,1)}, bf16[1024,512]{1,0:T(8,128)(2,1)}, bf16[1024,512]{1,0:T(8,128)(2,1)}) custom-call(f32[8]{0:T(128)} %rates.9, f32[8]{0:T(128)} %multiply_exponential_fusion.across, f32[1]{0:T(128)} %bitcast.8.keep, bf16[1024,1024]{1,0:T(8,128)(2,1)} %get-tuple-element.231.qraw, bf16[1024,1024]{1,0:T(8,128)(2,1)} %get-tuple-element.206.kraw, ...), custom_call_target="tpu_custom_call" | custom-call | flops 429496 | bytes 838 | tf_op jit(solution)/shard_map/mix_back/pallas_call | solution.py:680
  324.4 12.0 %collective-permute-done.28.refs_4_ = bf16[4,960,128]{2,1,0:T(8,128)(2,1)S(1)} collective-permute-done((bf16[4,960,128]{2,1,0:T(8,128)(2,1)}, bf16[4,960,128]{2,1,0:T(8,128)(2,1)S(1)}, u32[]{:S(2)}, u32[]{:S(2)}) %collective-permute-start.28) | collective-permute-done | bytes 983072 | tf_op jit(solution)/shard_map/ppermute | solution.py:851
  341.0 5.0 %far.4 = (bf16[4,896,128]{2,1,0:T(8,128)(2,1)}, bf16[4,896,128]{2,1,0:T(8,128)(2,1)}, bf16[4,896,128]{2,1,0:T(8,128)(2,1)}) custom-call(bf16[2,2,4,512,128]{4,3,2,1,0:T(8,128)(2,1)} %get-tuple-element.254.refs_0_, bf16[2,2,4,384,128]{4,3,2,1,0:T(8,128)(2,1)} %get-tuple-element.273.refs_1_, bf16[2,2,4,512,128]{4,3,2,1,0:T(8,128)(2,1)} %copy-done.5, ...), custom_call_target="tpu_custom_call" | custom-call | tf_op jit(solution)/shard_map/far/pallas_call | solution.py:912
  346.0 8.0 %query_grads.3 = (bf16[2,2,4,384,128]{4,3,2,1,0:T(8,128)(2,1)}, bf16[2,2,4,384,128]{4,3,2,1,0:T(8,128)(2,1)}) custom-call(s32[4]{0:T(128)} %pad_add_fusion.coords, bf16[1024,1024]{1,0:T(8,128)(2,1)} %get-tuple-element.242.a_t, bf16[1024,512]{1,0:T(8,128)(2,1)} %get-tuple-element.287.dq.refs_0_, bf16[1024,512]{1,0:T(8,128)(2,1)} %get-tuple-element.288.dk.refs_1_, ...), custom_call_target="tpu_custom_call" | custom-call | flops 322122 | bytes 1048 | tf_op jit(solution)/shard_map/query_grads/pallas_call | solution.py:707
  359.6 17.3 %collective-permute-done.35.refs_5_ = bf16[4,896,128]{2,1,0:T(8,128)(2,1)S(1)} collective-permute-done((bf16[4,896,128]{2,1,0:T(8,128)(2,1)}, bf16[4,896,128]{2,1,0:T(8,128)(2,1)S(1)}, u32[]{:S(2)}, u32[]{:S(2)}) %collective-permute-start.35) | collective-permute-done | bytes 917536 | tf_op jit(solution)/shard_map/ppermute | solution.py:844
  383.2 9.1 %input_back.2.start = bf16[1024,1024]{1,0:T(8,128)(2,1)} custom-call(s32[4]{0:T(128)} %pad_add_fusion.coords, bf16[1024,512]{1,0:T(8,128)(2,1)} %get-tuple-element.255.dq.refs_0_, bf16[1024,512]{1,0:T(8,128)(2,1)} %get-tuple-element.256.dk.refs_1_, bf16[1024,512]{1,0:T(8,128)(2,1)} %get-tuple-element.257.dv.refs_2_, ...), custom_call_target="tpu_custom_call" | custom-call | flops 429496 | bytes 1677 | tf_op jit(solution)/shard_map/input_back/pallas_call | solution.py:775
  400.1 13.1 %input_back.3 = bf16[1024,1024]{1,0:T(8,128)(2,1)} custom-call(s32[4]{0:T(128)} %pad_add_fusion.coords, bf16[1024,1024]{1,0:T(8,128)(2,1)} %input_back.2.start, bf16[1024,1024]{1,0:T(8,128)(2,1)} %bitcast.118, f32[1024,1024]{1,0:T(8,128)} %get-tuple-element.306.dh1, bf16[1024,512]{1,0:T(8,128)(2,1)} %get-tuple-element.287.dq.refs_0_, ...), custom_call_target="tpu_custom_call" | custom-call | flops 429496 | bytes 1677 | tf_op jit(solution)/shard_map/input_back/pallas_call | solution.py:775
  421.8 7.3 %collective-permute-done.41.refs_2_ = bf16[4,384,128]{2,1,0:T(8,128)(2,1)S(1)} collective-permute-done((bf16[4,384,128]{2,1,0:T(8,128)(2,1)}, bf16[4,384,128]{2,1,0:T(8,128)(2,1)S(1)}, u32[]{:S(2)}, u32[]{:S(2)}) %collective-permute-start.41) | collective-permute-done | bytes 393248 | tf_op jit(solution)/shard_map/ppermute | solution.py:842
  451.5 9.2 %collective-permute-done.48 = bf16[384,128]{1,0:T(8,128)(2,1)S(1)} collective-permute-done((bf16[384,128]{1,0:T(8,128)(2,1)}, bf16[384,128]{1,0:T(8,128)(2,1)S(1)}, u32[]{:S(2)}, u32[]{:S(2)}) %collective-permute-start.48) | collective-permute-done | bytes 98336 | tf_op jit(solution)/shard_map/ppermute | solution.py:842
  (254 shorter events, 133.9 us)
Async XLA Ops:
  7.2 154.1 %all-gather.2.cloned.1.call-start = ((), (), s32[]{:S(2)}) async-start(), calls=%async_computation.1 | async-start | bytes 18382848 | tf_op jit(solution)/shard_map/all_gather | solution.py:1086
  46.2 346.2 %reduce-scatter.2.cloned.1.call-start = ((), (), s32[]{:S(2)}) async-start(), calls=%async_computation.2 | async-start | bytes 10027008 | tf_op jit(solution)/shard_map/reduce_scatter | solution.py:1116
  79.3 28.8 %collective-permute-start.18 = (bf16[2,4,384,128]{3,2,1,0:T(8,128)(2,1)S(1)}, bf16[2,4,384,128]{3,2,1,0:T(8,128)(2,1)S(1)}, u32[]{:S(2)}, u32[]{:S(2)}) collective-permute-start(bf16[2,4,384,128]{3,2,1,0:T(8,128)(2,1)S(1)} %pad_maximum_fusion.4.refs_4_.refs_16_), channel_id=1, source_target_pairs={{0,2},{1,3},{2,0},{3,1},{4,6},{5,7},{6,4},{7,5},{8,10},{9,11},{10,... | collective-permute-start | bytes 2359304 | tf_op jit(solution)/shard_map/ppermute | solution.py:844
  79.8 28.3 %collective-permute-start.17 = (bf16[2,4,384,128]{3,2,1,0:T(8,128)(2,1)S(1)}, bf16[2,4,384,128]{3,2,1,0:T(8,128)(2,1)S(1)}, u32[]{:S(2)}, u32[]{:S(2)}) collective-permute-start(bf16[2,4,384,128]{3,2,1,0:T(8,128)(2,1)S(1)} %pad_maximum_fusion.3.refs_0_.refs_4_), channel_id=1, source_target_pairs={{0,16},{16,0},{1,17},{17,1},{2,18},{18,2},{3,19},{19,3},{4,20},{20... | collective-permute-start | bytes 2359304 | tf_op jit(solution)/shard_map/ppermute | solution.py:842
  80.4 27.7 %collective-permute-start.16 = (bf16[8,128,256]{2,1,0:T(8,128)(2,1)S(1)}, bf16[8,128,256]{2,1,0:T(8,128)(2,1)S(1)}, u32[]{:S(2)}, u32[]{:S(2)}) collective-permute-start(bf16[8,128,256]{2,1,0:T(8,128)(2,1)S(1)} %copy-done.42), channel_id=1, source_target_pairs={{0,16},{1,17},{2,18},{3,19},{4,20},{5,21},{6,22},{7,23},{8,24},{9,... | collective-permute-start | bytes 1572872 | tf_op jit(solution)/shard_map/ppermute | solution.py:1098
  84.0 26.1 %collective-permute-start.21 = (bf16[2,4,384,128]{3,2,1,0:T(8,128)(2,1)S(1)}, bf16[2,4,384,128]{3,2,1,0:T(8,128)(2,1)}, u32[]{:S(2)}, u32[]{:S(2)}) collective-permute-start(bf16[2,4,384,128]{3,2,1,0:T(8,128)(2,1)S(1)} %pad_maximum_fusion.4.refs_4_.refs_16_), channel_id=1, source_target_pairs={{0,1},{1,0},{2,3},{3,2},{4,5},{5,4},{6,7},{7,6},{8,9},{9,8},{10,11... | collective-permute-start | bytes 2359304 | tf_op jit(solution)/shard_map/ppermute | solution.py:844
  84.0 26.1 %collective-permute-start.19 = (bf16[2,4,384,128]{3,2,1,0:T(8,128)(2,1)S(1)}, bf16[2,4,384,128]{3,2,1,0:T(8,128)(2,1)}, u32[]{:S(2)}, u32[]{:S(2)}) collective-permute-start(bf16[2,4,384,128]{3,2,1,0:T(8,128)(2,1)S(1)} %pad_maximum_fusion.3.refs_0_.refs_4_), channel_id=1, source_target_pairs={{0,1},{1,0},{2,3},{3,2},{4,5},{5,4},{6,7},{7,6},{8,9},{9,8},{10,11... | collective-permute-start | bytes 2359304 | tf_op jit(solution)/shard_map/ppermute | solution.py:844
  273.4 28.7 %collective-permute-start.27 = (bf16[2,2,4,512,128]{4,3,2,1,0:T(8,128)(2,1)}, bf16[2,2,4,512,128]{4,3,2,1,0:T(8,128)(2,1)S(1)}, u32[]{:S(2)}, u32[]{:S(2)}) collective-permute-start(bf16[2,2,4,512,128]{4,3,2,1,0:T(8,128)(2,1)} %get-tuple-element.248), channel_id=1, source_target_pairs={{0,1},{1,0},{2,3},{3,2},{4,5},{5,4},{6,7},{7,6},{8,9},{9,8},{10,11... | collective-permute-start | bytes 6291464 | tf_op jit(solution)/shard_map/ppermute | solution.py:844
  273.4 28.7 %collective-permute-start.25 = (bf16[4,960,128]{2,1,0:T(8,128)(2,1)}, bf16[4,960,128]{2,1,0:T(8,128)(2,1)S(1)}, u32[]{:S(2)}, u32[]{:S(2)}) collective-permute-start(bf16[4,960,128]{2,1,0:T(8,128)(2,1)} %get-tuple-element.243), channel_id=1, source_target_pairs={{0,2},{1,3},{2,0},{3,1},{4,6},{5,7},{6,4},{7,5},{8,10},{9,11},{10,... | collective-permute-start | bytes 2949128 | tf_op jit(solution)/shard_map/ppermute | solution.py:844
  274.7 36.3 %collective-permute-start.24 = (bf16[4,960,128]{2,1,0:T(8,128)(2,1)}, bf16[4,960,128]{2,1,0:T(8,128)(2,1)}, u32[]{:S(2)}, u32[]{:S(2)}) collective-permute-start(bf16[4,960,128]{2,1,0:T(8,128)(2,1)} %get-tuple-element.241), channel_id=1, source_target_pairs={{0,16},{16,0},{1,17},{17,1},{2,18},{18,2},{3,19},{19,3},{4,20},{20... | collective-permute-start | bytes 2949128 | tf_op jit(solution)/shard_map/ppermute | solution.py:842
  311.0 25.4 %collective-permute-start.29 = (bf16[2,2,4,384,128]{4,3,2,1,0:T(8,128)(2,1)}, bf16[2,2,4,384,128]{4,3,2,1,0:T(8,128)(2,1)S(1)}, u32[]{:S(2)}, u32[]{:S(2)}) collective-permute-start(bf16[2,2,4,384,128]{4,3,2,1,0:T(8,128)(2,1)} %get-tuple-element.263), channel_id=1, source_target_pairs={{0,1},{1,0},{2,3},{3,2},{4,5},{5,4},{6,7},{7,6},{8,9},{9,8},{10,11... | collective-permute-start | bytes 4718600 | tf_op jit(solution)/shard_map/ppermute | solution.py:844
  311.1 25.3 %collective-permute-start.28 = (bf16[4,960,128]{2,1,0:T(8,128)(2,1)}, bf16[4,960,128]{2,1,0:T(8,128)(2,1)S(1)}, u32[]{:S(2)}, u32[]{:S(2)}) collective-permute-start(bf16[4,960,128]{2,1,0:T(8,128)(2,1)} %get-tuple-element.262), channel_id=1, source_target_pairs={{0,18},{1,19},{2,16},{3,17},{4,22},{5,23},{6,20},{7,21},{8,26},{9,... | collective-permute-start | bytes 2949128 | tf_op jit(solution)/shard_map/ppermute | solution.py:851
  354.0 25.3 %collective-permute-start.36 = (bf16[2,2,4,384,128]{4,3,2,1,0:T(8,128)(2,1)}, bf16[2,2,4,384,128]{4,3,2,1,0:T(8,128)(2,1)S(1)}, u32[]{:S(2)}, u32[]{:S(2)}) collective-permute-start(bf16[2,2,4,384,128]{4,3,2,1,0:T(8,128)(2,1)} %get-tuple-element.295), channel_id=1, source_target_pairs={{0,1},{1,0},{2,3},{3,2},{4,5},{5,4},{6,7},{7,6},{8,9},{9,8},{10,11... | collective-permute-start | bytes 4718600 | tf_op jit(solution)/shard_map/ppermute | solution.py:844
  354.0 23.0 %collective-permute-start.35 = (bf16[4,896,128]{2,1,0:T(8,128)(2,1)}, bf16[4,896,128]{2,1,0:T(8,128)(2,1)S(1)}, u32[]{:S(2)}, u32[]{:S(2)}) collective-permute-start(bf16[4,896,128]{2,1,0:T(8,128)(2,1)} %get-tuple-element.294), channel_id=1, source_target_pairs={{0,2},{1,3},{2,0},{3,1},{4,6},{5,7},{6,4},{7,5},{8,10},{9,11},{10,... | collective-permute-start | bytes 2752520 | tf_op jit(solution)/shard_map/ppermute | solution.py:844
  355.5 44.2 %collective-permute-start.30 = (bf16[4,896,128]{2,1,0:T(8,128)(2,1)}, bf16[4,896,128]{2,1,0:T(8,128)(2,1)S(1)}, u32[]{:S(2)}, u32[]{:S(2)}) collective-permute-start(bf16[4,896,128]{2,1,0:T(8,128)(2,1)} %get-tuple-element.282), channel_id=1, source_target_pairs={{0,16},{16,0},{1,17},{17,1},{2,18},{18,2},{3,19},{19,3},{4,20},{20... | collective-permute-start | bytes 2752520 | tf_op jit(solution)/shard_map/ppermute | solution.py:842
  357.0 56.2 %collective-permute-start.31 = (bf16[4,896,128]{2,1,0:T(8,128)(2,1)}, bf16[4,896,128]{2,1,0:T(8,128)(2,1)}, u32[]{:S(2)}, u32[]{:S(2)}) collective-permute-start(bf16[4,896,128]{2,1,0:T(8,128)(2,1)} %get-tuple-element.283), channel_id=1, source_target_pairs={{0,18},{1,19},{2,16},{3,17},{4,22},{5,23},{6,20},{7,21},{8,26},{9,... | collective-permute-start | bytes 2752520 | tf_op jit(solution)/shard_map/ppermute | solution.py:851
  357.5 38.6 %collective-permute-start.32 = (bf16[960,128]{1,0:T(8,128)(2,1)}, bf16[960,128]{1,0:T(8,128)(2,1)}, u32[]{:S(2)}, u32[]{:S(2)}) collective-permute-start(bf16[960,128]{1,0:T(8,128)(2,1)} %get-tuple-element.284), channel_id=1, source_target_pairs={{0,4},{1,5},{2,6},{3,7},{4,8},{5,9},{6,10},{7,11},{8,12},{9,13},{1... | collective-permute-start | bytes 737288 | tf_op jit(solution)/shard_map/ppermute | solution.py:858
  377.0 20.8 %collective-permute-start.33 = (bf16[960,128]{1,0:T(8,128)(2,1)}, bf16[960,128]{1,0:T(8,128)(2,1)}, u32[]{:S(2)}, u32[]{:S(2)}) collective-permute-start(bf16[960,128]{1,0:T(8,128)(2,1)} %get-tuple-element.285), channel_id=1, source_target_pairs={{0,8},{1,9},{2,10},{3,11},{4,12},{5,13},{6,14},{7,15},{8,0},{9,1},... | collective-permute-start | bytes 737288 | tf_op jit(solution)/shard_map/ppermute | solution.py:858
  396.2 22.6 %collective-permute-start.42 = (bf16[4,384,128]{2,1,0:T(8,128)(2,1)}, bf16[4,384,128]{2,1,0:T(8,128)(2,1)S(1)}, u32[]{:S(2)}, u32[]{:S(2)}) collective-permute-start(bf16[4,384,128]{2,1,0:T(8,128)(2,1)} %get-tuple-element.323), channel_id=1, source_target_pairs={{0,2},{1,3},{2,0},{3,1},{4,6},{5,7},{6,4},{7,5},{8,10},{9,11},{10,... | collective-permute-start | bytes 1179656 | tf_op jit(solution)/shard_map/ppermute | solution.py:844
  397.8 22.2 %collective-permute-start.43 = (bf16[4,384,128]{2,1,0:T(8,128)(2,1)}, bf16[4,384,128]{2,1,0:T(8,128)(2,1)S(1)}, u32[]{:S(2)}, u32[]{:S(2)}) collective-permute-start(bf16[4,384,128]{2,1,0:T(8,128)(2,1)} %get-tuple-element.324), channel_id=1, source_target_pairs={{0,18},{1,19},{2,16},{3,17},{4,22},{5,23},{6,20},{7,21},{8,26},{9,... | collective-permute-start | bytes 1179656 | tf_op jit(solution)/shard_map/ppermute | solution.py:851
  398.1 41.8 %collective-permute-start.40 = (bf16[1152,256]{1,0:T(8,128)(2,1)S(1)}, bf16[1152,256]{1,0:T(8,128)(2,1)S(1)}, u32[]{:S(2)}, u32[]{:S(2)}) collective-permute-start(bf16[1152,256]{1,0:T(8,128)(2,1)S(1)} %bitcast.150), channel_id=1, source_target_pairs={{0,16},{16,0},{1,17},{17,1},{2,18},{18,2},{3,19},{19,3},{4,20},{20... | collective-permute-start | bytes 1769480 | tf_op jit(solution)/shard_map/ppermute | solution.py:842
  399.7 29.4 %collective-permute-start.41 = (bf16[4,384,128]{2,1,0:T(8,128)(2,1)}, bf16[4,384,128]{2,1,0:T(8,128)(2,1)S(1)}, u32[]{:S(2)}, u32[]{:S(2)}) collective-permute-start(bf16[4,384,128]{2,1,0:T(8,128)(2,1)} %get-tuple-element.307), channel_id=1, source_target_pairs={{0,16},{16,0},{1,17},{17,1},{2,18},{18,2},{3,19},{19,3},{4,20},{20... | collective-permute-start | bytes 1179656 | tf_op jit(solution)/shard_map/ppermute | solution.py:842
  418.7 20.9 %collective-permute-start.38 = (bf16[896,128]{1,0:T(8,128)(2,1)}, bf16[896,128]{1,0:T(8,128)(2,1)S(1)}, u32[]{:S(2)}, u32[]{:S(2)}) collective-permute-start(bf16[896,128]{1,0:T(8,128)(2,1)} %get-tuple-element.320), channel_id=1, source_target_pairs={{0,8},{1,9},{2,10},{3,11},{4,12},{5,13},{6,14},{7,15},{8,0},{9,1},... | collective-permute-start | bytes 688136 | tf_op jit(solution)/shard_map/ppermute | solution.py:858
  420.0 19.9 %collective-permute-start.39 = (bf16[896,128]{1,0:T(8,128)(2,1)}, bf16[896,128]{1,0:T(8,128)(2,1)S(1)}, u32[]{:S(2)}, u32[]{:S(2)}) collective-permute-start(bf16[896,128]{1,0:T(8,128)(2,1)} %get-tuple-element.321), channel_id=1, source_target_pairs={{0,12},{1,13},{2,14},{3,15},{4,0},{5,1},{6,2},{7,3},{8,4},{9,5},{1... | collective-permute-start | bytes 688136 | tf_op jit(solution)/shard_map/ppermute | solution.py:858
  (71 other events, 651.4 us)
Sparse Core Ops, SparseCore 0:
  46.3 114.9 all-gather.1
  198.7 125.6 reduce-scatter.1

commit v4 on v3

--- a/solution.py
+++ b/solution.py
@@ -828,6 +828,107 @@
     return wide(blocks[:, :, :64]), wide(blocks[:, :, 64:128]), low.reshape(-1, 1024)
 
 
+def halves(x0, own, other):
+    near = jnp.concatenate([own, other], axis=1)
+    far = jnp.concatenate([other, own], axis=1)
+    return jnp.where(x0 == 0, near, far)
+
+
+def unpack_feed_kernel(
+    coords,
+    early,
+    early_other,
+    wide,
+    wide_other,
+    g1_out,
+    g2_out,
+    gd_out,
+    out_out,
+    gate_out,
+    offset,
+    total,
+):
+    early_tiles, hidden = early.shape[0] // 192, g1_out.shape[1]
+    tiles = hidden // TILE
+    unit = lax.broadcasted_iota(jnp.int32, offset.shape, 0)
+    target = (unit // 16) * (16 * tiles) + unit % 16
+    offset[...] = lax.broadcasted_iota(jnp.int32, offset.shape, 1) - target
+    total[...] = jnp.zeros_like(total)
+
+    def rows_of(tile, first, count):
+        if tile < early_tiles:
+            rows = slice(tile * 192 + first, tile * 192 + first + count)
+            return (early[rows, :].astype(f32) + early_other[rows, :].astype(f32)).astype(bf16)
+        base = (tile - early_tiles) * 192 + first
+        rows = slice(base, base + count)
+        return halves(coords[3], wide[rows, :], wide_other[rows, :])
+
+    for tile in range(tiles):
+        place = jnp.where(offset[...] == 16 * tile, 1.0, 0.0).astype(bf16)
+        total[...] += nn(rows_of(tile, 0, 128), place)
+        for b in range(4):
+            low = rows_of(tile, 128 + 16 * b, 16).astype(f32)
+            gd_out[16 * tile : 16 * tile + 16, b * TILE : (b + 1) * TILE] = low
+    g1_out[...] = total[0:64, :]
+    g2_out[...] = total[64:128, :]
+    base = (tiles - early_tiles) * 192
+    for out in (out_out, gate_out):
+        for b in range(4):
+            rows = slice(base + b * 64, base + b * 64 + 64)
+            out[:, b * TILE : (b + 1) * TILE] = halves(
+                coords[3], wide[rows, :], wide_other[rows, :]
+            ).astype(f32)
+        base += 256
+
+
+def unpack_feed(coords, early, early_other, wide, wide_other):
+    tiles = (early.shape[0] + wide.shape[0] - 512 - 384) // 192
+    arrays = (early, early_other, wide, wide_other)
+    shapes = ((64, tiles * TILE), (64, tiles * TILE), (16 * tiles, 4 * TILE), (64, 1024), (64, 1024))
+    return pl.pallas_call(
+        unpack_feed_kernel,
+        grid=(1,),
+        in_specs=[smem()] + [fixed(array.shape) for array in arrays],
+        out_specs=[fixed(shape) for shape in shapes],
+        out_shape=[struct(shape, f32) for shape in shapes],
+        scratch_shapes=[
+            pltpu.VMEM((TILE, tiles * TILE), jnp.int32),
+            pltpu.VMEM((128, tiles * TILE), f32),
+        ],
+        compiler_params=params(),
+        cost_estimate=cost(0, 0),
+        name="unpack_feed",
+    )(coords, *arrays)
+
+
+def unpack_squares_kernel(coords, wide, wide_other, narrow, narrow_other, *outs):
+    base = wide.shape[0] - 384
+    for n, out in enumerate(outs):
+        for b in range(4):
+            first = (b % 2) * 192 + n * 64
+            if b < 2:
+                rows = slice(base + first, base + first + 64)
+                block = halves(coords[3], wide[rows, :], wide_other[rows, :])
+            else:
+                rows = slice(first, first + 64)
+                block = halves(coords[3], narrow[rows, :], narrow_other[rows, :])
+            out[:, b * TILE : (b + 1) * TILE] = block.astype(f32)
+
+
+def unpack_squares(coords, wide, wide_other, narrow, narrow_other):
+    arrays = (wide, wide_other, narrow, narrow_other)
+    return pl.pallas_call(
+        unpack_squares_kernel,
+        grid=(1,),
+        in_specs=[smem()] + [fixed(array.shape) for array in arrays],
+        out_specs=[fixed((64, 1024))] * 3,
+        out_shape=[struct((64, 1024), f32)] * 3,
+        compiler_params=params(),
+        cost_estimate=cost(0, 0),
+        name="unpack_squares",
+    )(coords, *arrays)
+
+
 class Grid:
     def __init__(self):
         index = lax.axis_index("wt")
@@ -1134,56 +1235,60 @@
         own_og, other_og, back_in = order.point(own_og, other_og, back_in)
         got_og = grid.over("core", other_og)
         dq, dk, dv = mix_back(0, *back_args, do, cosine, sine, state_in, back_in)
-        late_got[1], got_og, dq, dk, dv = order.point(late_got[1], got_og, dq, dk, dv)
+        late_got[1], dq, dk, dv = order.point(late_got[1], dq, dk, dv)
         grads_0 = (dq, dk, dv)
         own_0, other_0 = query_grads(coords, a_t, *grads_0)
         late_got[0], own_0, other_0, do = order.point(late_got[0], own_0, other_0, do)
         got_0 = grid.over("core", other_0)
+        got_og, got_0, do = order.point(got_og, got_0, do)
+        *sends, do = order.point(*far([own_og, own_0], [got_og, got_0]), do)
+        middle_got = grid.corners(sends)
         dq, dk, dv = mix_back(1, *back_args, do, cosine, sine, state_in, back_in)
-        late_got[2], got_0, dq, dk, dv = order.point(late_got[2], got_0, dq, dk, dv)
-        z_sends = near([own_late], [got_late], late_got)
-        *sends, dq, dk, dv = order.point(
-            *z_sends, *far([own_og, own_0], [got_og, got_0]), dq, dk, dv
-        )
-        middle_got = grid.corners(sends[4:])
-        late_got = grid.shifts(sends[:4])
+        late_got[2], dq, dk, dv = order.point(late_got[2], dq, dk, dv)
+        *sends, dq, dk, dv = order.point(*near([own_late], [got_late], late_got), dq, dk, dv)
+        late_got = grid.shifts(sends)
         grads_1 = (dq, dk, dv)
         own_1, other_1 = query_grads(coords, a_t, *grads_1)
-        own_1, other_1, du = order.point(own_1, other_1, du)
+        middle_got[1], own_1, other_1, du = order.point(middle_got[1], own_1, other_1, du)
         got_1 = grid.over("core", other_1)
+        got_1, du = order.point(got_1, du)
+        *sends, du = order.point(*far([own_1], [got_1]), du)
+        end_got = grid.corners(sends)
         partial_sum = input_back(0, coords, (), grads_0, du, weights)
-        middle_got[1], got_1, partial_sum, early_share = order.point(
-            middle_got[1], got_1, partial_sum, early_share
+        middle_got[0], partial_sum = order.point(middle_got[0], partial_sum)
+        input_grad = input_back(1, coords, (partial_sum, x, dh1), grads_1, du, weights)
+        middle_got[2], input_grad, *rest = order.point(
+            middle_got[2], input_grad, *late_got[1:]
         )
-        *sends, partial_sum, early_share = order.point(
-            *far([own_1], [got_1]), partial_sum, early_share
-        )
-        end_got = grid.corners(sends)
-        early_other = grid.over("x", early_share)
-        input_grad = input_back(1, coords, (partial_sum, x, dh1), grads_1, du, weights)
-        *rest, input_grad = order.point(middle_got[0], middle_got[2], *late_got[1:], input_grad)
-        middle_got = [rest[0], middle_got[1], rest[1]]
-        late_got = [late_got[0], *rest[2:]]
+        late_got = [late_got[0], *rest]
         sends = order.point(*near([own_og, own_0], [got_og, got_0], middle_got))
         middle_got = grid.shifts(sends)
-        end_got = order.point(*end_got)
+        early_share, *end_got = order.point(early_share, *end_got)
+        early_other = grid.over("x", early_share)
         sends = order.point(*near([own_1], [got_1], end_got))
         end_got = grid.shifts(sends)
-        *middle_got, early_other = order.point(*middle_got, early_other)
+        middle_got = order.point(*middle_got)
         wide = order.point(last(late_got, middle_got))[0]
         wide_other = grid.over("x", wide)
+        wide, wide_other, early_share, early_other = order.point(
+            wide, wide_other, early_share, early_other
+        )
+        feed_grads = unpack_feed(coords, early_share, early_other, wide, wide_other)
         end_got = order.point(*end_got)
         narrow = order.point(last(end_got))[0]
         narrow_other = grid.over("x", narrow)
-        wide_other = order.point(wide_other)[0]
-        early_total = early_share.astype(f32) + early_other.astype(f32)
-        wide = grid.in_order(grid.x, wide, wide_other, 1).astype(f32)
-        narrow = grid.in_order(grid.x, narrow, narrow_other, 1).astype(f32)
-        split = own_late.shape[3]
-        feed_total = jnp.concatenate([early_total, wide[:split]])[None]
-        og_total = wide[None, split : split + 512]
-        qkv_total = jnp.concatenate([wide[split + 512 :], narrow])[None]
-        shards = 1
+        g_first, g_second, g_down, g_out, g_gate = feed_grads
+        squares = unpack_squares(coords, wide, wide_other, narrow, narrow_other)
+        return (
+            layer_out[None],
+            input_grad[None],
+            *squares,
+            g_gate,
+            g_out,
+            g_first,
+            g_second,
+            g_down,
+        )
     else:
         du, do, own_back = gate_back(*gate_args, f32)
         back_in = jnp.zeros_like(own_back)
@@ -1201,15 +1306,13 @@
         qkv_total = jnp.concatenate(
             [natural(*query_grads(coords, a_t, *part)) for part in parts], axis=1
         )
-        shards = SHARDS
-    qkv_total = qkv_total.reshape(shards, 4, 3, 64, TILE)
+    qkv_total = qkv_total.reshape(SHARDS, 4, 3, 64, TILE)
     squares = [qkv_total[:, :, n] for n in range(3)] + [og_total[:, 256:], og_total[:, :256]]
-    totals = [square_back(g, shards) for g in squares] + list(feed_back(feed_total, shards))
-    if not direct:
-        totals = [
-            lax.psum(lax.psum_scatter(g, "wt", scatter_dimension=0, tiled=True), "seq").astype(f32)
-            for g in totals
-        ]
+    totals = [square_back(g, SHARDS) for g in squares] + list(feed_back(feed_total, SHARDS))
+    totals = [
+        lax.psum(lax.psum_scatter(g, "wt", scatter_dimension=0, tiled=True), "seq").astype(f32)
+        for g in totals
+    ]
     return (layer_out[None], input_grad[None], *totals)
 
 

time: 491 us -> 473 us (0.963)
  waiting for transfers between devices: 139 us -> 127 us
  local copies, waits for them, and re-layouts: 29.2 us -> 18.9 us
  Pallas kernels: 226 us -> 233 us
    ppermute x15, waiting for transfers between devices: 12.3 us -> 26.6 us  [shift_z(): lax.ppermute(value, 'wt', [(i, (i + 4 * k) % SHARDS) for i in range(SHARD...]
    ppermute x19, waiting for transfers between devices: 44.2 us -> 32.9 us  [over(): return lax.ppermute(value, 'wt', [(i, i ^ step) for i in range(SHARDS)])]
    ppermute x3, waiting for transfers between devices: 12 us -> 2.68 us  [corners(): lax.ppermute(values[2], ('seq', 'wt'), both)]
    unnamed x98 -> x92, local copies, waits for them, and re-layouts: 19.1 us -> 11.5 us
    pallas_call x0 -> x2, Pallas kernels: none -> 7.51 us  [the longest x1 5.39 us: unpack_feed(): pl.pallas_call(unpack_feed_kernel, grid=(1,), in_specs=[smem()] + [fixed(...]
  transfers between devices with their start and end apart: 51 -> 51, of which waited for: 17 -> 21; matrix products, arithmetic and copies ran while one was open for 3% -> 3% of each run, Pallas kernels for 39% -> 41%
where the time goes in v4:
time: 473 us; the launch traced here: 465 us
  Pallas kernels  233 us (49%)
  waiting for transfers between devices  127 us (27%)
  starting transfers between devices  61.5 us (13%)
  local copies, waits for them, and re-layouts  18.9 us (4%)
  between operations  16.5 us (3%)
  other arithmetic  8.64 us (2%)
    pallas_call x1, Pallas kernels, feed_end(): pl.pallas_call(feed_end_kernel, grid=(tiles,), in_specs=[smem(), fixed((r...  39.3 us
    pallas_call x1, Pallas kernels, feed_start(): pl.pallas_call(feed_start_kernel, grid=(tiles,), in_specs=[fixed((rows, d...  37.3 us
    ppermute x19, waiting for transfers between devices, over(): return lax.ppermute(value, 'wt', [(i, i ^ step) for i in range(SHARDS)])  32.9 us
    ppermute x15, waiting for transfers between devices, shift_z(): lax.ppermute(value, 'wt', [(i, (i + 4 * k) % SHARDS) for i in range(SHARD...  26.6 us
    all_gather x1, waiting for transfers between devices, body(): feed_weights = lax.all_gather(feed_block, 'wt', axis=0, tiled=True)  26.2 us
    ppermute x15, starting transfers between devices, shift_z(): lax.ppermute(value, 'wt', [(i, (i + 4 * k) % SHARDS) for i in range(SHARD...  25.4 us
    ppermute x1, waiting for transfers between devices, body(): state_in = lax.ppermute(own_state, 'seq', ahead)  23 us
    pallas_call x2, Pallas kernels, input_back(): pl.pallas_call(input_end_kernel if part else input_start_kernel, grid=(co...  22.2 us
  transfers between devices with their start and end apart: 51, of which 21 were waited for; matrix products, arithmetic and copies ran while one was open for 3% of the time, Pallas kernels for 41%

profile of v4, /device:TPU:12, one launch (start us, length us, event | category | flops | bytes accessed | tf_op | source)
XLA Modules:
  0.0 465.4 jit_solution(3236383945529130791)
XLA Ops:
  34.3 9.6 %collective-permute-done.7 = bf16[768,128]{1,0:T(8,128)(2,1)S(1)} collective-permute-done((bf16[768,128]{1,0:T(8,128)(2,1)S(1)}, bf16[768,128]{1,0:T(8,128)(2,1)S(1)}, u32[]{:S(2)}, u32[]{:S(2)}) %collective-permute-start.7) | collective-permute-done | bytes 196640 | tf_op jit(solution)/shard_map/ppermute | solution.py:959
  53.4 6.7 %collective-permute-done.9.refs_5_.refs_13_ = bf16[2,4,256,128]{3,2,1,0:T(8,128)(2,1)S(1)} collective-permute-done((bf16[2,4,256,128]{3,2,1,0:T(8,128)(2,1)S(1)}, bf16[2,4,256,128]{3,2,1,0:T(8,128)(2,1)S(1)}, u32[]{:S(2)}, u32[]{:S(2)}) %collective-permute-start.9) | collective-permute-done | bytes 524320 | tf_op jit(solution)/shard_map/ppermute | solution.py:945
  65.6 10.5 %key_value.1 = (bf16[1024,1024]{1,0:T(8,128)(2,1)}, bf16[1024,1024]{1,0:T(8,128)(2,1)}, bf16[8,128,256]{2,1,0:T(8,128)(2,1)}) custom-call(f32[8]{0:T(128)} %rates.9, f32[8]{0:T(128)} %multiply_exponential_fusion.across, s32[4]{0:T(128)} %pad_add_fusion.coords, bf16[1024,1024]{1,0:T(8,128)(2,1)} %get-tuple-element.193.a, ...), custom_call_target="tpu_custom_call" | custom-call | flops 536870 | bytes 1048 | tf_op jit(solution)/shard_map/key_value/pallas_call | solution.py:190
  83.3 23.0 %collective-permute-done.16.state_in = bf16[8,128,256]{2,1,0:T(8,128)(2,1)S(1)} collective-permute-done((bf16[8,128,256]{2,1,0:T(8,128)(2,1)S(1)}, bf16[8,128,256]{2,1,0:T(8,128)(2,1)S(1)}, u32[]{:S(2)}, u32[]{:S(2)}) %collective-permute-start.16) | collective-permute-done | bytes 524320 | tf_op jit(solution)/shard_map/ppermute | solution.py:1199
  110.7 16.5 %mix.1 = (bf16[1024,1024]{1,0:T(8,128)(2,1)}, bf16[1024,1024]{1,0:T(8,128)(2,1)}, bf16[1024,1024]{1,0:T(8,128)(2,1)}, bf16[1024,1024]{1,0:T(8,128)(2,1)}) custom-call(f32[8]{0:T(128)} %rates.9, f32[8]{0:T(128)} %multiply_exponential_fusion.across, f32[1]{0:T(128)} %bitcast.8.keep, s32[4]{0:T(128)} %pad_add_fusion.coords, ...), custom_call_target="tpu_custom_call" | custom-call | flops 858993 | bytes 1887 | tf_op jit(solution)/shard_map/mix/pallas_call | solution.py:247
  127.2 7.9 %residual.1 = (f32[1024,1024]{1,0:T(8,128)}, bf16[1024,1024]{1,0:T(8,128)(2,1)}, bf16[1024,1024]{1,0:T(8,128)(2,1)}) custom-call(s32[4]{0:T(128)} %pad_add_fusion.coords, bf16[1024,1024]{1,0:T(8,128)(2,1)} %bitcast.67, bf16[1024,1024]{1,0:T(8,128)(2,1)} %get-tuple-element.230.gated, bf16[2,4,384,128]{3,2,1,0:T(8,128)(2,1)} %copy-done, ...), custom_call_target="tpu_custom_call" | custom-call | flops 214748 | bytes 1468 | tf_op jit(solution)/shard_map/residual/pallas_call | solution.py:305
  135.1 26.2 %all-gather.2.cloned.1.call-done = bf16[33792,256]{1,0:T(8,128)(2,1)} async-done(((bf16[2112,256]{1,0:T(8,128)(2,1)}), bf16[33792,256]{1,0:T(8,128)(2,1)}) %all-gather.2.cloned.1.call-update) | async-done | bytes 17301520 | tf_op jit(solution)/shard_map/all_gather | solution.py:1187
  161.3 37.3 %feed_start.1 = (bf16[16,1152,256]{2,1,0:T(8,128)(2,1)}, bf16[1024,1024]{1,0:T(8,128)(2,1)}, bf16[1024,1024]{1,0:T(8,128)(2,1)}) custom-call(bf16[1024,1024]{1,0:T(8,128)(2,1)} %get-tuple-element.232.bn, bf16[1024,1024]{1,0:T(8,128)(2,1)} %get-tuple-element.233.bnt, bf16[1024,1024]{1,0:T(8,128)(2,1)} %bitcast.69, bf16[4,2,2,2112,256]{4,3,2,1,0:T(8,128)(2,1)} %bitcast.64), custom_call_target="tpu_custom_call" | custom-call | flops 2899102 | bytes 2936 | tf_op jit(solution)/shard_map/feed_start/pallas_call | solution.py:371
  198.6 39.3 %feed_end.1 = (bf16[2,2,4,960,128]{4,3,2,1,0:T(8,128)(2,1)}, bf16[2,2,4,960,128]{4,3,2,1,0:T(8,128)(2,1)}, bf16[1024,1024]{1,0:T(8,128)(2,1)}, f32[1024,1024]{1,0:T(8,128)}, bf16[1024,1024]{1,0:T(8,128)(2,1)}) custom-call(s32[4]{0:T(128)} %pad_add_fusion.coords, f32[1024,1024]{1,0:T(8,128)} %get-tuple-element.231.h1, ...), custom_call_target="tpu_custom_call" | custom-call | flops 2415919 | bytes 3670 | tf_op jit(solution)/shard_map/feed_end/pallas_call | solution.py:437
  238.3 11.5 %gate_back.1 = (bf16[1024,1024]{1,0:T(8,128)(2,1)}, bf16[1024,1024]{1,0:T(8,128)(2,1)}, bf16[8,128,256]{2,1,0:T(8,128)(2,1)}) custom-call(f32[8]{0:T(128)} %rates.9, f32[8]{0:T(128)} %multiply_exponential_fusion.across, f32[1]{0:T(128)} %bitcast.8.keep, s32[4]{0:T(128)} %pad_add_fusion.coords, bf16[1024,1024]{1,0:T(8,128)(2,1)} %get-tuple-element.241.dattn, ...), custom_call_target="tpu_custom_call" | custom-call | flops 322122 | bytes 1677 | tf_op jit(solution)/shard_map/gate_back/pallas_call | solution.py:518
  251.6 5.3 %far.3 = (bf16[4,960,128]{2,1,0:T(8,128)(2,1)}, bf16[4,960,128]{2,1,0:T(8,128)(2,1)}, bf16[4,960,128]{2,1,0:T(8,128)(2,1)}) custom-call(bf16[2,2,4,960,128]{4,3,2,1,0:T(8,128)(2,1)} %get-tuple-element.239.refs_0_, bf16[2,2,4,960,128]{4,3,2,1,0:T(8,128)(2,1)} %copy-done.4), custom_call_target="tpu_custom_call" | custom-call | tf_op jit(solution)/shard_map/far/pallas_call | solution.py:1013
  262.3 10.6 %out_gate_grads.1 = (bf16[2,2,4,512,128]{4,3,2,1,0:T(8,128)(2,1)}, bf16[2,2,4,512,128]{4,3,2,1,0:T(8,128)(2,1)}) custom-call(s32[4]{0:T(128)} %pad_add_fusion.coords, bf16[1024,1024]{1,0:T(8,128)(2,1)} %get-tuple-element.238.a_t, bf16[1024,1024]{1,0:T(8,128)(2,1)} %get-tuple-element.314.du.refs_3_, bf16[1024,1024]{1,0:T(8,128)(2,1)} %get-tuple-element.230.gated, ...), custom_call_target="tpu_custom_call" | custom-call | flops 429496 | bytes 1258 | tf_op jit(solution)/shard_map/out_gate_grads/pallas_call | solution.py:584
  274.6 10.7 %mix_back.2 = (bf16[1024,512]{1,0:T(8,128)(2,1)}, bf16[1024,512]{1,0:T(8,128)(2,1)}, bf16[1024,512]{1,0:T(8,128)(2,1)}) custom-call(f32[8]{0:T(128)} %rates.9, f32[8]{0:T(128)} %multiply_exponential_fusion.across, f32[1]{0:T(128)} %bitcast.8.keep, bf16[1024,1024]{1,0:T(8,128)(2,1)} %get-tuple-element.244.qraw, bf16[1024,1024]{1,0:T(8,128)(2,1)} %get-tuple-element.218.kraw, ...), custom_call_target="tpu_custom_call" | custom-call | flops 429496 | bytes 838 | tf_op jit(solution)/shard_map/mix_back/pallas_call | solution.py:680
  285.3 9.8 %collective-permute-done.26.refs_3_ = bf16[4,960,128]{2,1,0:T(8,128)(2,1)S(1)} collective-permute-done((bf16[4,960,128]{2,1,0:T(8,128)(2,1)}, bf16[4,960,128]{2,1,0:T(8,128)(2,1)S(1)}, u32[]{:S(2)}, u32[]{:S(2)}) %collective-permute-start.26) | collective-permute-done | bytes 983072 | tf_op jit(solution)/shard_map/ppermute | solution.py:945
  295.1 8.3 %query_grads.2 = (bf16[2,2,4,384,128]{4,3,2,1,0:T(8,128)(2,1)}, bf16[2,2,4,384,128]{4,3,2,1,0:T(8,128)(2,1)}) custom-call(s32[4]{0:T(128)} %pad_add_fusion.coords, bf16[1024,1024]{1,0:T(8,128)(2,1)} %get-tuple-element.238.a_t, bf16[1024,512]{1,0:T(8,128)(2,1)} %get-tuple-element.266.dq.refs_0_, bf16[1024,512]{1,0:T(8,128)(2,1)} %get-tuple-element.267.dk.refs_1_, ...), custom_call_target="tpu_custom_call" | custom-call | flops 322122 | bytes 1048 | tf_op jit(solution)/shard_map/query_grads/pallas_call | solution.py:707
  309.6 5.0 %far.4 = (bf16[4,896,128]{2,1,0:T(8,128)(2,1)}, bf16[4,896,128]{2,1,0:T(8,128)(2,1)}, bf16[4,896,128]{2,1,0:T(8,128)(2,1)}) custom-call(bf16[2,2,4,512,128]{4,3,2,1,0:T(8,128)(2,1)} %get-tuple-element.259.refs_0_, bf16[2,2,4,384,128]{4,3,2,1,0:T(8,128)(2,1)} %get-tuple-element.272.refs_1_, bf16[2,2,4,512,128]{4,3,2,1,0:T(8,128)(2,1)} %copy-done.5, ...), custom_call_target="tpu_custom_call" | custom-call | tf_op jit(solution)/shard_map/far/pallas_call | solution.py:1013
  316.0 10.7 %mix_back.3 = (bf16[1024,512]{1,0:T(8,128)(2,1)}, bf16[1024,512]{1,0:T(8,128)(2,1)}, bf16[1024,512]{1,0:T(8,128)(2,1)}) custom-call(f32[8]{0:T(128)} %rates.9, f32[8]{0:T(128)} %multiply_exponential_fusion.across, f32[1]{0:T(128)} %bitcast.8.keep, bf16[1024,1024]{1,0:T(8,128)(2,1)} %get-tuple-element.244.qraw, bf16[1024,1024]{1,0:T(8,128)(2,1)} %get-tuple-element.218.kraw, ...), custom_call_target="tpu_custom_call" | custom-call | flops 429496 | bytes 838 | tf_op jit(solution)/shard_map/mix_back/pallas_call | solution.py:680
  333.1 8.0 %query_grads.3 = (bf16[2,2,4,384,128]{4,3,2,1,0:T(8,128)(2,1)}, bf16[2,2,4,384,128]{4,3,2,1,0:T(8,128)(2,1)}) custom-call(s32[4]{0:T(128)} %pad_add_fusion.coords, bf16[1024,1024]{1,0:T(8,128)(2,1)} %get-tuple-element.238.a_t, bf16[1024,512]{1,0:T(8,128)(2,1)} %get-tuple-element.299.dq.refs_0_, bf16[1024,512]{1,0:T(8,128)(2,1)} %get-tuple-element.300.dk.refs_1_, ...), custom_call_target="tpu_custom_call" | custom-call | flops 322122 | bytes 1048 | tf_op jit(solution)/shard_map/query_grads/pallas_call | solution.py:707
  341.1 12.5 %collective-permute-done.31.refs_5_ = bf16[4,896,128]{2,1,0:T(8,128)(2,1)S(1)} collective-permute-done((bf16[4,896,128]{2,1,0:T(8,128)(2,1)}, bf16[4,896,128]{2,1,0:T(8,128)(2,1)S(1)}, u32[]{:S(2)}, u32[]{:S(2)}) %collective-permute-start.31) | collective-permute-done | bytes 917536 | tf_op jit(solution)/shard_map/ppermute | solution.py:945
  381.5 9.1 %input_back.2.start = bf16[1024,1024]{1,0:T(8,128)(2,1)} custom-call(s32[4]{0:T(128)} %pad_add_fusion.coords, bf16[1024,512]{1,0:T(8,128)(2,1)} %get-tuple-element.266.dq.refs_0_, bf16[1024,512]{1,0:T(8,128)(2,1)} %get-tuple-element.267.dk.refs_1_, bf16[1024,512]{1,0:T(8,128)(2,1)} %get-tuple-element.268.dv.refs_2_, ...), custom_call_target="tpu_custom_call" | custom-call | flops 429496 | bytes 1677 | tf_op jit(solution)/shard_map/input_back/pallas_call | solution.py:775
  390.6 13.1 %input_back.3 = bf16[1024,1024]{1,0:T(8,128)(2,1)} custom-call(s32[4]{0:T(128)} %pad_add_fusion.coords, bf16[1024,1024]{1,0:T(8,128)(2,1)} %input_back.2.start, bf16[1024,1024]{1,0:T(8,128)(2,1)} %bitcast.68, f32[1024,1024]{1,0:T(8,128)} %get-tuple-element.317.dh1, bf16[1024,512]{1,0:T(8,128)(2,1)} %get-tuple-element.299.dq.refs_0_, ...), custom_call_target="tpu_custom_call" | custom-call | flops 429496 | bytes 1677 | tf_op jit(solution)/shard_map/input_back/pallas_call | solution.py:775
  417.0 6.5 %collective-permute-done.37.refs_5_ = bf16[896,128]{1,0:T(8,128)(2,1)S(1)} collective-permute-done((bf16[896,128]{1,0:T(8,128)(2,1)}, bf16[896,128]{1,0:T(8,128)(2,1)S(1)}, u32[]{:S(2)}, u32[]{:S(2)}) %collective-permute-start.37) | collective-permute-done | bytes 229408 | tf_op jit(solution)/shard_map/ppermute | solution.py:959
  436.9 9.0 %collective-permute-done.43.wide_other = bf16[1856,128]{1,0:T(8,128)(2,1)S(1)} collective-permute-done((bf16[1856,128]{1,0:T(8,128)(2,1)}, bf16[1856,128]{1,0:T(8,128)(2,1)S(1)}, u32[]{:S(2)}, u32[]{:S(2)}) %collective-permute-start.43) | collective-permute-done | bytes 475168 | tf_op jit(solution)/shard_map/ppermute | solution.py:943
  449.9 5.4 %unpack_feed.1 = (f32[64,2816]{1,0:T(8,128)}, f32[64,2816]{1,0:T(8,128)}, f32[176,1024]{1,0:T(8,128)}, f32[64,1024]{1,0:T(8,128)}, f32[64,1024]{1,0:T(8,128)}) custom-call(s32[4]{0:T(128)} %pad_add_fusion.coords, bf16[1152,256]{1,0:T(8,128)(2,1)} %bitcast.85, bf16[1152,256]{1,0:T(8,128)(2,1)} %copy-done.21, bf16[1856,128]{1,0:T(8,128)(2,1)} %last.2.wide, ...), custom_call_target="tpu_custom_call" | custom-call | tf_op jit(solution)/shard_map/unpack_feed/pallas_call | solution.py:888
  (230 shorter events, 136.5 us)
Async XLA Ops:
  7.2 154.1 %all-gather.2.cloned.1.call-start = ((), (), s32[]{:S(2)}) async-start(), calls=%async_computation.1 | async-start | bytes 18382848 | tf_op jit(solution)/shard_map/all_gather | solution.py:1187
  9.4 16.2 %collective-permute-start.2 = (bf16[512,128]{1,0:T(8,128)(2,1)S(1)}, bf16[512,128]{1,0:T(8,128)(2,1)S(1)}, u32[]{:S(2)}, u32[]{:S(2)}) collective-permute-start(bf16[512,128]{1,0:T(8,128)(2,1)S(1)} %fusion.3), channel_id=1, source_target_pairs={{0,12},{1,13},{2,14},{3,15},{4,0},{5,1},{6,2},{7,3},{8,4},{9,5},{1... | collective-permute-start | bytes 393224 | tf_op jit(solution)/shard_map/ppermute | solution.py:959
  46.2 367.0 %reduce-scatter.2.cloned.1.call-start = ((), (), s32[]{:S(2)}) async-start(), calls=%async_computation.2 | async-start | bytes 10027008 | tf_op jit(solution)/shard_map/reduce_scatter | solution.py:1217
  77.6 28.7 %collective-permute-start.18 = (bf16[2,4,384,128]{3,2,1,0:T(8,128)(2,1)S(1)}, bf16[2,4,384,128]{3,2,1,0:T(8,128)(2,1)S(1)}, u32[]{:S(2)}, u32[]{:S(2)}) collective-permute-start(bf16[2,4,384,128]{3,2,1,0:T(8,128)(2,1)S(1)} %pad_maximum_fusion.3.refs_4_.refs_16_), channel_id=1, source_target_pairs={{0,2},{1,3},{2,0},{3,1},{4,6},{5,7},{6,4},{7,5},{8,10},{9,11},{10,... | collective-permute-start | bytes 2359304 | tf_op jit(solution)/shard_map/ppermute | solution.py:945
  78.2 28.1 %collective-permute-start.17 = (bf16[2,4,384,128]{3,2,1,0:T(8,128)(2,1)S(1)}, bf16[2,4,384,128]{3,2,1,0:T(8,128)(2,1)S(1)}, u32[]{:S(2)}, u32[]{:S(2)}) collective-permute-start(bf16[2,4,384,128]{3,2,1,0:T(8,128)(2,1)S(1)} %pad_maximum_fusion.2.refs_0_.refs_4_), channel_id=1, source_target_pairs={{0,16},{16,0},{1,17},{17,1},{2,18},{18,2},{3,19},{19,3},{4,20},{20... | collective-permute-start | bytes 2359304 | tf_op jit(solution)/shard_map/ppermute | solution.py:943
  78.7 27.6 %collective-permute-start.16 = (bf16[8,128,256]{2,1,0:T(8,128)(2,1)S(1)}, bf16[8,128,256]{2,1,0:T(8,128)(2,1)S(1)}, u32[]{:S(2)}, u32[]{:S(2)}) collective-permute-start(bf16[8,128,256]{2,1,0:T(8,128)(2,1)S(1)} %copy-done.40), channel_id=1, source_target_pairs={{0,16},{1,17},{2,18},{3,19},{4,20},{5,21},{6,22},{7,23},{8,24},{9,... | collective-permute-start | bytes 1572872 | tf_op jit(solution)/shard_map/ppermute | solution.py:1199
  82.7 25.6 %collective-permute-start.21 = (bf16[2,4,384,128]{3,2,1,0:T(8,128)(2,1)S(1)}, bf16[2,4,384,128]{3,2,1,0:T(8,128)(2,1)}, u32[]{:S(2)}, u32[]{:S(2)}) collective-permute-start(bf16[2,4,384,128]{3,2,1,0:T(8,128)(2,1)S(1)} %pad_maximum_fusion.3.refs_4_.refs_16_), channel_id=1, source_target_pairs={{0,1},{1,0},{2,3},{3,2},{4,5},{5,4},{6,7},{7,6},{8,9},{9,8},{10,11... | collective-permute-start | bytes 2359304 | tf_op jit(solution)/shard_map/ppermute | solution.py:945
  82.8 25.5 %collective-permute-start.19 = (bf16[2,4,384,128]{3,2,1,0:T(8,128)(2,1)S(1)}, bf16[2,4,384,128]{3,2,1,0:T(8,128)(2,1)}, u32[]{:S(2)}, u32[]{:S(2)}) collective-permute-start(bf16[2,4,384,128]{3,2,1,0:T(8,128)(2,1)S(1)} %pad_maximum_fusion.2.refs_0_.refs_4_), channel_id=1, source_target_pairs={{0,1},{1,0},{2,3},{3,2},{4,5},{5,4},{6,7},{7,6},{8,9},{9,8},{10,11... | collective-permute-start | bytes 2359304 | tf_op jit(solution)/shard_map/ppermute | solution.py:945
  256.9 16.8 %collective-permute-start.24 = (bf16[8,128,256]{2,1,0:T(8,128)(2,1)}, bf16[8,128,256]{2,1,0:T(8,128)(2,1)S(1)}, u32[]{:S(2)}, u32[]{:S(2)}) collective-permute-start(bf16[8,128,256]{2,1,0:T(8,128)(2,1)} %get-tuple-element.257), channel_id=1, source_target_pairs={{16,0},{17,1},{18,2},{19,3},{20,4},{21,5},{22,6},{23,7},{24,8},{25... | collective-permute-start | bytes 1572872 | tf_op jit(solution)/shard_map/ppermute | solution.py:1232
  258.2 36.8 %collective-permute-start.26 = (bf16[4,960,128]{2,1,0:T(8,128)(2,1)}, bf16[4,960,128]{2,1,0:T(8,128)(2,1)S(1)}, u32[]{:S(2)}, u32[]{:S(2)}) collective-permute-start(bf16[4,960,128]{2,1,0:T(8,128)(2,1)} %get-tuple-element.260), channel_id=1, source_target_pairs={{0,2},{1,3},{2,0},{3,1},{4,6},{5,7},{6,4},{7,5},{8,10},{9,11},{10,... | collective-permute-start | bytes 2949128 | tf_op jit(solution)/shard_map/ppermute | solution.py:945
  259.7 43.7 %collective-permute-start.25 = (bf16[4,960,128]{2,1,0:T(8,128)(2,1)}, bf16[4,960,128]{2,1,0:T(8,128)(2,1)}, u32[]{:S(2)}, u32[]{:S(2)}) collective-permute-start(bf16[4,960,128]{2,1,0:T(8,128)(2,1)} %get-tuple-element.258), channel_id=1, source_target_pairs={{0,16},{16,0},{1,17},{17,1},{2,18},{18,2},{3,19},{19,3},{4,20},{20... | collective-permute-start | bytes 2949128 | tf_op jit(solution)/shard_map/ppermute | solution.py:943
  273.8 33.3 %collective-permute-start.27 = (bf16[2,2,4,512,128]{4,3,2,1,0:T(8,128)(2,1)}, bf16[2,2,4,512,128]{4,3,2,1,0:T(8,128)(2,1)S(1)}, u32[]{:S(2)}, u32[]{:S(2)}) collective-permute-start(bf16[2,2,4,512,128]{4,3,2,1,0:T(8,128)(2,1)} %get-tuple-element.273), channel_id=1, source_target_pairs={{0,1},{1,0},{2,3},{3,2},{4,5},{5,4},{6,7},{7,6},{8,9},{9,8},{10,11... | collective-permute-start | bytes 6291464 | tf_op jit(solution)/shard_map/ppermute | solution.py:945
  303.4 25.9 %collective-permute-start.32 = (bf16[4,960,128]{2,1,0:T(8,128)(2,1)}, bf16[4,960,128]{2,1,0:T(8,128)(2,1)}, u32[]{:S(2)}, u32[]{:S(2)}) collective-permute-start(bf16[4,960,128]{2,1,0:T(8,128)(2,1)} %get-tuple-element.286), channel_id=1, source_target_pairs={{0,18},{1,19},{2,16},{3,17},{4,22},{5,23},{6,20},{7,21},{8,26},{9,... | collective-permute-start | bytes 2949128 | tf_op jit(solution)/shard_map/ppermute | solution.py:952
  314.6 38.9 %collective-permute-start.31 = (bf16[4,896,128]{2,1,0:T(8,128)(2,1)}, bf16[4,896,128]{2,1,0:T(8,128)(2,1)S(1)}, u32[]{:S(2)}, u32[]{:S(2)}) collective-permute-start(bf16[4,896,128]{2,1,0:T(8,128)(2,1)} %get-tuple-element.285), channel_id=1, source_target_pairs={{0,2},{1,3},{2,0},{3,1},{4,6},{5,7},{6,4},{7,5},{8,10},{9,11},{10,... | collective-permute-start | bytes 2752520 | tf_op jit(solution)/shard_map/ppermute | solution.py:945
  353.7 23.4 %collective-permute-start.30 = (bf16[4,896,128]{2,1,0:T(8,128)(2,1)}, bf16[4,896,128]{2,1,0:T(8,128)(2,1)S(1)}, u32[]{:S(2)}, u32[]{:S(2)}) collective-permute-start(bf16[4,896,128]{2,1,0:T(8,128)(2,1)} %get-tuple-element.284), channel_id=1, source_target_pairs={{0,16},{16,0},{1,17},{17,1},{2,18},{18,2},{3,19},{19,3},{4,20},{20... | collective-permute-start | bytes 2752520 | tf_op jit(solution)/shard_map/ppermute | solution.py:943
  355.2 48.6 %collective-permute-start.29 = (bf16[4,896,128]{2,1,0:T(8,128)(2,1)}, bf16[4,896,128]{2,1,0:T(8,128)(2,1)}, u32[]{:S(2)}, u32[]{:S(2)}) collective-permute-start(bf16[4,896,128]{2,1,0:T(8,128)(2,1)} %get-tuple-element.283), channel_id=1, source_target_pairs={{0,18},{1,19},{2,16},{3,17},{4,22},{5,23},{6,20},{7,21},{8,26},{9,... | collective-permute-start | bytes 2752520 | tf_op jit(solution)/shard_map/ppermute | solution.py:952
  357.4 16.4 %collective-permute-start.35 = (bf16[960,128]{1,0:T(8,128)(2,1)}, bf16[960,128]{1,0:T(8,128)(2,1)}, u32[]{:S(2)}, u32[]{:S(2)}) collective-permute-start(bf16[960,128]{1,0:T(8,128)(2,1)} %get-tuple-element.319), channel_id=1, source_target_pairs={{0,8},{1,9},{2,10},{3,11},{4,12},{5,13},{6,14},{7,15},{8,0},{9,1},... | collective-permute-start | bytes 737288 | tf_op jit(solution)/shard_map/ppermute | solution.py:959
  367.3 42.8 %collective-permute-start.41 = (bf16[4,384,128]{2,1,0:T(8,128)(2,1)}, bf16[4,384,128]{2,1,0:T(8,128)(2,1)S(1)}, u32[]{:S(2)}, u32[]{:S(2)}) collective-permute-start(bf16[4,384,128]{2,1,0:T(8,128)(2,1)} %get-tuple-element.336), channel_id=1, source_target_pairs={{0,2},{1,3},{2,0},{3,1},{4,6},{5,7},{6,4},{7,5},{8,10},{9,11},{10,... | collective-permute-start | bytes 1179656 | tf_op jit(solution)/shard_map/ppermute | solution.py:945
  368.1 42.0 %collective-permute-start.42 = (bf16[4,384,128]{2,1,0:T(8,128)(2,1)}, bf16[4,384,128]{2,1,0:T(8,128)(2,1)S(1)}, u32[]{:S(2)}, u32[]{:S(2)}) collective-permute-start(bf16[4,384,128]{2,1,0:T(8,128)(2,1)} %get-tuple-element.337), channel_id=1, source_target_pairs={{0,18},{1,19},{2,16},{3,17},{4,22},{5,23},{6,20},{7,21},{8,26},{9,... | collective-permute-start | bytes 1179656 | tf_op jit(solution)/shard_map/ppermute | solution.py:952
  373.8 39.4 %collective-permute-start.40 = (bf16[4,384,128]{2,1,0:T(8,128)(2,1)}, bf16[4,384,128]{2,1,0:T(8,128)(2,1)}, u32[]{:S(2)}, u32[]{:S(2)}) collective-permute-start(bf16[4,384,128]{2,1,0:T(8,128)(2,1)} %get-tuple-element.315), channel_id=1, source_target_pairs={{0,16},{16,0},{1,17},{17,1},{2,18},{18,2},{3,19},{19,3},{4,20},{20... | collective-permute-start | bytes 1179656 | tf_op jit(solution)/shard_map/ppermute | solution.py:943
  377.1 26.6 %collective-permute-start.36 = (bf16[960,128]{1,0:T(8,128)(2,1)}, bf16[960,128]{1,0:T(8,128)(2,1)S(1)}, u32[]{:S(2)}, u32[]{:S(2)}) collective-permute-start(bf16[960,128]{1,0:T(8,128)(2,1)} %get-tuple-element.320), channel_id=1, source_target_pairs={{0,12},{1,13},{2,14},{3,15},{4,0},{5,1},{6,2},{7,3},{8,4},{9,5},{1... | collective-permute-start | bytes 737288 | tf_op jit(solution)/shard_map/ppermute | solution.py:959
  407.5 19.1 %collective-permute-start.38 = (bf16[896,128]{1,0:T(8,128)(2,1)}, bf16[896,128]{1,0:T(8,128)(2,1)S(1)}, u32[]{:S(2)}, u32[]{:S(2)}) collective-permute-start(bf16[896,128]{1,0:T(8,128)(2,1)} %get-tuple-element.333), channel_id=1, source_target_pairs={{0,8},{1,9},{2,10},{3,11},{4,12},{5,13},{6,14},{7,15},{8,0},{9,1},... | collective-permute-start | bytes 688136 | tf_op jit(solution)/shard_map/ppermute | solution.py:959
  410.1 19.5 %collective-permute-start.39 = (bf16[896,128]{1,0:T(8,128)(2,1)}, bf16[896,128]{1,0:T(8,128)(2,1)S(1)}, u32[]{:S(2)}, u32[]{:S(2)}) collective-permute-start(bf16[896,128]{1,0:T(8,128)(2,1)} %get-tuple-element.334), channel_id=1, source_target_pairs={{0,12},{1,13},{2,14},{3,15},{4,0},{5,1},{6,2},{7,3},{8,4},{9,5},{1... | collective-permute-start | bytes 688136 | tf_op jit(solution)/shard_map/ppermute | solution.py:959
  413.2 32.8 %collective-permute-start.44 = (bf16[1152,256]{1,0:T(8,128)(2,1)}, bf16[1152,256]{1,0:T(8,128)(2,1)S(1)}, u32[]{:S(2)}, u32[]{:S(2)}) collective-permute-start(bf16[1152,256]{1,0:T(8,128)(2,1)} %bitcast.84), channel_id=1, source_target_pairs={{0,16},{16,0},{1,17},{17,1},{2,18},{18,2},{3,19},{19,3},{4,20},{20... | collective-permute-start | bytes 1769480 | tf_op jit(solution)/shard_map/ppermute | solution.py:943
  (72 other events, 671.6 us)
Sparse Core Ops, SparseCore 0:
  46.3 114.9 all-gather.1
  198.7 151.8 reduce-scatter.1

commit v5 on v4

--- a/solution.py
+++ b/solution.py
@@ -1255,28 +1255,27 @@
         *sends, du = order.point(*far([own_1], [got_1]), du)
         end_got = grid.corners(sends)
         partial_sum = input_back(0, coords, (), grads_0, du, weights)
-        middle_got[0], partial_sum = order.point(middle_got[0], partial_sum)
-        input_grad = input_back(1, coords, (partial_sum, x, dh1), grads_1, du, weights)
-        middle_got[2], input_grad, *rest = order.point(
-            middle_got[2], input_grad, *late_got[1:]
+        middle_got[0], middle_got[2], partial_sum, *rest = order.point(
+            middle_got[0], middle_got[2], partial_sum, *late_got[1:]
         )
         late_got = [late_got[0], *rest]
-        sends = order.point(*near([own_og, own_0], [got_og, got_0], middle_got))
+        *sends, partial_sum, early_share = order.point(
+            *near([own_og, own_0], [got_og, got_0], middle_got), partial_sum, early_share
+        )
         middle_got = grid.shifts(sends)
-        early_share, *end_got = order.point(early_share, *end_got)
         early_other = grid.over("x", early_share)
+        input_grad = input_back(1, coords, (partial_sum, x, dh1), grads_1, du, weights)
+        input_grad = order.point(input_grad)[0]
+        end_got = order.point(*end_got)
         sends = order.point(*near([own_1], [got_1], end_got))
         end_got = grid.shifts(sends)
         middle_got = order.point(*middle_got)
         wide = order.point(last(late_got, middle_got))[0]
         wide_other = grid.over("x", wide)
-        wide, wide_other, early_share, early_other = order.point(
-            wide, wide_other, early_share, early_other
-        )
-        feed_grads = unpack_feed(coords, early_share, early_other, wide, wide_other)
         end_got = order.point(*end_got)
         narrow = order.point(last(end_got))[0]
         narrow_other = grid.over("x", narrow)
+        feed_grads = unpack_feed(coords, early_share, early_other, wide, wide_other)
         g_first, g_second, g_down, g_out, g_gate = feed_grads
         squares = unpack_squares(coords, wide, wide_other, narrow, narrow_other)
         return (

time: 473 us -> 475 us (level)
    ppermute x10, waiting for transfers between devices: 14.6 us -> 8.01 us  [over(): return lax.ppermute(value, 'seq', [(0, 1), (1, 0)])]
    ppermute x15, waiting for transfers between devices: 26.6 us -> 32.8 us  [shift_z(): lax.ppermute(value, 'wt', [(i, (i + 4 * k) % SHARDS) for i in range(SHARD...]
    unnamed x92 -> x90, local copies, waits for them, and re-layouts: 11.5 us -> 12.4 us
  transfers between devices with their start and end apart: 51 -> 51, of which waited for: 21 -> 22; matrix products, arithmetic and copies ran while one was open for 3% -> 3% of each run, Pallas kernels for 41% -> 41%
where the time goes in v5:
time: 475 us; the launch traced here: 466 us
  Pallas kernels  233 us (49%)
  waiting for transfers between devices  126 us (27%)
  starting transfers between devices  61.6 us (13%)
  local copies, waits for them, and re-layouts  19.8 us (4%)
  between operations  16.5 us (3%)
  other arithmetic  8.62 us (2%)
    pallas_call x1, Pallas kernels, feed_end(): pl.pallas_call(feed_end_kernel, grid=(tiles,), in_specs=[smem(), fixed((r...  39.3 us
    pallas_call x1, Pallas kernels, feed_start(): pl.pallas_call(feed_start_kernel, grid=(tiles,), in_specs=[fixed((rows, d...  37.2 us
    ppermute x19, waiting for transfers between devices, over(): return lax.ppermute(value, 'wt', [(i, i ^ step) for i in range(SHARDS)])  32.9 us
    ppermute x15, waiting for transfers between devices, shift_z(): lax.ppermute(value, 'wt', [(i, (i + 4 * k) % SHARDS) for i in range(SHARD...  32.8 us
    all_gather x1, waiting for transfers between devices, body(): feed_weights = lax.all_gather(feed_block, 'wt', axis=0, tiled=True)  26.2 us
    ppermute x15, starting transfers between devices, shift_z(): lax.ppermute(value, 'wt', [(i, (i + 4 * k) % SHARDS) for i in range(SHARD...  23.2 us
    ppermute x1, waiting for transfers between devices, body(): state_in = lax.ppermute(own_state, 'seq', ahead)  23.1 us
    pallas_call x2, Pallas kernels, input_back(): pl.pallas_call(input_end_kernel if part else input_start_kernel, grid=(co...  22.2 us
  transfers between devices with their start and end apart: 51, of which 22 were waited for; matrix products, arithmetic and copies ran while one was open for 3% of the time, Pallas kernels for 41%

profile of v5, /device:TPU:12, one launch (start us, length us, event | category | flops | bytes accessed | tf_op | source)
XLA Modules:
  0.0 465.7 jit_solution(16416878572277767815)
XLA Ops:
  34.3 9.6 %collective-permute-done.7 = bf16[768,128]{1,0:T(8,128)(2,1)S(1)} collective-permute-done((bf16[768,128]{1,0:T(8,128)(2,1)S(1)}, bf16[768,128]{1,0:T(8,128)(2,1)S(1)}, u32[]{:S(2)}, u32[]{:S(2)}) %collective-permute-start.7) | collective-permute-done | bytes 196640 | tf_op jit(solution)/shard_map/ppermute | solution.py:959
  53.4 6.7 %collective-permute-done.9.refs_5_.refs_13_ = bf16[2,4,256,128]{3,2,1,0:T(8,128)(2,1)S(1)} collective-permute-done((bf16[2,4,256,128]{3,2,1,0:T(8,128)(2,1)S(1)}, bf16[2,4,256,128]{3,2,1,0:T(8,128)(2,1)S(1)}, u32[]{:S(2)}, u32[]{:S(2)}) %collective-permute-start.9) | collective-permute-done | bytes 524320 | tf_op jit(solution)/shard_map/ppermute | solution.py:945
  65.6 10.5 %key_value.1 = (bf16[1024,1024]{1,0:T(8,128)(2,1)}, bf16[1024,1024]{1,0:T(8,128)(2,1)}, bf16[8,128,256]{2,1,0:T(8,128)(2,1)}) custom-call(f32[8]{0:T(128)} %rates.9, f32[8]{0:T(128)} %multiply_exponential_fusion.across, s32[4]{0:T(128)} %pad_add_fusion.coords, bf16[1024,1024]{1,0:T(8,128)(2,1)} %get-tuple-element.190.a, ...), custom_call_target="tpu_custom_call" | custom-call | flops 536870 | bytes 1048 | tf_op jit(solution)/shard_map/key_value/pallas_call | solution.py:190
  83.3 23.1 %collective-permute-done.16.state_in = bf16[8,128,256]{2,1,0:T(8,128)(2,1)S(1)} collective-permute-done((bf16[8,128,256]{2,1,0:T(8,128)(2,1)S(1)}, bf16[8,128,256]{2,1,0:T(8,128)(2,1)S(1)}, u32[]{:S(2)}, u32[]{:S(2)}) %collective-permute-start.16) | collective-permute-done | bytes 524320 | tf_op jit(solution)/shard_map/ppermute | solution.py:1199
  110.7 16.5 %mix.1 = (bf16[1024,1024]{1,0:T(8,128)(2,1)}, bf16[1024,1024]{1,0:T(8,128)(2,1)}, bf16[1024,1024]{1,0:T(8,128)(2,1)}, bf16[1024,1024]{1,0:T(8,128)(2,1)}) custom-call(f32[8]{0:T(128)} %rates.9, f32[8]{0:T(128)} %multiply_exponential_fusion.across, f32[1]{0:T(128)} %bitcast.8.keep, s32[4]{0:T(128)} %pad_add_fusion.coords, ...), custom_call_target="tpu_custom_call" | custom-call | flops 858993 | bytes 1887 | tf_op jit(solution)/shard_map/mix/pallas_call | solution.py:247
  127.2 7.9 %residual.1 = (f32[1024,1024]{1,0:T(8,128)}, bf16[1024,1024]{1,0:T(8,128)(2,1)}, bf16[1024,1024]{1,0:T(8,128)(2,1)}) custom-call(s32[4]{0:T(128)} %pad_add_fusion.coords, bf16[1024,1024]{1,0:T(8,128)(2,1)} %bitcast.67, bf16[1024,1024]{1,0:T(8,128)(2,1)} %get-tuple-element.227.gated, bf16[2,4,384,128]{3,2,1,0:T(8,128)(2,1)} %copy-done, ...), custom_call_target="tpu_custom_call" | custom-call | flops 214748 | bytes 1468 | tf_op jit(solution)/shard_map/residual/pallas_call | solution.py:305
  135.1 26.2 %all-gather.2.cloned.1.call-done = bf16[33792,256]{1,0:T(8,128)(2,1)} async-done(((bf16[2112,256]{1,0:T(8,128)(2,1)}), bf16[33792,256]{1,0:T(8,128)(2,1)}) %all-gather.2.cloned.1.call-update) | async-done | bytes 17301520 | tf_op jit(solution)/shard_map/all_gather | solution.py:1187
  161.3 37.2 %feed_start.1 = (bf16[16,1152,256]{2,1,0:T(8,128)(2,1)}, bf16[1024,1024]{1,0:T(8,128)(2,1)}, bf16[1024,1024]{1,0:T(8,128)(2,1)}) custom-call(bf16[1024,1024]{1,0:T(8,128)(2,1)} %get-tuple-element.229.bn, bf16[1024,1024]{1,0:T(8,128)(2,1)} %get-tuple-element.230.bnt, bf16[1024,1024]{1,0:T(8,128)(2,1)} %bitcast.69, bf16[4,2,2,2112,256]{4,3,2,1,0:T(8,128)(2,1)} %bitcast.64), custom_call_target="tpu_custom_call" | custom-call | flops 2899102 | bytes 2936 | tf_op jit(solution)/shard_map/feed_start/pallas_call | solution.py:371
  198.6 39.3 %feed_end.1 = (bf16[2,2,4,960,128]{4,3,2,1,0:T(8,128)(2,1)}, bf16[2,2,4,960,128]{4,3,2,1,0:T(8,128)(2,1)}, bf16[1024,1024]{1,0:T(8,128)(2,1)}, f32[1024,1024]{1,0:T(8,128)}, bf16[1024,1024]{1,0:T(8,128)(2,1)}) custom-call(s32[4]{0:T(128)} %pad_add_fusion.coords, f32[1024,1024]{1,0:T(8,128)} %get-tuple-element.228.h1, ...), custom_call_target="tpu_custom_call" | custom-call | flops 2415919 | bytes 3670 | tf_op jit(solution)/shard_map/feed_end/pallas_call | solution.py:437
  238.2 11.5 %gate_back.1 = (bf16[1024,1024]{1,0:T(8,128)(2,1)}, bf16[1024,1024]{1,0:T(8,128)(2,1)}, bf16[8,128,256]{2,1,0:T(8,128)(2,1)}) custom-call(f32[8]{0:T(128)} %rates.9, f32[8]{0:T(128)} %multiply_exponential_fusion.across, f32[1]{0:T(128)} %bitcast.8.keep, s32[4]{0:T(128)} %pad_add_fusion.coords, bf16[1024,1024]{1,0:T(8,128)(2,1)} %get-tuple-element.238.dattn, ...), custom_call_target="tpu_custom_call" | custom-call | flops 322122 | bytes 1677 | tf_op jit(solution)/shard_map/gate_back/pallas_call | solution.py:518
  251.6 5.3 %far.3 = (bf16[4,960,128]{2,1,0:T(8,128)(2,1)}, bf16[4,960,128]{2,1,0:T(8,128)(2,1)}, bf16[4,960,128]{2,1,0:T(8,128)(2,1)}) custom-call(bf16[2,2,4,960,128]{4,3,2,1,0:T(8,128)(2,1)} %get-tuple-element.236.refs_0_, bf16[2,2,4,960,128]{4,3,2,1,0:T(8,128)(2,1)} %copy-done.4), custom_call_target="tpu_custom_call" | custom-call | tf_op jit(solution)/shard_map/far/pallas_call | solution.py:1013
  262.3 10.6 %out_gate_grads.1 = (bf16[2,2,4,512,128]{4,3,2,1,0:T(8,128)(2,1)}, bf16[2,2,4,512,128]{4,3,2,1,0:T(8,128)(2,1)}) custom-call(s32[4]{0:T(128)} %pad_add_fusion.coords, bf16[1024,1024]{1,0:T(8,128)(2,1)} %get-tuple-element.235.a_t, bf16[1024,1024]{1,0:T(8,128)(2,1)} %get-tuple-element.311.du.refs_3_, bf16[1024,1024]{1,0:T(8,128)(2,1)} %get-tuple-element.227.gated, ...), custom_call_target="tpu_custom_call" | custom-call | flops 429496 | bytes 1258 | tf_op jit(solution)/shard_map/out_gate_grads/pallas_call | solution.py:584
  274.6 10.8 %mix_back.2 = (bf16[1024,512]{1,0:T(8,128)(2,1)}, bf16[1024,512]{1,0:T(8,128)(2,1)}, bf16[1024,512]{1,0:T(8,128)(2,1)}) custom-call(f32[8]{0:T(128)} %rates.9, f32[8]{0:T(128)} %multiply_exponential_fusion.across, f32[1]{0:T(128)} %bitcast.8.keep, bf16[1024,1024]{1,0:T(8,128)(2,1)} %get-tuple-element.241.qraw, bf16[1024,1024]{1,0:T(8,128)(2,1)} %get-tuple-element.215.kraw, ...), custom_call_target="tpu_custom_call" | custom-call | flops 429496 | bytes 838 | tf_op jit(solution)/shard_map/mix_back/pallas_call | solution.py:680
  285.3 9.7 %collective-permute-done.26.refs_3_ = bf16[4,960,128]{2,1,0:T(8,128)(2,1)S(1)} collective-permute-done((bf16[4,960,128]{2,1,0:T(8,128)(2,1)}, bf16[4,960,128]{2,1,0:T(8,128)(2,1)S(1)}, u32[]{:S(2)}, u32[]{:S(2)}) %collective-permute-start.26) | collective-permute-done | bytes 983072 | tf_op jit(solution)/shard_map/ppermute | solution.py:945
  295.1 8.3 %query_grads.2 = (bf16[2,2,4,384,128]{4,3,2,1,0:T(8,128)(2,1)}, bf16[2,2,4,384,128]{4,3,2,1,0:T(8,128)(2,1)}) custom-call(s32[4]{0:T(128)} %pad_add_fusion.coords, bf16[1024,1024]{1,0:T(8,128)(2,1)} %get-tuple-element.235.a_t, bf16[1024,512]{1,0:T(8,128)(2,1)} %get-tuple-element.263.dq.refs_0_, bf16[1024,512]{1,0:T(8,128)(2,1)} %get-tuple-element.264.dk.refs_1_, ...), custom_call_target="tpu_custom_call" | custom-call | flops 322122 | bytes 1048 | tf_op jit(solution)/shard_map/query_grads/pallas_call | solution.py:707
  309.6 5.1 %far.4 = (bf16[4,896,128]{2,1,0:T(8,128)(2,1)}, bf16[4,896,128]{2,1,0:T(8,128)(2,1)}, bf16[4,896,128]{2,1,0:T(8,128)(2,1)}) custom-call(bf16[2,2,4,512,128]{4,3,2,1,0:T(8,128)(2,1)} %get-tuple-element.256.refs_0_, bf16[2,2,4,384,128]{4,3,2,1,0:T(8,128)(2,1)} %get-tuple-element.269.refs_1_, bf16[2,2,4,512,128]{4,3,2,1,0:T(8,128)(2,1)} %copy-done.5, ...), custom_call_target="tpu_custom_call" | custom-call | tf_op jit(solution)/shard_map/far/pallas_call | solution.py:1013
  316.0 10.8 %mix_back.3 = (bf16[1024,512]{1,0:T(8,128)(2,1)}, bf16[1024,512]{1,0:T(8,128)(2,1)}, bf16[1024,512]{1,0:T(8,128)(2,1)}) custom-call(f32[8]{0:T(128)} %rates.9, f32[8]{0:T(128)} %multiply_exponential_fusion.across, f32[1]{0:T(128)} %bitcast.8.keep, bf16[1024,1024]{1,0:T(8,128)(2,1)} %get-tuple-element.241.qraw, bf16[1024,1024]{1,0:T(8,128)(2,1)} %get-tuple-element.215.kraw, ...), custom_call_target="tpu_custom_call" | custom-call | flops 429496 | bytes 838 | tf_op jit(solution)/shard_map/mix_back/pallas_call | solution.py:680
  333.1 8.0 %query_grads.3 = (bf16[2,2,4,384,128]{4,3,2,1,0:T(8,128)(2,1)}, bf16[2,2,4,384,128]{4,3,2,1,0:T(8,128)(2,1)}) custom-call(s32[4]{0:T(128)} %pad_add_fusion.coords, bf16[1024,1024]{1,0:T(8,128)(2,1)} %get-tuple-element.235.a_t, bf16[1024,512]{1,0:T(8,128)(2,1)} %get-tuple-element.296.dq.refs_0_, bf16[1024,512]{1,0:T(8,128)(2,1)} %get-tuple-element.297.dk.refs_1_, ...), custom_call_target="tpu_custom_call" | custom-call | flops 322122 | bytes 1048 | tf_op jit(solution)/shard_map/query_grads/pallas_call | solution.py:707
  341.1 12.4 %collective-permute-done.31.refs_5_ = bf16[4,896,128]{2,1,0:T(8,128)(2,1)S(1)} collective-permute-done((bf16[4,896,128]{2,1,0:T(8,128)(2,1)}, bf16[4,896,128]{2,1,0:T(8,128)(2,1)S(1)}, u32[]{:S(2)}, u32[]{:S(2)}) %collective-permute-start.31) | collective-permute-done | bytes 917536 | tf_op jit(solution)/shard_map/ppermute | solution.py:945
  368.2 10.7 %collective-permute-done.35.refs_2_ = bf16[960,128]{1,0:T(8,128)(2,1)} collective-permute-done((bf16[960,128]{1,0:T(8,128)(2,1)S(1)}, bf16[960,128]{1,0:T(8,128)(2,1)}, u32[]{:S(2)}, u32[]{:S(2)}) %collective-permute-start.35) | collective-permute-done | bytes 245792 | tf_op jit(solution)/shard_map/ppermute | solution.py:959
  385.2 9.1 %input_back.2.start = bf16[1024,1024]{1,0:T(8,128)(2,1)} custom-call(s32[4]{0:T(128)} %pad_add_fusion.coords, bf16[1024,512]{1,0:T(8,128)(2,1)} %get-tuple-element.263.dq.refs_0_, bf16[1024,512]{1,0:T(8,128)(2,1)} %get-tuple-element.264.dk.refs_1_, bf16[1024,512]{1,0:T(8,128)(2,1)} %get-tuple-element.265.dv.refs_2_, ...), custom_call_target="tpu_custom_call" | custom-call | flops 429496 | bytes 1677 | tf_op jit(solution)/shard_map/input_back/pallas_call | solution.py:775
  401.7 5.0 %collective-permute-start.38 = (bf16[896,128]{1,0:T(8,128)(2,1)}, bf16[896,128]{1,0:T(8,128)(2,1)S(1)}, u32[]{:S(2)}, u32[]{:S(2)}) collective-permute-start(bf16[896,128]{1,0:T(8,128)(2,1)} %get-tuple-element.332), channel_id=1, source_target_pairs={{0,8},{1,9},{2,10},{3,11},{4,12},{5,13},{6,14},{7,15},{8,0},{9,1},... | collective-permute-start | bytes 688136 | tf_op jit(solution)/shard_map/ppermute | solution.py:959
  409.2 13.1 %input_back.3 = bf16[1024,1024]{1,0:T(8,128)(2,1)} custom-call(s32[4]{0:T(128)} %pad_add_fusion.coords, bf16[1024,1024]{1,0:T(8,128)(2,1)} %input_back.2.start, bf16[1024,1024]{1,0:T(8,128)(2,1)} %bitcast.68, f32[1024,1024]{1,0:T(8,128)} %get-tuple-element.325.dh1, bf16[1024,512]{1,0:T(8,128)(2,1)} %get-tuple-element.296.dq.refs_0_, ...), custom_call_target="tpu_custom_call" | custom-call | flops 429496 | bytes 1677 | tf_op jit(solution)/shard_map/input_back/pallas_call | solution.py:775
  453.0 5.4 %unpack_feed.1 = (f32[64,2816]{1,0:T(8,128)}, f32[64,2816]{1,0:T(8,128)}, f32[176,1024]{1,0:T(8,128)}, f32[64,1024]{1,0:T(8,128)}, f32[64,1024]{1,0:T(8,128)}) custom-call(s32[4]{0:T(128)} %pad_add_fusion.coords, bf16[1152,256]{1,0:T(8,128)(2,1)} %bitcast.85, bf16[1152,256]{1,0:T(8,128)(2,1)} %copy-done.21, bf16[1856,128]{1,0:T(8,128)(2,1)} %last.2.wide, ...), custom_call_target="tpu_custom_call" | custom-call | tf_op jit(solution)/shard_map/unpack_feed/pallas_call | solution.py:888
  (228 shorter events, 136.4 us)
Async XLA Ops:
  7.2 154.1 %all-gather.2.cloned.1.call-start = ((), (), s32[]{:S(2)}) async-start(), calls=%async_computation.1 | async-start | bytes 18382848 | tf_op jit(solution)/shard_map/all_gather | solution.py:1187
  46.2 355.2 %reduce-scatter.2.cloned.1.call-start = ((), (), s32[]{:S(2)}) async-start(), calls=%async_computation.2 | async-start | bytes 10027008 | tf_op jit(solution)/shard_map/reduce_scatter | solution.py:1217
  77.6 28.7 %collective-permute-start.18 = (bf16[2,4,384,128]{3,2,1,0:T(8,128)(2,1)S(1)}, bf16[2,4,384,128]{3,2,1,0:T(8,128)(2,1)S(1)}, u32[]{:S(2)}, u32[]{:S(2)}) collective-permute-start(bf16[2,4,384,128]{3,2,1,0:T(8,128)(2,1)S(1)} %pad_maximum_fusion.3.refs_4_.refs_16_), channel_id=1, source_target_pairs={{0,2},{1,3},{2,0},{3,1},{4,6},{5,7},{6,4},{7,5},{8,10},{9,11},{10,... | collective-permute-start | bytes 2359304 | tf_op jit(solution)/shard_map/ppermute | solution.py:945
  78.2 28.1 %collective-permute-start.17 = (bf16[2,4,384,128]{3,2,1,0:T(8,128)(2,1)S(1)}, bf16[2,4,384,128]{3,2,1,0:T(8,128)(2,1)S(1)}, u32[]{:S(2)}, u32[]{:S(2)}) collective-permute-start(bf16[2,4,384,128]{3,2,1,0:T(8,128)(2,1)S(1)} %pad_maximum_fusion.2.refs_0_.refs_4_), channel_id=1, source_target_pairs={{0,16},{16,0},{1,17},{17,1},{2,18},{18,2},{3,19},{19,3},{4,20},{20... | collective-permute-start | bytes 2359304 | tf_op jit(solution)/shard_map/ppermute | solution.py:943
  78.7 27.6 %collective-permute-start.16 = (bf16[8,128,256]{2,1,0:T(8,128)(2,1)S(1)}, bf16[8,128,256]{2,1,0:T(8,128)(2,1)S(1)}, u32[]{:S(2)}, u32[]{:S(2)}) collective-permute-start(bf16[8,128,256]{2,1,0:T(8,128)(2,1)S(1)} %copy-done.39), channel_id=1, source_target_pairs={{0,16},{1,17},{2,18},{3,19},{4,20},{5,21},{6,22},{7,23},{8,24},{9,... | collective-permute-start | bytes 1572872 | tf_op jit(solution)/shard_map/ppermute | solution.py:1199
  82.7 25.6 %collective-permute-start.21 = (bf16[2,4,384,128]{3,2,1,0:T(8,128)(2,1)S(1)}, bf16[2,4,384,128]{3,2,1,0:T(8,128)(2,1)}, u32[]{:S(2)}, u32[]{:S(2)}) collective-permute-start(bf16[2,4,384,128]{3,2,1,0:T(8,128)(2,1)S(1)} %pad_maximum_fusion.3.refs_4_.refs_16_), channel_id=1, source_target_pairs={{0,1},{1,0},{2,3},{3,2},{4,5},{5,4},{6,7},{7,6},{8,9},{9,8},{10,11... | collective-permute-start | bytes 2359304 | tf_op jit(solution)/shard_map/ppermute | solution.py:945
  82.8 25.5 %collective-permute-start.19 = (bf16[2,4,384,128]{3,2,1,0:T(8,128)(2,1)S(1)}, bf16[2,4,384,128]{3,2,1,0:T(8,128)(2,1)}, u32[]{:S(2)}, u32[]{:S(2)}) collective-permute-start(bf16[2,4,384,128]{3,2,1,0:T(8,128)(2,1)S(1)} %pad_maximum_fusion.2.refs_0_.refs_4_), channel_id=1, source_target_pairs={{0,1},{1,0},{2,3},{3,2},{4,5},{5,4},{6,7},{7,6},{8,9},{9,8},{10,11... | collective-permute-start | bytes 2359304 | tf_op jit(solution)/shard_map/ppermute | solution.py:945
  258.2 36.8 %collective-permute-start.26 = (bf16[4,960,128]{2,1,0:T(8,128)(2,1)}, bf16[4,960,128]{2,1,0:T(8,128)(2,1)S(1)}, u32[]{:S(2)}, u32[]{:S(2)}) collective-permute-start(bf16[4,960,128]{2,1,0:T(8,128)(2,1)} %get-tuple-element.257), channel_id=1, source_target_pairs={{0,2},{1,3},{2,0},{3,1},{4,6},{5,7},{6,4},{7,5},{8,10},{9,11},{10,... | collective-permute-start | bytes 2949128 | tf_op jit(solution)/shard_map/ppermute | solution.py:945
  259.7 43.7 %collective-permute-start.25 = (bf16[4,960,128]{2,1,0:T(8,128)(2,1)}, bf16[4,960,128]{2,1,0:T(8,128)(2,1)}, u32[]{:S(2)}, u32[]{:S(2)}) collective-permute-start(bf16[4,960,128]{2,1,0:T(8,128)(2,1)} %get-tuple-element.255), channel_id=1, source_target_pairs={{0,16},{16,0},{1,17},{17,1},{2,18},{18,2},{3,19},{19,3},{4,20},{20... | collective-permute-start | bytes 2949128 | tf_op jit(solution)/shard_map/ppermute | solution.py:943
  273.8 33.3 %collective-permute-start.27 = (bf16[2,2,4,512,128]{4,3,2,1,0:T(8,128)(2,1)}, bf16[2,2,4,512,128]{4,3,2,1,0:T(8,128)(2,1)S(1)}, u32[]{:S(2)}, u32[]{:S(2)}) collective-permute-start(bf16[2,2,4,512,128]{4,3,2,1,0:T(8,128)(2,1)} %get-tuple-element.270), channel_id=1, source_target_pairs={{0,1},{1,0},{2,3},{3,2},{4,5},{5,4},{6,7},{7,6},{8,9},{9,8},{10,11... | collective-permute-start | bytes 6291464 | tf_op jit(solution)/shard_map/ppermute | solution.py:945
  303.4 25.9 %collective-permute-start.32 = (bf16[4,960,128]{2,1,0:T(8,128)(2,1)}, bf16[4,960,128]{2,1,0:T(8,128)(2,1)}, u32[]{:S(2)}, u32[]{:S(2)}) collective-permute-start(bf16[4,960,128]{2,1,0:T(8,128)(2,1)} %get-tuple-element.283), channel_id=1, source_target_pairs={{0,18},{1,19},{2,16},{3,17},{4,22},{5,23},{6,20},{7,21},{8,26},{9,... | collective-permute-start | bytes 2949128 | tf_op jit(solution)/shard_map/ppermute | solution.py:952
  314.7 38.9 %collective-permute-start.31 = (bf16[4,896,128]{2,1,0:T(8,128)(2,1)}, bf16[4,896,128]{2,1,0:T(8,128)(2,1)S(1)}, u32[]{:S(2)}, u32[]{:S(2)}) collective-permute-start(bf16[4,896,128]{2,1,0:T(8,128)(2,1)} %get-tuple-element.282), channel_id=1, source_target_pairs={{0,2},{1,3},{2,0},{3,1},{4,6},{5,7},{6,4},{7,5},{8,10},{9,11},{10,... | collective-permute-start | bytes 2752520 | tf_op jit(solution)/shard_map/ppermute | solution.py:945
  353.7 40.7 %collective-permute-start.30 = (bf16[4,896,128]{2,1,0:T(8,128)(2,1)}, bf16[4,896,128]{2,1,0:T(8,128)(2,1)S(1)}, u32[]{:S(2)}, u32[]{:S(2)}) collective-permute-start(bf16[4,896,128]{2,1,0:T(8,128)(2,1)} %get-tuple-element.281), channel_id=1, source_target_pairs={{0,18},{1,19},{2,16},{3,17},{4,22},{5,23},{6,20},{7,21},{8,26},{9,... | collective-permute-start | bytes 2752520 | tf_op jit(solution)/shard_map/ppermute | solution.py:952
  356.1 41.7 %collective-permute-start.29 = (bf16[4,896,128]{2,1,0:T(8,128)(2,1)}, bf16[4,896,128]{2,1,0:T(8,128)(2,1)}, u32[]{:S(2)}, u32[]{:S(2)}) collective-permute-start(bf16[4,896,128]{2,1,0:T(8,128)(2,1)} %get-tuple-element.280), channel_id=1, source_target_pairs={{0,16},{16,0},{1,17},{17,1},{2,18},{18,2},{3,19},{19,3},{4,20},{20... | collective-permute-start | bytes 2752520 | tf_op jit(solution)/shard_map/ppermute | solution.py:943
  357.4 21.5 %collective-permute-start.35 = (bf16[960,128]{1,0:T(8,128)(2,1)S(1)}, bf16[960,128]{1,0:T(8,128)(2,1)}, u32[]{:S(2)}, u32[]{:S(2)}) collective-permute-start(bf16[960,128]{1,0:T(8,128)(2,1)S(1)} %copy-done.40), channel_id=1, source_target_pairs={{0,8},{1,9},{2,10},{3,11},{4,12},{5,13},{6,14},{7,15},{8,0},{9,1},... | collective-permute-start | bytes 737288 | tf_op jit(solution)/shard_map/ppermute | solution.py:959
  362.4 21.1 %collective-permute-start.36 = (bf16[960,128]{1,0:T(8,128)(2,1)}, bf16[960,128]{1,0:T(8,128)(2,1)}, u32[]{:S(2)}, u32[]{:S(2)}) collective-permute-start(bf16[960,128]{1,0:T(8,128)(2,1)} %get-tuple-element.314), channel_id=1, source_target_pairs={{0,12},{1,13},{2,14},{3,15},{4,0},{5,1},{6,2},{7,3},{8,4},{9,5},{1... | collective-permute-start | bytes 737288 | tf_op jit(solution)/shard_map/ppermute | solution.py:959
  367.3 39.5 %collective-permute-start.41 = (bf16[4,384,128]{2,1,0:T(8,128)(2,1)}, bf16[4,384,128]{2,1,0:T(8,128)(2,1)S(1)}, u32[]{:S(2)}, u32[]{:S(2)}) collective-permute-start(bf16[4,384,128]{2,1,0:T(8,128)(2,1)} %get-tuple-element.334), channel_id=1, source_target_pairs={{0,2},{1,3},{2,0},{3,1},{4,6},{5,7},{6,4},{7,5},{8,10},{9,11},{10,... | collective-permute-start | bytes 1179656 | tf_op jit(solution)/shard_map/ppermute | solution.py:945
  378.9 27.9 %collective-permute-start.42 = (bf16[4,384,128]{2,1,0:T(8,128)(2,1)}, bf16[4,384,128]{2,1,0:T(8,128)(2,1)S(1)}, u32[]{:S(2)}, u32[]{:S(2)}) collective-permute-start(bf16[4,384,128]{2,1,0:T(8,128)(2,1)} %get-tuple-element.335), channel_id=1, source_target_pairs={{0,18},{1,19},{2,16},{3,17},{4,22},{5,23},{6,20},{7,21},{8,26},{9,... | collective-permute-start | bytes 1179656 | tf_op jit(solution)/shard_map/ppermute | solution.py:952
  383.5 38.8 %collective-permute-start.40 = (bf16[4,384,128]{2,1,0:T(8,128)(2,1)}, bf16[4,384,128]{2,1,0:T(8,128)(2,1)}, u32[]{:S(2)}, u32[]{:S(2)}) collective-permute-start(bf16[4,384,128]{2,1,0:T(8,128)(2,1)} %get-tuple-element.315), channel_id=1, source_target_pairs={{0,16},{16,0},{1,17},{17,1},{2,18},{18,2},{3,19},{19,3},{4,20},{20... | collective-permute-start | bytes 1179656 | tf_op jit(solution)/shard_map/ppermute | solution.py:943
  401.4 23.3 %collective-permute-start.37 = (bf16[896,128]{1,0:T(8,128)(2,1)}, bf16[896,128]{1,0:T(8,128)(2,1)S(1)}, u32[]{:S(2)}, u32[]{:S(2)}) collective-permute-start(bf16[896,128]{1,0:T(8,128)(2,1)} %get-tuple-element.331), channel_id=1, source_target_pairs={{0,4},{1,5},{2,6},{3,7},{4,8},{5,9},{6,10},{7,11},{8,12},{9,13},{1... | collective-permute-start | bytes 688136 | tf_op jit(solution)/shard_map/ppermute | solution.py:959
  401.7 23.0 %collective-permute-start.38 = (bf16[896,128]{1,0:T(8,128)(2,1)}, bf16[896,128]{1,0:T(8,128)(2,1)S(1)}, u32[]{:S(2)}, u32[]{:S(2)}) collective-permute-start(bf16[896,128]{1,0:T(8,128)(2,1)} %get-tuple-element.332), channel_id=1, source_target_pairs={{0,8},{1,9},{2,10},{3,11},{4,12},{5,13},{6,14},{7,15},{8,0},{9,1},... | collective-permute-start | bytes 688136 | tf_op jit(solution)/shard_map/ppermute | solution.py:959
  406.8 18.9 %collective-permute-start.39 = (bf16[896,128]{1,0:T(8,128)(2,1)}, bf16[896,128]{1,0:T(8,128)(2,1)S(1)}, u32[]{:S(2)}, u32[]{:S(2)}) collective-permute-start(bf16[896,128]{1,0:T(8,128)(2,1)} %get-tuple-element.333), channel_id=1, source_target_pairs={{0,12},{1,13},{2,14},{3,15},{4,0},{5,1},{6,2},{7,3},{8,4},{9,5},{1... | collective-permute-start | bytes 688136 | tf_op jit(solution)/shard_map/ppermute | solution.py:959
  406.8 45.3 %collective-permute-start.48 = (bf16[1152,256]{1,0:T(8,128)(2,1)}, bf16[1152,256]{1,0:T(8,128)(2,1)S(1)}, u32[]{:S(2)}, u32[]{:S(2)}) collective-permute-start(bf16[1152,256]{1,0:T(8,128)(2,1)} %bitcast.84), channel_id=1, source_target_pairs={{0,16},{16,0},{1,17},{17,1},{2,18},{18,2},{3,19},{19,3},{4,20},{20... | collective-permute-start | bytes 1769480 | tf_op jit(solution)/shard_map/ppermute | solution.py:943
  429.0 19.6 %collective-permute-start.43 = (bf16[1856,128]{1,0:T(8,128)(2,1)}, bf16[1856,128]{1,0:T(8,128)(2,1)S(1)}, u32[]{:S(2)}, u32[]{:S(2)}) collective-permute-start(bf16[1856,128]{1,0:T(8,128)(2,1)} %last.2.wide), channel_id=1, source_target_pairs={{0,16},{16,0},{1,17},{17,1},{2,18},{18,2},{3,19},{19,3},{4,20},{20... | collective-permute-start | bytes 1425416 | tf_op jit(solution)/shard_map/ppermute | solution.py:943
  (71 other events, 638.8 us)
Sparse Core Ops, SparseCore 0:
  46.3 114.9 all-gather.1
  198.7 151.8 reduce-scatter.1
